TPU v7x, 32 devices: a whole 2x2x4 slice. The times are simulated.
32 devices in a mesh: dp: 4 (over y, x), fsdp: 8 (over z, core).
Axes of the slice: x: 2, y: 2, z: 4, core: 2. Of those that a mesh axis runs over, the one named last changes fastest.
Arguments:
- tokens: bfloat16 [4, 2048, 1536], P('dp', 'fsdp'), may hold values from -6 to 6
- segment_ids: int32 [4, 2048], P('dp', 'fsdp'), may hold values from 0 to 1, as said below
- routes: int32 [4, 2048, 2], P('dp', 'fsdp'), may hold values from 0 to 7, as said below
- query_weight: bfloat16 [1536, 1536], P(('dp', 'fsdp')), may hold values from -0.15625 to 0.15625
- key_value_weight: bfloat16 [1536, 1024], P(('dp', 'fsdp')), may hold values from -0.15625 to 0.15625
- output_weight: bfloat16 [1536, 1536], P(None, ('dp', 'fsdp')), may hold values from -0.625 to 0.625
- router_weight: bfloat16 [1536, 8], P(('dp', 'fsdp')), may hold values from -0.109375 to 0.109375
- gain_before: bfloat16 [1536], P(('dp', 'fsdp')), may hold values from 0.099609375 to 1.8984375
- gain_middle: bfloat16 [1536], P(('dp', 'fsdp')), may hold values from 0.099609375 to 1.8984375
- inner_weight: bfloat16 [1536, 2, 8192], P('dp', None, 'fsdp'), may hold values from -0.15625 to 0.15625
- outer_weight: bfloat16 [8192, 1536], P('fsdp', 'dp'), may hold values from -0.1875 to 0.1875
- cotangent: bfloat16 [4, 2048, 1536], P('dp', 'fsdp'), may hold values from -6 to 6
Outputs:
- block_out: bfloat16 [4, 2048, 1536], P('dp', 'fsdp')
- tokens_grad: float32 [4, 2048, 1536], P('dp', 'fsdp')
- query_grad: float32 [1536, 1536], P(('dp', 'fsdp'))
- keyval_grad: float32 [1536, 1024], P(('dp', 'fsdp'))
- output_grad: float32 [1536, 1536], P(None, ('dp', 'fsdp'))
- router_grad: float32 [1536, 8], P(('dp', 'fsdp'))
- before_grad: float32 [1536], P(('dp', 'fsdp'))
- middle_grad: float32 [1536], P(('dp', 'fsdp'))
- inner_grad: float32 [1536, 2, 8192], P('dp', None, 'fsdp')
- outer_grad: float32 [8192, 1536], P('fsdp', 'dp')
Inputs may be any that keep to these rules, and one draw needn't show every extreme that they name: `segment_ids`: ids never fall along a sequence and are 0 at its start. Among the 1 sequence of each dp index, one holds a short document within its first 256 positions and then one document to its end. Where 1 is 2 or more, another one is cut into 7 documents. `routes`: each token names two different experts. Among the tokens of one device (one index of dp and of fsdp) no expert is named more than 96 times, and for each dp index some expert is named exactly 96 times by every device.
All inputs are finite; a program needn't handle non-finite values.
Results may differ from a plain program's by a relative error of at most 0.015.
Values may be sent and summed in bfloat16 or wider, within the bound.
No kernel may reach another device: no remote copies, remote signals or barrier semaphores. Data moves between devices by JAX's collectives and lax.ppermute only.
A program may use at most 320 MiB of HBM per device.

v0:
```python
import jax
import jax.numpy as jnp
from jax import lax
from jax.sharding import PartitionSpec as P

QUERY_HEADS = 24
KEY_VALUE_HEADS = 8
HEAD_SIZE = 64


HIGHEST_PRECISION = lax.Precision.HIGHEST
EPSILON = 1e-05
NEGATIVE_LARGE = -1e30


def normalize(hidden, gain_vec):
    factor = lax.rsqrt(jnp.mean(hidden * hidden, -1, keepdims=True) + EPSILON)
    unit_rows = hidden * factor
    return (unit_rows * gain_vec.astype(jnp.float32), unit_rows, factor)


def normalize_back(grad_rows, unit_rows, factor, gain_vec):
    scaled = grad_rows * gain_vec.astype(jnp.float32)
    inner_part = factor * (scaled - unit_rows * jnp.mean(scaled * unit_rows, -1, keepdims=True))
    return (inner_part, jnp.sum(grad_rows * unit_rows, 0))


def split_block(gathered, offset, key_tile_block):
    sequence_count = gathered.shape[0]
    portion_rows = lax.slice_in_dim(gathered, offset, offset + key_tile_block, axis=1)
    half_columns = KEY_VALUE_HEADS * HEAD_SIZE
    key_portion = portion_rows[..., :half_columns].reshape(
        sequence_count, key_tile_block, KEY_VALUE_HEADS, HEAD_SIZE
    )
    value_portion = portion_rows[..., half_columns:].reshape(
        sequence_count, key_tile_block, KEY_VALUE_HEADS, HEAD_SIZE
    )
    return (key_portion, value_portion)


def block_scores(query_matrix, key_portion, allowed):
    raw_scores = jnp.einsum(
        "sikgd,sjkd->skgij", query_matrix, key_portion, preferred_element_type=jnp.float32
    ) * HEAD_SIZE ** (-0.5)
    return jnp.where(allowed[:, None, None], raw_scores, NEGATIVE_LARGE)


def mask_for(seg_all, seg_mine, positions, offset, key_tile_block):
    key_seg = lax.slice_in_dim(seg_all, offset, offset + key_tile_block, axis=1)
    key_spots = offset + jnp.arange(key_tile_block, dtype=jnp.int32)
    same_doc = seg_mine[:, :, None] == key_seg[:, None, :]
    causal = key_spots[None, None, :] <= positions[None, :, None]
    return same_doc & causal


def log_totals(query_matrix, gathered, block_masks, key_tile_block):
    sequence_count, resident_rows = (query_matrix.shape[0], query_matrix.shape[1])
    running_totals = jnp.full(
        (sequence_count, KEY_VALUE_HEADS, QUERY_HEADS // KEY_VALUE_HEADS, resident_rows),
        NEGATIVE_LARGE,
        jnp.float32,
    )
    for block_index, allowed in enumerate(block_masks):
        key_portion, value_portion = split_block(
            gathered, block_index * key_tile_block, key_tile_block
        )

        def log_live(present_value, key_portion=key_portion, allowed=allowed):
            scores = block_scores(query_matrix, key_portion, allowed)
            return jnp.logaddexp(present_value, jax.nn.logsumexp(scores, -1))

        running_totals = lax.cond(
            jnp.any(allowed), log_live, lambda present_value: present_value, running_totals
        )
    return running_totals


def attend_values(query_matrix, gathered, block_masks, key_tile_block, running_totals):
    result = jnp.zeros(query_matrix.shape, jnp.float32)
    for block_index, allowed in enumerate(block_masks):
        key_portion, value_portion = split_block(
            gathered, block_index * key_tile_block, key_tile_block
        )

        def attend_live(
            present_value, key_portion=key_portion, value_portion=value_portion, allowed=allowed
        ):
            probs = jnp.exp(
                block_scores(query_matrix, key_portion, allowed) - running_totals[..., None]
            ).astype(jnp.bfloat16)
            return present_value + jnp.einsum(
                "skgij,sjkd->sikgd", probs, value_portion, preferred_element_type=jnp.float32
            )

        result = lax.cond(
            jnp.any(allowed), attend_live, lambda present_value: present_value, result
        )
    token_count = query_matrix.shape[0] * query_matrix.shape[1]
    return result.reshape(token_count, -1).astype(jnp.bfloat16)


def attend_back(
    query_matrix, mixed_gradient, gathered, block_masks, key_tile_block, running_totals
):
    sequence_count = query_matrix.shape[0]
    delta = jnp.zeros(running_totals.shape, jnp.float32)
    for block_index, allowed in enumerate(block_masks):
        key_portion, value_portion = split_block(
            gathered, block_index * key_tile_block, key_tile_block
        )

        def live_delta(
            present_value, key_portion=key_portion, value_portion=value_portion, allowed=allowed
        ):
            probs = jnp.exp(
                block_scores(query_matrix, key_portion, allowed) - running_totals[..., None]
            )
            grad_probs = jnp.einsum(
                "sikgd,sjkd->skgij",
                mixed_gradient,
                value_portion,
                preferred_element_type=jnp.float32,
            )
            return present_value + jnp.sum(probs * grad_probs, -1)

        delta = lax.cond(jnp.any(allowed), live_delta, lambda present_value: present_value, delta)
    grad_queries = jnp.zeros(query_matrix.shape, jnp.float32)
    key_terms = []
    for block_index, allowed in enumerate(block_masks):
        key_portion, value_portion = split_block(
            gathered, block_index * key_tile_block, key_tile_block
        )

        def live_grad(
            present_value, key_portion=key_portion, value_portion=value_portion, allowed=allowed
        ):
            probs = jnp.exp(
                block_scores(query_matrix, key_portion, allowed) - running_totals[..., None]
            )
            grad_probs = jnp.einsum(
                "sikgd,sjkd->skgij",
                mixed_gradient,
                value_portion,
                preferred_element_type=jnp.float32,
            )
            grad_scores = (probs * (grad_probs - delta[..., None])).astype(jnp.bfloat16)
            updated = present_value + jnp.einsum(
                "skgij,sjkd->sikgd", grad_scores, key_portion, preferred_element_type=jnp.float32
            ) * HEAD_SIZE ** (-0.5)
            grad_keys = jnp.einsum(
                "skgij,sikgd->sjkd", grad_scores, query_matrix, preferred_element_type=jnp.float32
            ) * HEAD_SIZE ** (-0.5)
            grad_values = jnp.einsum(
                "skgij,sikgd->sjkd",
                probs.astype(jnp.bfloat16),
                mixed_gradient,
                preferred_element_type=jnp.float32,
            )
            both_parts = jnp.concatenate(
                [
                    grad_keys.reshape(sequence_count, key_tile_block, -1),
                    grad_values.reshape(sequence_count, key_tile_block, -1),
                ],
                -1,
            )
            return (updated, both_parts)

        def dead_grad(present_value):
            return (
                present_value,
                jnp.zeros(
                    (sequence_count, key_tile_block, 2 * KEY_VALUE_HEADS * HEAD_SIZE), jnp.float32
                ),
            )

        grad_queries, block_term = lax.cond(jnp.any(allowed), live_grad, dead_grad, grad_queries)
        key_terms.append(block_term)
    return (grad_queries, jnp.concatenate(key_terms, 1), delta)


def expert_forward(inner_use, outer_use, received):
    model_width = received.shape[-1]
    rows_in = received.reshape(-1, model_width)
    pre_rows = jnp.dot(rows_in, inner_use, preferred_element_type=jnp.float32)
    slab_width = outer_use.shape[0]
    hidden_rows = (jax.nn.silu(pre_rows[:, :slab_width]) * pre_rows[:, slab_width:]).astype(
        jnp.bfloat16
    )
    part_rows = jnp.dot(hidden_rows, outer_use, preferred_element_type=jnp.float32).astype(
        jnp.bfloat16
    )
    return part_rows.reshape(received.shape)


def expert_back(inner_use, outer_use, rows_flat, grad_flat):
    pre_rows = jnp.dot(rows_flat, inner_use, preferred_element_type=jnp.float32)
    slab_width = outer_use.shape[0]
    gate_pre = pre_rows[:, :slab_width]
    up_pre = pre_rows[:, slab_width:]
    sigma = jax.nn.sigmoid(gate_pre)
    swish = gate_pre * sigma
    hidden_rows = (swish * up_pre).astype(jnp.bfloat16)
    grad_hidden = jnp.dot(grad_flat, outer_use.T, preferred_element_type=jnp.float32)
    grad_gate = grad_hidden * up_pre * sigma * (1.0 + gate_pre * (1.0 - sigma))
    grad_up = grad_hidden * swish
    grad_pre = jnp.concatenate([grad_gate, grad_up], 1).astype(jnp.bfloat16)
    grad_in = jnp.dot(grad_pre, inner_use.T, preferred_element_type=jnp.float32).astype(
        jnp.bfloat16
    )
    return (hidden_rows, grad_pre, grad_in)


def per_device(
    tokens,
    segment_ids,
    routes,
    query_weight,
    key_value_weight,
    output_weight,
    router_weight,
    gain_before,
    gain_middle,
    inner_weight,
    outer_weight,
    cotangent,
):
    sequence_count, resident_rows, model_width = tokens.shape
    token_count = sequence_count * resident_rows
    experts = router_weight.shape[1]
    copies = lax.axis_size("fsdp") // experts
    capacity = 3 * token_count // 8
    seg_all = lax.all_gather(segment_ids, "fsdp", axis=1, tiled=True)
    seq_length = seg_all.shape[1]
    key_tile_block = min(256, seq_length)
    positions = lax.axis_index("fsdp") * resident_rows + jnp.arange(resident_rows, dtype=jnp.int32)
    block_masks = [
        mask_for(seg_all, segment_ids, positions, offset, key_tile_block)
        for offset in range(0, seq_length, key_tile_block)
    ]
    start_rows = tokens.reshape(token_count, model_width).astype(jnp.float32)
    route_flat = routes.reshape(token_count * 2)
    picks = route_flat[:, None] == jnp.arange(experts, dtype=jnp.int32)[None, :]
    marks = picks.astype(jnp.int32)
    slot_index = route_flat * capacity + jnp.sum((jnp.cumsum(marks, 0) - marks) * marks, 1)
    chosen_mask = picks.reshape(token_count, 2, experts)

    def layer_weights():
        return (
            lax.all_gather(query_weight, ("dp", "fsdp"), axis=0, tiled=True),
            lax.all_gather(key_value_weight, ("dp", "fsdp"), axis=0, tiled=True),
            lax.all_gather(output_weight, ("dp", "fsdp"), axis=1, tiled=True),
            lax.all_gather(router_weight, ("dp", "fsdp"), axis=0, tiled=True),
            lax.all_gather(gain_before, ("dp", "fsdp"), axis=0, tiled=True),
            lax.all_gather(gain_middle, ("dp", "fsdp"), axis=0, tiled=True),
        )

    def expert_weights():
        inner_full, outer_full = (
            lax.all_gather(inner_weight, "dp", axis=0, tiled=True),
            lax.all_gather(outer_weight, "dp", axis=1, tiled=True),
        )
        return (inner_full.reshape(model_width, -1), outer_full)

    def attention_front(weights):
        normed, unit_rows, factor = normalize(start_rows, weights[4])
        normed_low = normed.astype(jnp.bfloat16)
        query_matrix = jnp.dot(normed_low, weights[0], preferred_element_type=jnp.float32).astype(
            jnp.bfloat16
        )
        query_matrix = query_matrix.reshape(
            sequence_count,
            resident_rows,
            KEY_VALUE_HEADS,
            QUERY_HEADS // KEY_VALUE_HEADS,
            HEAD_SIZE,
        )
        key_value_rows = jnp.dot(normed_low, weights[1], preferred_element_type=jnp.float32).astype(
            jnp.bfloat16
        )
        gathered = lax.all_gather(
            key_value_rows.reshape(sequence_count, resident_rows, -1), "fsdp", axis=1, tiled=True
        )
        return (normed_low, unit_rows, factor, query_matrix, gathered)

    def middle_part(weights, mixed_low):
        middle = start_rows + jnp.dot(mixed_low, weights[2], preferred_element_type=jnp.float32)
        expert_in, unit_rows, factor = normalize(middle, weights[5])
        expert_low = expert_in.astype(jnp.bfloat16)
        logits = jnp.dot(
            expert_low.astype(jnp.float32),
            weights[3].astype(jnp.float32),
            precision=HIGHEST_PRECISION,
        )
        return (middle, unit_rows, factor, expert_low, logits)

    def gates_for(logits):
        chosen_logits = jnp.sum(jnp.where(chosen_mask, logits[:, None, :], 0.0), -1)
        return jax.nn.softmax(chosen_logits, -1)

    def to_slots(pair_rows):
        packed = (
            jnp.zeros((experts * capacity, model_width), pair_rows.dtype)
            .at[slot_index]
            .set(pair_rows)
        )
        return jnp.repeat(packed.reshape(experts, capacity, model_width), copies, axis=0)

    def from_slots(returned_rows):
        summed = jnp.sum(
            returned_rows.reshape(experts, copies, capacity, model_width).astype(jnp.float32), 1
        )
        return summed.reshape(experts * capacity, model_width)[slot_index]

    weights = layer_weights()
    inner_all, outer_all = expert_weights()
    normed_low, unit_first, factor_first, query_matrix, gathered = attention_front(weights)
    running_totals = log_totals(query_matrix, gathered, block_masks, key_tile_block)
    mixed_low = attend_values(query_matrix, gathered, block_masks, key_tile_block, running_totals)
    middle, unit_second, factor_second, expert_low, logits = middle_part(weights, mixed_low)
    gates = gates_for(logits)
    sent = to_slots(jnp.repeat(expert_low, 2, axis=0))
    part_rows = expert_forward(
        inner_all, outer_all, lax.all_to_all(sent, "fsdp", split_axis=0, concat_axis=0, tiled=True)
    )
    returned_part = lax.all_to_all(part_rows, "fsdp", split_axis=0, concat_axis=0, tiled=True)
    returned_rows = returned_part
    expert_sum = from_slots(returned_rows).reshape(token_count, 2, model_width)
    block_out = (middle + jnp.sum(gates[..., None] * expert_sum, 1)).astype(jnp.bfloat16)
    grad_out = cotangent.reshape(token_count, model_width).astype(jnp.float32)
    weights = layer_weights()
    inner_use, outer_use = expert_weights()
    normed_low, unit_first, factor_first, query_matrix, gathered = attention_front(weights)
    mixed_low = attend_values(query_matrix, gathered, block_masks, key_tile_block, running_totals)
    middle, unit_second, factor_second, expert_low, logits = middle_part(weights, mixed_low)
    gates = gates_for(logits)
    sent = to_slots(jnp.repeat(expert_low, 2, axis=0))
    grad_sent = to_slots(
        (gates[..., None] * grad_out[:, None, :])
        .astype(jnp.bfloat16)
        .reshape(2 * token_count, model_width)
    )
    rows_in = lax.all_to_all(sent, "fsdp", split_axis=0, concat_axis=0, tiled=True)
    rows_grad = lax.all_to_all(grad_sent, "fsdp", split_axis=0, concat_axis=0, tiled=True)
    row_shape = rows_in.shape
    hidden_flat, grad_pre_flat, grad_in_flat = expert_back(
        inner_use, outer_use, rows_in.reshape(-1, model_width), rows_grad.reshape(-1, model_width)
    )
    part_rows = jnp.dot(hidden_flat, outer_use, preferred_element_type=jnp.float32).astype(
        jnp.bfloat16
    )
    grad_home = lax.all_to_all(
        grad_in_flat.reshape(row_shape), "fsdp", split_axis=0, concat_axis=0, tiled=True
    )
    part_home = lax.all_to_all(
        part_rows.reshape(row_shape), "fsdp", split_axis=0, concat_axis=0, tiled=True
    )
    item_shape = row_shape[:2]
    grad_pre = grad_pre_flat.reshape(item_shape + (-1,))
    hidden_rows = hidden_flat.reshape(item_shape + (-1,))
    expert_sum = from_slots(part_home).reshape(token_count, 2, model_width)
    rows_flat = rows_in.reshape(-1, model_width)
    row_total = rows_flat.shape[0]
    inner_grad_all = jnp.dot(
        rows_flat.T, grad_pre.reshape(row_total, -1), preferred_element_type=jnp.float32
    )
    outer_grad_all = jnp.dot(
        hidden_rows.reshape(row_total, -1).T,
        rows_grad.reshape(row_total, model_width),
        preferred_element_type=jnp.float32,
    )
    inner_grad, outer_grad = (
        lax.psum_scatter(
            inner_grad_all.reshape(model_width, 2, -1).astype(jnp.bfloat16),
            "dp",
            scatter_dimension=0,
            tiled=True,
        ).astype(jnp.float32),
        lax.psum_scatter(
            outer_grad_all.astype(jnp.bfloat16), "dp", scatter_dimension=1, tiled=True
        ).astype(jnp.float32),
    )
    grad_gates = jnp.sum(grad_out[:, None, :] * expert_sum, -1)
    grad_choice = gates * (grad_gates - jnp.sum(gates * grad_gates, -1, keepdims=True))
    grad_logits = jnp.sum(jnp.where(chosen_mask, grad_choice[..., None], 0.0), 1)
    router_grad_all = jnp.dot(
        expert_low.astype(jnp.float32).T, grad_logits, precision=HIGHEST_PRECISION
    )
    grad_expert_in = jnp.sum(from_slots(grad_home).reshape(token_count, 2, model_width), 1)
    grad_expert_in = grad_expert_in + jnp.dot(
        grad_logits, weights[3].astype(jnp.float32).T, precision=HIGHEST_PRECISION
    )
    grad_norm_second, middle_gain_grad = normalize_back(
        grad_expert_in, unit_second, factor_second, weights[5]
    )
    grad_middle = grad_out + grad_norm_second
    grad_branch = grad_middle.astype(jnp.bfloat16)
    output_grad_all = jnp.dot(mixed_low.T, grad_branch, preferred_element_type=jnp.float32)
    mixed_gradient = jnp.dot(grad_branch, weights[2].T, preferred_element_type=jnp.float32).astype(
        jnp.bfloat16
    )
    mixed_gradient = mixed_gradient.reshape(
        sequence_count, resident_rows, KEY_VALUE_HEADS, QUERY_HEADS // KEY_VALUE_HEADS, HEAD_SIZE
    )
    grad_queries, key_terms, delta = attend_back(
        query_matrix, mixed_gradient, gathered, block_masks, key_tile_block, running_totals
    )
    key_grads = lax.psum_scatter(
        key_terms.astype(jnp.bfloat16), "fsdp", scatter_dimension=1, tiled=True
    ).reshape(token_count, -1)
    query_low = grad_queries.reshape(token_count, -1).astype(jnp.bfloat16)
    grad_normed = jnp.dot(query_low, weights[0].T, preferred_element_type=jnp.float32) + jnp.dot(
        key_grads, weights[1].T, preferred_element_type=jnp.float32
    )
    query_grad_all = jnp.dot(normed_low.T, query_low, preferred_element_type=jnp.float32)
    keyval_grad_all = jnp.dot(normed_low.T, key_grads, preferred_element_type=jnp.float32)
    grad_norm_first, before_gain_grad = normalize_back(
        grad_normed, unit_first, factor_first, weights[4]
    )
    tokens_grad = grad_middle + grad_norm_first
    summed_grads = (
        lax.psum_scatter(query_grad_all, ("dp", "fsdp"), scatter_dimension=0, tiled=True),
        lax.psum_scatter(keyval_grad_all, ("dp", "fsdp"), scatter_dimension=0, tiled=True),
        lax.psum_scatter(output_grad_all, ("dp", "fsdp"), scatter_dimension=1, tiled=True),
        lax.psum_scatter(router_grad_all, ("dp", "fsdp"), scatter_dimension=0, tiled=True),
        lax.psum_scatter(before_gain_grad, ("dp", "fsdp"), scatter_dimension=0, tiled=True),
        lax.psum_scatter(middle_gain_grad, ("dp", "fsdp"), scatter_dimension=0, tiled=True),
    )
    return (
        block_out.reshape(sequence_count, resident_rows, model_width),
        tokens_grad.reshape(sequence_count, resident_rows, model_width),
        summed_grads[0],
        summed_grads[1],
        summed_grads[2],
        summed_grads[3],
        summed_grads[4],
        summed_grads[5],
        inner_grad,
        outer_grad,
    )


def solution(mesh):
    in_specs = (
        P("dp", "fsdp", None),
        P("dp", "fsdp"),
        P("dp", "fsdp", None),
        P(("dp", "fsdp"), None),
        P(("dp", "fsdp"), None),
        P(None, ("dp", "fsdp")),
        P(("dp", "fsdp"), None),
        P(("dp", "fsdp")),
        P(("dp", "fsdp")),
        P("dp", None, "fsdp"),
        P("fsdp", "dp"),
        P("dp", "fsdp", None),
    )
    out_specs = (
        P("dp", "fsdp", None),
        P("dp", "fsdp", None),
        P(("dp", "fsdp"), None),
        P(("dp", "fsdp"), None),
        P(None, ("dp", "fsdp")),
        P(("dp", "fsdp"), None),
        P(("dp", "fsdp")),
        P(("dp", "fsdp")),
        P("dp", None, "fsdp"),
        P("fsdp", "dp"),
    )
    return jax.shard_map(
        per_device, mesh=mesh, in_specs=in_specs, out_specs=out_specs, check_vma=False
    )
```

profile of v0, /device:TPU:1, one launch (start us, length us, event | category | flops | bytes accessed | tf_op | source)
XLA Modules:
  0.0 1465.9 jit_solution(2441711517841797913)
XLA Ops:
  10.4 41.2 %all-reduce.5 = (bf16[1536]{0:T(1024)(128)(2,1)S(1)}, bf16[1536]{0:T(1024)(128)(2,1)S(1)}) all-reduce(bf16[1536]{0:T(1024)(128)(2,1)S(1)} %dynamic-update-slice, bf16[1536]{0:T(1024)(128)(2,1)S(1)} %dynamic-update-slice.1), channel_id=1, replica_groups=mesh['dp'=4,'fsdp'=8] {'dp','fsdp'}, use_global_device_ids=true, to_apply=%add | all-reduce | flops 3072 | bytes 12288
  53.1 19.6 %all-gather.9.cloned.1.call-done = bf16[1536,1024]{1,0:T(8,128)(2,1)} async-done(((bf16[48,1024]{1,0:T(8,128)(2,1)}), bf16[1536,1024]{1,0:T(8,128)(2,1)}) %all-gather.9.cloned.1.call-update) | async-done | bytes 3145744 | tf_op jit(solution)/shard_map/all_gather | solution.py:250
  78.3 10.6 all_gather.39
  98.1 40.2 %all-gather.11.cloned.1.call-done = bf16[1536,1536]{1,0:T(8,128)(2,1)} async-done(((bf16[48,1536]{1,0:T(8,128)(2,1)}), bf16[1536,1536]{1,0:T(8,128)(2,1)}) %all-gather.11.cloned.1.call-update) | async-done | bytes 4718608 | tf_op jit(solution)/shard_map/all_gather | solution.py:249
  142.3 44.1 %all-gather.19.cloned.1.call-done = bf16[2048,1024]{1,0:T(8,128)(2,1)} async-done(((bf16[256,1024]{1,0:T(8,128)(2,1)}), bf16[2048,1024]{1,0:T(8,128)(2,1)}) %all-gather.19.cloned.1.call-update) | async-done | bytes 4194320 | tf_op jit(solution)/shard_map/all_gather | solution.py:280
  203.7 7.9 conditional.46
  238.6 5.1 conditional.49
  261.4 5.9 scatter_custom_fusion.2
  267.3 64.7 %all-to-all-start.3 = ((bf16[8,96,1536]{2,1,0:T(8,128)(2,1)}), bf16[8,96,1536]{2,1,0:T(8,128)(2,1)}, u32[]{:S(2)}, u32[]{:S(2)}) async-start(bf16[8,96,1536]{2,1,0:T(8,128)(2,1)} %bitcast.2179), calls=%async_computation.3 | async-start | bytes 4718592 | tf_op jit(solution)/shard_map/all_to_all | solution.py:342
  332.6 8.1 copy.605
  340.7 45.2 %all-to-all-done.3 = bf16[8,96,1536]{2,1,0:T(8,128)(2,1)} async-done(((bf16[8,96,1536]{2,1,0:T(8,128)(2,1)}), bf16[8,96,1536]{2,1,0:T(8,128)(2,1)}, u32[]{:S(2)}, u32[]{:S(2)}) %all-to-all-start.3) | async-done | bytes 2359328 | tf_op jit(solution)/shard_map/all_to_all | solution.py:342
  386.0 7.9 fusion.675
  397.5 6.2 convolution_convert_fusion.2
  403.7 5.3 all-to-all-start.5
  409.0 83.9 %all-gather.1 = bf16[32,48,8]{1,2,0:T(8,128)(2,1)S(1)} all-gather(bf16[1,48,8]{1,2,0:T(8,128)(2,1)S(1)} %bitcast.2427), channel_id=1, replica_groups=mesh['dp'=4,'fsdp'=8] {'dp','fsdp'}, dimensions={0}, use_global_device_ids=true | all-gather | bytes 25344 | tf_op jit(solution)/shard_map/all_gather | solution.py:252
  497.1 5.2 mul.847
  507.2 6.9 gather_fusion.2
  514.1 5.1 gather.14
  523.5 5.1 scatter_custom_fusion.1
  528.7 56.8 %all_to_all.30 = bf16[8,96,1536]{2,1,0:T(8,128)(2,1)S(1)} all-to-all(bf16[8,96,1536]{2,1,0:T(8,128)(2,1)S(1)} %bitcast.2181), channel_id=1, replica_groups=mesh['dp'=4,'fsdp'=8] {'fsdp'}, dimensions={0} | all-to-all | bytes 4718592 | tf_op jit(solution)/shard_map/all_to_all | solution.py:343
  585.5 6.6 multiply_convert_fusion.2
  592.2 6.4 convolution_convert_fusion.4
  606.5 50.4 %all-to-all-done.4 = bf16[8,96,1536]{2,1,0:T(8,128)(2,1)S(1)} async-done(((bf16[8,96,1536]{2,1,0:T(8,128)(2,1)}), bf16[8,96,1536]{2,1,0:T(8,128)(2,1)S(1)}, u32[]{:S(2)}, u32[]{:S(2)}) %all-to-all-start.4) | async-done | bytes 2359328 | tf_op jit(solution)/shard_map/all_to_all | solution.py:351
  659.9 7.0 gather_fusion.1
  667.0 5.2 reshape.2867
  672.2 6.8 reduce_sum.341
  699.7 12.1 conditional.72
  712.6 7.4 conditional.73
  722.8 6.0 conditional.76
  730.4 6.6 conditional.78
  750.3 6.5 convolution_convert_fusion.1
  770.2 9.3 convolution_convert_fusion
  780.5 6.5 fusion.643
  788.3 5.1 fusion.648
  801.5 95.8 %all_to_all.31 = bf16[8,96,1536]{2,1,0:T(8,128)(2,1)S(1)} all-to-all(bf16[8,96,1536]{2,1,0:T(8,128)(2,1)S(1)} %bitcast.2180), channel_id=1, replica_groups=mesh['dp'=4,'fsdp'=8] {'fsdp'}, dimensions={0} | all-to-all | bytes 4718592 | tf_op jit(solution)/shard_map/all_to_all | solution.py:323
  897.3 9.7 fusion.673
  911.9 7.9 convolution_convert_fusion.3
  919.8 4.9 all-to-all-start.1
  925.0 53.8 %all-to-all-done.1 = bf16[8,96,1536]{2,1,0:T(8,128)(2,1)S(1)} async-done(((bf16[8,96,1536]{2,1,0:T(8,128)(2,1)}), bf16[8,96,1536]{2,1,0:T(8,128)(2,1)S(1)}, u32[]{:S(2)}, u32[]{:S(2)}) %all-to-all-start.1) | async-done | bytes 2359328 | tf_op jit(solution)/shard_map/all_to_all | solution.py:325
  981.7 7.0 gather_fusion
  988.7 5.2 reshape.2859
  993.9 6.6 multiply_reduce_fusion.1
  1003.0 5.3 fusion.676
  1011.1 5.5 fusion.625
  1016.6 38.1 %all-reduce.4 = (f32[1536]{0:T(1024)S(1)}, f32[1536]{0:T(1024)S(1)}) all-reduce(f32[1536]{0:T(1024)S(1)} %get-tuple-element.1217, f32[1536]{0:T(1024)S(1)} %copy-done.103), channel_id=8, replica_groups=mesh['dp'=4,'fsdp'=8] {'dp','fsdp'}, use_global_device_ids=true, to_apply=%region_140.141.clone | all-reduce | flops 3072 | bytes 24576
  1063.5 133.7 %reduce-scatter.18.cloned.1.call-done = f32[1536,48]{0,1:T(8,128)} async-done(((f32[1536,1536]{0,1:T(8,128)}), f32[1536,48]{0,1:T(8,128)}) %reduce-scatter.18.cloned.1.call-update) | async-done | bytes 294928 | tf_op jit(solution)/shard_map/reduce_scatter | solution.py:423
  1197.2 142.2 %reduce-scatter.14.cloned.1.call-done = f32[48,1536]{1,0:T(8,128)} async-done(((f32[1536,1536]{1,0:T(8,128)}), f32[48,1536]{1,0:T(8,128)}) %reduce-scatter.14.cloned.1.call-update) | async-done | bytes 294928 | tf_op jit(solution)/shard_map/reduce_scatter | solution.py:421
  1339.4 119.7 %reduce-scatter.16.cloned.1.call-done = f32[48,1024]{1,0:T(8,128)} async-done(((f32[1536,1024]{1,0:T(8,128)}), f32[48,1024]{1,0:T(8,128)}) %reduce-scatter.16.cloned.1.call-update) | async-done | bytes 196624 | tf_op jit(solution)/shard_map/reduce_scatter | solution.py:422
  (405 shorter events, 239.0 us)
Async XLA Ops:
  7.2 65.5 %all-gather.9.cloned.1.call-start = ((), (), s32[]{:S(2)}) async-start(), calls=%async_computation.13 | async-start | bytes 3244032 | tf_op jit(solution)/shard_map/all_gather | solution.py:250
  7.9 130.4 %all-gather.11.cloned.1.call-start = ((), (), s32[]{:S(2)}) async-start(), calls=%async_computation.14 | async-start | bytes 4866048 | tf_op jit(solution)/shard_map/all_gather | solution.py:249
  8.7 177.8 %all-gather.19.cloned.1.call-start = ((), (), s32[]{:S(2)}) async-start(), calls=%async_computation.23 | async-start | bytes 4718592 | tf_op jit(solution)/shard_map/all_gather | solution.py:280
  51.6 86.7 %copy-start.80 = (f32[1536]{0:T(1024)}, f32[1536]{0:T(1024)S(1)}, u32[]{:S(2)}) copy-start(f32[1536]{0:T(1024)S(1)} %convert_element_type.316) | copy-start | bytes 18436
  51.6 26.2 %copy-start.104 = (s32[1,256,2]{1,2,0:T(2,128)S(1)}, s32[1,256,2]{1,2,0:T(2,128)}, u32[]{:S(2)}) copy-start(s32[1,256,2]{1,2,0:T(2,128)} %param.94) | copy-start | bytes 6148
  53.0 25.3 %copy-start.112 = (s32[1,256]{1,0:T(1,128)S(1)}, s32[1,256]{1,0:T(1,128)}, u32[]{:S(2)}) copy-start(s32[1,256]{1,0:T(1,128)} %param.93) | copy-start | bytes 3076
  53.0 85.3 %copy-start.101 = (f32[256]{0:T(256)}, f32[256]{0:T(256)S(1)}, u32[]{:S(2)}) copy-start(f32[256]{0:T(256)S(1)} %add_rsqrt_fusion.2) | copy-start | bytes 3076
  53.0 85.3 %copy-start = (bf16[1,256,1536]{2,1,0:T(8,128)(2,1)S(1)}, bf16[1,256,1536]{2,1,0:T(8,128)(2,1)}, u32[]{:S(2)}) copy-start(bf16[1,256,1536]{2,1,0:T(8,128)(2,1)} %param.92) | copy-start | bytes 2359300
  76.7 175.4 %all-gather.13.cloned.1.call-start = ((), (), s32[]{:S(2)}) async-start(), calls=%async_computation.15 | async-start | bytes 4866048 | tf_op jit(solution)/shard_map/all_gather | solution.py:251
  77.3 255.4 %all-gather.15.cloned.1.call-start = ((), (), s32[]{:S(2)}) async-start(), calls=%async_computation.16 | async-start | bytes 7864320 | tf_op jit(solution)/shard_map/all_gather | solution.py:259
  98.1 163.3 %copy-start.110 = (s32[512,1]{0,1:T(1,128)}, s32[512,1]{0,1:T(1,128)S(1)}, u32[]{:S(2)}) copy-start(s32[512,1]{0,1:T(1,128)S(1)} %compare_select_fusion) | copy-start | bytes 6148
  191.0 47.6 %copy-start.21 = (bf16[1,256,512]{1,2,0:T(8,128)(2,1)}, bf16[1,256,512]{1,2,0:T(8,128)(2,1)S(1)}, u32[]{:S(2)}) copy-start(bf16[1,256,512]{1,2,0:T(8,128)(2,1)S(1)} %copy.443) | copy-start | bytes 786436
  191.1 52.6 %copy-start.18 = (bf16[1,256,512]{1,2,0:T(8,128)(2,1)}, bf16[1,256,512]{1,2,0:T(8,128)(2,1)S(1)}, u32[]{:S(2)}) copy-start(bf16[1,256,512]{1,2,0:T(8,128)(2,1)S(1)} %copy.444) | copy-start | bytes 786436
  191.3 53.3 %copy-start.15 = (bf16[1,256,512]{1,2,0:T(8,128)(2,1)}, bf16[1,256,512]{1,2,0:T(8,128)(2,1)S(1)}, u32[]{:S(2)}) copy-start(bf16[1,256,512]{1,2,0:T(8,128)(2,1)S(1)} %copy.445) | copy-start | bytes 786436
  191.4 54.0 %copy-start.13 = (bf16[1,256,512]{1,2,0:T(8,128)(2,1)}, bf16[1,256,512]{1,2,0:T(8,128)(2,1)S(1)}, u32[]{:S(2)}) copy-start(bf16[1,256,512]{1,2,0:T(8,128)(2,1)S(1)} %copy.446) | copy-start | bytes 786436
  191.6 54.8 %copy-start.11 = (bf16[1,256,512]{1,2,0:T(8,128)(2,1)}, bf16[1,256,512]{1,2,0:T(8,128)(2,1)S(1)}, u32[]{:S(2)}) copy-start(bf16[1,256,512]{1,2,0:T(8,128)(2,1)S(1)} %copy.447) | copy-start | bytes 786436
  191.7 55.7 %copy-start.9 = (bf16[1,256,512]{1,2,0:T(8,128)(2,1)}, bf16[1,256,512]{1,2,0:T(8,128)(2,1)S(1)}, u32[]{:S(2)}) copy-start(bf16[1,256,512]{1,2,0:T(8,128)(2,1)S(1)} %copy.448) | copy-start | bytes 786436
  259.1 243.2 %copy-start.6 = (bf16[256,1536]{1,0:T(8,128)(2,1)}, bf16[256,1536]{1,0:T(8,128)(2,1)S(1)}, u32[]{:S(2)}) copy-start(bf16[256,1536]{1,0:T(8,128)(2,1)S(1)} %get-tuple-element.1275) | copy-start | bytes 2359300
  267.3 118.7 %all-to-all-start.3 = ((bf16[8,96,1536]{2,1,0:T(8,128)(2,1)}), bf16[8,96,1536]{2,1,0:T(8,128)(2,1)}, u32[]{:S(2)}, u32[]{:S(2)}) async-start(bf16[8,96,1536]{2,1,0:T(8,128)(2,1)} %bitcast.2179), calls=%async_computation.3 | async-start | bytes 4718592 | tf_op jit(solution)/shard_map/all_to_all | solution.py:342
  332.0 65.4 %all-gather.17.cloned.1.call-start = ((), (), s32[]{:S(2)}) async-start(), calls=%async_computation.17 | async-start | bytes 3932160 | tf_op jit(solution)/shard_map/all_gather | solution.py:260
  397.4 6.3 copy-start.46
  403.7 99.1 %all-to-all-start.5 = ((bf16[8,96,1536]{2,1,0:T(8,128)(2,1)}), bf16[8,96,1536]{2,1,0:T(8,128)(2,1)}, u32[]{:S(2)}, u32[]{:S(2)}) async-start(bf16[8,96,1536]{2,1,0:T(8,128)(2,1)} %bitcast.2237), calls=%async_computation.5 | async-start | bytes 4718592 | tf_op jit(solution)/shard_map/all_to_all | solution.py:354
  502.3 11.7 copy-start.106
  528.7 56.9 %copy-start.115 = (bf16[1024,1536]{1,0:T(8,128)(2,1)S(1)}, bf16[1024,1536]{1,0:T(8,128)(2,1)}, u32[]{:S(2)}) copy-start(bf16[1024,1536]{1,0:T(8,128)(2,1)} %all-gather.17.cloned.1.call-done) | copy-start | bytes 9437188
  528.7 63.5 %slice-start = ((s8[6291456]{0:T(1024)(128)(4,1)}), s8[4194304]{0:T(1024)(128)(4,1)S(1)}, s32[]{:S(2)}) async-start(s8[6291456]{0:T(1024)(128)(4,1)} %bitcast.2224), calls=%async_computation.26 | async-start | bytes 8388608
  585.5 6.6 copy-start.34
  585.5 6.7 slice-start.1
  592.2 6.4 copy-start.44
  592.2 6.4 copy-start.45
  598.6 58.4 %all-to-all-start.4 = ((bf16[8,96,1536]{2,1,0:T(8,128)(2,1)}), bf16[8,96,1536]{2,1,0:T(8,128)(2,1)S(1)}, u32[]{:S(2)}, u32[]{:S(2)}) async-start(bf16[8,96,1536]{2,1,0:T(8,128)(2,1)} %bitcast.2238), calls=%async_computation.4 | async-start | bytes 4718592 | tf_op jit(solution)/shard_map/all_to_all | solution.py:351
  603.1 303.9 %reduce-scatter.12.cloned.1.call-start = ((), (), s32[]{:S(2)}) async-start(), calls=%async_computation.18 | async-start | bytes 4718592 | tf_op jit(solution)/shard_map/reduce_scatter | solution.py:407
  667.0 12.0 copy-start.5
  667.0 12.0 copy-start.109
  672.2 10.1 copy-start.31
  688.0 11.7 copy-start.47
  737.9 7.6 copy-start.41
  737.9 8.5 copy-start.43
  748.1 253.4 %reduce-scatter.22.cloned.1.call-start = ((), (), s32[]{:S(2)}) async-start(), calls=%async_computation.24 | async-start | bytes 811008
  750.0 258.3 %reduce-scatter.24.cloned.1.call-start = ((), (), s32[]{:S(2)}) async-start(), calls=%async_computation.25 | async-start | bytes 3932160
  761.5 297.3 %reduce-scatter.20.cloned.1.call-start = ((), (), s32[]{:S(2)}) async-start(), calls=%async_computation.22 | async-start | bytes 7864320 | tf_op jit(solution)/shard_map/reduce_scatter | solution.py:372
  779.4 417.8 %reduce-scatter.18.cloned.1.call-start = ((), (), s32[]{:S(2)}) async-start(), calls=%async_computation.21 | async-start | bytes 9732096 | tf_op jit(solution)/shard_map/reduce_scatter | solution.py:423
  787.1 552.3 %reduce-scatter.14.cloned.1.call-start = ((), (), s32[]{:S(2)}) async-start(), calls=%async_computation.19 | async-start | bytes 9732096 | tf_op jit(solution)/shard_map/reduce_scatter | solution.py:421
  793.4 665.7 %reduce-scatter.16.cloned.1.call-start = ((), (), s32[]{:S(2)}) async-start(), calls=%async_computation.20 | async-start | bytes 6488064 | tf_op jit(solution)/shard_map/reduce_scatter | solution.py:422
  919.8 58.9 %all-to-all-start.1 = ((bf16[8,96,1536]{2,1,0:T(8,128)(2,1)}), bf16[8,96,1536]{2,1,0:T(8,128)(2,1)S(1)}, u32[]{:S(2)}, u32[]{:S(2)}) async-start(bf16[8,96,1536]{2,1,0:T(8,128)(2,1)} %bitcast.2236), calls=%async_computation.1 | async-start | bytes 4718592 | tf_op jit(solution)/shard_map/all_to_all | solution.py:325
  924.7 57.0 %copy-start.107 = (s32[1024]{0:T(1024)S(1)}, s32[1024]{0:T(1024)}, u32[]{:S(2)}) copy-start(s32[1024]{0:T(1024)} %copy-done.106) | copy-start | bytes 12292
  988.7 11.8 copy-start.28
  993.9 9.1 copy-start.33
  1011.1 44.7 %copy-start.3 = (f32[256,1536]{1,0:T(8,128)S(1)}, f32[256,1536]{1,0:T(8,128)}, u32[]{:S(2)}) copy-start(f32[256,1536]{1,0:T(8,128)} %copy-done.2) | copy-start | bytes 4718596
  (63 other events, 119.5 us)
Sparse Core Ops, SparseCore 0:
  11.0 61.6 all-gather.8
  75.7 62.5 all-gather.10
  140.5 45.9 all-gather.18
  189.3 62.2 all-gather.12
  253.3 68.5 all-gather.14
  334.4 44.6 all-gather.16
  748.3 82.7 reduce-scatter.11
  836.1 94.6 reduce-scatter.21
  933.8 48.8 reduce-scatter.23
  985.5 71.6 reduce-scatter.19
  1063.6 133.5 reduce-scatter.17
  1204.6 134.7 reduce-scatter.13
  1345.6 113.4 reduce-scatter.15
where the time goes:
time: 1480 us; the launch traced here: 1470 us
  waiting for transfers between devices  652 us (44%)
  blocking collectives  326 us (22%)
  matrix products  154 us (10%)
  local copies, waits for them, and re-layouts  143 us (10%)
  starting transfers between devices  80.6 us (5%)
  other arithmetic  60.7 us (4%)
  loops' own time  29.2 us (2%)
  between operations  20.4 us (1%)
    reduce_scatter x1, waiting for transfers between devices, per_device(): lax.psum_scatter(query_grad_all, ('dp', 'fsdp'), scatter_dimension=0, til...  142 us
    reduce_scatter x1, waiting for transfers between devices, per_device(): lax.psum_scatter(output_grad_all, ('dp', 'fsdp'), scatter_dimension=1, ti...  134 us
    reduce_scatter x1, waiting for transfers between devices, per_device(): lax.psum_scatter(keyval_grad_all, ('dp', 'fsdp'), scatter_dimension=0, ti...  120 us
    all_to_all x1, blocking collectives, per_device(): lax.all_to_all(sent, 'fsdp', split_axis=0, concat_axis=0, tiled=True)  95.8 us
    all_gather x1, blocking collectives, layer_weights(): lax.all_gather(router_weight, ('dp', 'fsdp'), axis=0, tiled=True)  83.9 us
    unnamed x2, blocking collectives  79.2 us
    all_to_all x1, starting transfers between devices, per_device(): lax.all_to_all(sent, 'fsdp', split_axis=0, concat_axis=0, tiled=True)  64.7 us
    all_to_all x1, blocking collectives, per_device(): lax.all_to_all(grad_sent, 'fsdp', split_axis=0, concat_axis=0, tiled=True)  56.8 us
  transfers between devices with their start and end apart: 17, of which 9 were waited for; matrix products, arithmetic and copies ran while one was open for 16% of the time, Pallas kernels for 0%

commit v1 on v0

--- a/solution.py
+++ b/solution.py
@@ -1,6 +1,8 @@
 import jax
 import jax.numpy as jnp
 from jax import lax
+from jax.experimental import pallas as pl
+from jax.experimental.pallas import tpu as pltpu
 from jax.sharding import PartitionSpec as P
 
 QUERY_HEADS = 24
@@ -439,7 +441,549 @@
     )
 
 
+def attend_kernel(spans, q_ref, k_ref, v_ref, segr_ref, segc_ref, o_ref, ot_ref, lse_ref):
+    step = pl.program_id(0)
+    block = q_ref.shape[0]
+    heads = q_ref.shape[1] // HEAD_SIZE
+    queries = q_ref[...] * jnp.bfloat16(HEAD_SIZE ** (-0.5))
+    stacked = jnp.concatenate(
+        [queries[:, h * HEAD_SIZE : (h + 1) * HEAD_SIZE] for h in range(heads)], 0
+    )
+    seg_row = segr_ref[...]
+
+    def scores_of(j):
+        keys = k_ref[pl.ds(pl.multiple_of(j * block, block), block), :]
+        return lax.dot_general(
+            keys, stacked, (((1,), (1,)), ((), ())), preferred_element_type=jnp.float32
+        )
+
+    def same_doc(j):
+        seg_col = segc_ref[pl.ds(pl.multiple_of(j * block, block), block), :]
+        return seg_col == seg_row
+
+    def fold(j, scores, carry):
+        top, total, out = carry
+        values = v_ref[pl.ds(pl.multiple_of(j * block, block), block), :]
+        new_top = jnp.maximum(top, jnp.max(scores, 0, keepdims=True))
+        probs = jnp.exp(scores - new_top)
+        decay = jnp.exp(top - new_top)
+        total = total * decay + jnp.sum(probs, 0, keepdims=True)
+        out = out * decay + lax.dot_general(
+            values,
+            probs.astype(jnp.bfloat16),
+            (((0,), (0,)), ((), ())),
+            preferred_element_type=jnp.float32,
+        )
+        return (new_top, total, out)
+
+    def masked(j, carry):
+        allowed = jnp.concatenate([same_doc(j)] * heads, 1)
+        return fold(j, jnp.where(allowed, scores_of(j), NEGATIVE_LARGE), carry)
+
+    def whole(j, carry):
+        return fold(j, scores_of(j), carry)
+
+    columns = heads * block
+    carry = (
+        jnp.full((1, columns), NEGATIVE_LARGE, jnp.float32),
+        jnp.zeros((1, columns), jnp.float32),
+        jnp.zeros((HEAD_SIZE, columns), jnp.float32),
+    )
+    first, full = spans[0, step], spans[1, step]
+    carry = lax.fori_loop(first, full, masked, carry)
+    carry = lax.fori_loop(full, step, whole, carry)
+    key_spot = lax.broadcasted_iota(jnp.int32, (block, block), 0)
+    query_spot = lax.broadcasted_iota(jnp.int32, (block, block), 1)
+    allowed = same_doc(step) & (key_spot <= query_spot)
+    allowed = jnp.concatenate([allowed] * heads, 1)
+    top, total, out = fold(step, jnp.where(allowed, scores_of(step), NEGATIVE_LARGE), carry)
+    out = out / total
+    totals = top + jnp.log(total)
+    for h in range(heads):
+        part = out[:, h * block : (h + 1) * block]
+        ot_ref[h * HEAD_SIZE : (h + 1) * HEAD_SIZE, :] = part
+        lse_ref[h : h + 1, :] = totals[:, h * block : (h + 1) * block]
+    o_ref[...] = jnp.concatenate(
+        [out[:, h * block : (h + 1) * block].T for h in range(heads)], 1
+    ).astype(jnp.bfloat16)
+
+
+def attend_back_kernel(
+    spans, q_ref, g_ref, k_ref, v_ref, segr_ref, segc_ref, ot_ref, lse_ref,
+    dq_ref, dkv_ref, dk_sum, dv_sum,
+):
+    step = pl.program_id(0)
+    block = q_ref.shape[0]
+    heads = q_ref.shape[1] // HEAD_SIZE
+    queries = q_ref[...] * jnp.bfloat16(HEAD_SIZE ** (-0.5))
+    grads = g_ref[...]
+    cuts = [slice(h * HEAD_SIZE, (h + 1) * HEAD_SIZE) for h in range(heads)]
+    stacked = jnp.concatenate([queries[:, cut] for cut in cuts], 0)
+    stacked_grad = jnp.concatenate([grads[:, cut] for cut in cuts], 0)
+    delta = jnp.concatenate(
+        [
+            jnp.sum(grads[:, cut].astype(jnp.float32).T * ot_ref[cut, :], 0, keepdims=True)
+            for cut in cuts
+        ],
+        1,
+    )
+    totals = jnp.concatenate([lse_ref[h : h + 1, :] for h in range(heads)], 1)
+    seg_row = segr_ref[...]
+
+    @pl.when(step == 0)
+    def _():
+        dk_sum[...] = jnp.zeros_like(dk_sum)
+        dv_sum[...] = jnp.zeros_like(dv_sum)
+
+    def turn(j, query_sum, allowed):
+        rows = pl.ds(pl.multiple_of(j * block, block), block)
+        keys, values = k_ref[rows, :], v_ref[rows, :]
+        scores = lax.dot_general(
+            keys, stacked, (((1,), (1,)), ((), ())), preferred_element_type=jnp.float32
+        )
+        probs = jnp.exp(scores - totals)
+        if allowed is not None:
+            probs = jnp.where(jnp.concatenate([allowed] * heads, 1), probs, 0.0)
+        grad_probs = lax.dot_general(
+            values, stacked_grad, (((1,), (1,)), ((), ())), preferred_element_type=jnp.float32
+        )
+        grad_scores = (probs * (grad_probs - delta)).astype(jnp.bfloat16)
+        dv_sum[rows, :] += jnp.dot(
+            probs.astype(jnp.bfloat16), stacked_grad, preferred_element_type=jnp.float32
+        )
+        dk_sum[rows, :] += jnp.dot(grad_scores, stacked, preferred_element_type=jnp.float32)
+        return query_sum + lax.dot_general(
+            keys, grad_scores, (((0,), (0,)), ((), ())), preferred_element_type=jnp.float32
+        )
+
+    def same_doc(j):
+        seg_col = segc_ref[pl.ds(pl.multiple_of(j * block, block), block), :]
+        return seg_col == seg_row
+
+    query_sum = jnp.zeros((HEAD_SIZE, heads * block), jnp.float32)
+    first, full = spans[0, step], spans[1, step]
+    query_sum = lax.fori_loop(first, full, lambda j, c: turn(j, c, same_doc(j)), query_sum)
+    query_sum = lax.fori_loop(full, step, lambda j, c: turn(j, c, None), query_sum)
+    key_spot = lax.broadcasted_iota(jnp.int32, (block, block), 0)
+    query_spot = lax.broadcasted_iota(jnp.int32, (block, block), 1)
+    query_sum = turn(step, query_sum, same_doc(step) & (key_spot <= query_spot))
+    query_sum = query_sum * HEAD_SIZE ** (-0.5)
+    dq_ref[...] = jnp.concatenate(
+        [query_sum[:, h * block : (h + 1) * block].T for h in range(heads)], 1
+    ).astype(jnp.bfloat16)
+
+    @pl.when(step == pl.num_programs(0) - 1)
+    def _():
+        dkv_ref[...] = jnp.concatenate([dk_sum[...], dv_sum[...]], 1).astype(jnp.bfloat16)
+
+
+def attention_specs(length, block, wide):
+    along = lambda width: pl.BlockSpec((block, width), lambda i, spans: (i, 0))
+    across = lambda height: pl.BlockSpec((height, block), lambda i, spans: (0, i))
+    fixed = lambda width: pl.BlockSpec((length, width), lambda i, spans: (0, 0))
+    return along, across, fixed
+
+
+def attend(spans, queries, keys, values, seg_row, seg_col, block):
+    length, wide = queries.shape
+    along, across, fixed = attention_specs(length, block, wide)
+    return pl.pallas_call(
+        attend_kernel,
+        grid_spec=pltpu.PrefetchScalarGridSpec(
+            num_scalar_prefetch=1,
+            grid=(length // block,),
+            in_specs=[along(wide), fixed(HEAD_SIZE), fixed(HEAD_SIZE), across(1), fixed(1)],
+            out_specs=[along(wide), across(wide), across(8)],
+        ),
+        out_shape=[
+            jax.ShapeDtypeStruct((length, wide), jnp.bfloat16),
+            jax.ShapeDtypeStruct((wide, length), jnp.float32),
+            jax.ShapeDtypeStruct((8, length), jnp.float32),
+        ],
+        compiler_params=pltpu.CompilerParams(vmem_limit_bytes=48 * 2**20),
+        name="attend",
+    )(spans, queries, keys, values, seg_row, seg_col)
+
+
+def attend_backward(
+    spans, queries, grads, keys, values, seg_row, seg_col, mixed_t, totals, block
+):
+    length, wide = queries.shape
+    along, across, fixed = attention_specs(length, block, wide)
+    return pl.pallas_call(
+        attend_back_kernel,
+        grid_spec=pltpu.PrefetchScalarGridSpec(
+            num_scalar_prefetch=1,
+            grid=(length // block,),
+            in_specs=[
+                along(wide), along(wide), fixed(HEAD_SIZE), fixed(HEAD_SIZE), across(1), fixed(1),
+                across(wide), across(8),
+            ],
+            out_specs=[along(wide), fixed(2 * HEAD_SIZE)],
+            scratch_shapes=[
+                pltpu.VMEM((length, HEAD_SIZE), jnp.float32),
+                pltpu.VMEM((length, HEAD_SIZE), jnp.float32),
+            ],
+        ),
+        out_shape=[
+            jax.ShapeDtypeStruct((length, wide), jnp.bfloat16),
+            jax.ShapeDtypeStruct((length, 2 * HEAD_SIZE), jnp.bfloat16),
+        ],
+        compiler_params=pltpu.CompilerParams(vmem_limit_bytes=48 * 2**20),
+        name="attend_backward",
+    )(spans, queries, grads, keys, values, seg_row, seg_col, mixed_t, totals)
+
+
+def flip_exchange(block, axis, flip):
+    count = lax.axis_size(axis)
+    return lax.ppermute(block, axis, [(i, i ^ flip) for i in range(count)])
+
+
+def swap_blocks(blocks, axis):
+    return [blocks[0]] + [flip_exchange(blocks[k], axis, k) for k in range(1, len(blocks))]
+
+
+def line_gather(own):
+    count = lax.axis_size("fsdp")
+    chips = count // 2
+    place = lax.axis_index("fsdp") // 2
+    ups, downs = [own], [own]
+    for step in range(1, chips):
+        ups.append(
+            lax.ppermute(ups[-1], "fsdp", [(i, i + 2) for i in range(2 * (step - 1), count - 2)])
+        )
+        downs.append(
+            lax.ppermute(
+                downs[-1], "fsdp", [(i, i - 2) for i in range(2, count - 2 * (step - 1))]
+            )
+        )
+    return [own] + [
+        jnp.where(place >= step, ups[step], downs[chips - step]) for step in range(1, chips)
+    ]
+
+
+def gather_tokens(own):
+    count = lax.axis_size("fsdp")
+    chips = count // 2
+    index = lax.axis_index("fsdp")
+    place, core = index // 2, index % 2
+    rows, width = own.shape
+    mine = line_gather(own)
+    theirs = [flip_exchange(block, "fsdp", 1) for block in mine]
+    whole = jnp.zeros((count * rows, width), own.dtype)
+    for step in range(chips):
+        chip = lax.rem(place - step + chips, chips)
+        whole = lax.dynamic_update_slice_in_dim(whole, mine[step], (2 * chip + core) * rows, 0)
+        whole = lax.dynamic_update_slice_in_dim(whole, theirs[step], (2 * chip + 1 - core) * rows, 0)
+    return whole
+
+
+def gather_over_dp(block, order):
+    other = 3 - order
+    near = flip_exchange(block, "dp", order)
+    side = flip_exchange(block, "dp", other)
+    far = flip_exchange(near, "dp", other)
+    parts = [block, None, None, None]
+    parts[order], parts[other], parts[3] = near, side, far
+    return parts
+
+
+def scatter_over_dp(parts, order):
+    other = 3 - order
+    near = flip_exchange(parts[order].astype(jnp.bfloat16), "dp", order)
+    far = flip_exchange(parts[3].astype(jnp.bfloat16), "dp", order)
+    passed = (parts[other] + far.astype(jnp.float32)).astype(jnp.bfloat16)
+    side = flip_exchange(passed, "dp", other)
+    return parts[0] + near.astype(jnp.float32) + side.astype(jnp.float32)
+
+
+def in_order(parts, axis):
+    stacked = jnp.stack(parts)
+    index = lax.axis_index(axis)
+    return jnp.stack(
+        [
+            lax.dynamic_index_in_dim(stacked, jnp.bitwise_xor(index, j), 0, keepdims=False)
+            for j in range(len(parts))
+        ]
+    )
+
+
+def split_low(value, pieces):
+    parts = []
+    for _ in range(pieces):
+        part = value.astype(jnp.bfloat16)
+        parts.append(part)
+        value = value - part.astype(jnp.float32)
+    return parts
+
+
+def all_to_all(blocks):
+    return lax.all_to_all(blocks, "fsdp", split_axis=0, concat_axis=0, tiled=True)
+
+
+def per_device_heads(
+    tokens,
+    segment_ids,
+    routes,
+    query_weight,
+    key_value_weight,
+    output_weight,
+    router_weight,
+    gain_before,
+    gain_middle,
+    inner_weight,
+    outer_weight,
+    cotangent,
+):
+    f32, low = jnp.float32, jnp.bfloat16
+    _, rows, width = tokens.shape
+    count = lax.axis_size("fsdp")
+    experts = router_weight.shape[1]
+    index, group = lax.axis_index("fsdp"), lax.axis_index("dp")
+    capacity = 3 * rows // 8
+    length = count * rows
+    shard = query_weight.shape[0]
+    share = QUERY_HEADS // KEY_VALUE_HEADS * HEAD_SIZE
+    cols = share + 2 * HEAD_SIZE
+    half = KEY_VALUE_HEADS * HEAD_SIZE
+    ff = outer_weight.shape[0]
+
+    start_low = tokens.reshape(rows, width)
+    cot_low = cotangent.reshape(rows, width)
+
+    route = routes.reshape(rows, 2)
+    route_flat = route.reshape(rows * 2)
+    picks = route_flat[:, None] == jnp.arange(experts, dtype=jnp.int32)[None, :]
+    before = jnp.dot(
+        jnp.tril(jnp.ones((rows * 2, rows * 2), low), -1),
+        picks.astype(low),
+        preferred_element_type=f32,
+    )
+    rank = jnp.sum(jnp.where(picks, before, 0.0), 1).astype(jnp.int32).reshape(rows, 2)
+    slots = jnp.arange(experts * capacity, dtype=jnp.int32)
+    slot_near = jnp.bitwise_xor(route, index) * capacity + rank
+    hit = [slot_near[:, c][None, :] == slots[:, None] for c in range(2)]
+    to_slots = (hit[0] | hit[1]).astype(low)
+    slot_named = route * capacity + rank
+    named = [slot_named[:, c][None, :] == slots[:, None] for c in range(2)]
+    other_route = jnp.sum(
+        jnp.where(named[0], route[:, 1][None, :], 0) + jnp.where(named[1], route[:, 0][None, :], 0),
+        1,
+    )
+
+    by_head = jnp.concatenate(
+        [
+            query_weight.reshape(shard, count, share),
+            key_value_weight[:, :half].reshape(shard, count, HEAD_SIZE),
+            key_value_weight[:, half:].reshape(shard, count, HEAD_SIZE),
+        ],
+        2,
+    )
+    lanes = 128 * -(-(cols + 2 + experts) // 128)
+    extras = jnp.concatenate([gain_before[:, None], gain_middle[:, None], router_weight], 1)
+    extras = jnp.broadcast_to(extras[None], (count, shard, 2 + experts))
+    head_block = jnp.concatenate([by_head.transpose(1, 0, 2), extras], 2)
+    head_block = jnp.pad(head_block, ((0, 0), (0, 0), (0, lanes - cols - 2 - experts)))
+    seg_line = jnp.broadcast_to(segment_ids.reshape(1, 1, rows), (count, 1, rows)).astype(low)
+    seg_line = jnp.pad(seg_line, ((0, 0), (0, 0), (0, lanes - rows)))
+    other_line = other_route.reshape(experts, 1, capacity).astype(low)
+    other_line = jnp.pad(other_line, ((0, 0), (0, 14), (0, lanes - capacity)))
+    arrived = all_to_all(jnp.concatenate([head_block, seg_line, other_line], 1))
+    segments = arrived[:, shard, :rows].reshape(length).astype(jnp.int32)
+    other_expert = arrived[:, shard + 1, :capacity].astype(jnp.int32)
+    other_expert = jnp.concatenate(
+        [
+            lax.dynamic_index_in_dim(other_expert, jnp.bitwise_xor(index, k), 0, keepdims=False)
+            for k in range(count)
+        ]
+    )
+    head_rows = arrived[:, :shard].reshape(count * shard, lanes)
+    head_weights = in_order(gather_over_dp(head_rows, 1), "dp").reshape(width, lanes)
+    head_weight = head_weights[:, :cols]
+    gain_first = head_weights[:, cols].astype(f32)
+    gain_second = head_weights[:, cols + 1].astype(f32)
+    router = head_weights[:, cols + 2 : cols + 2 + experts]
+
+    inner_parts = gather_over_dp(inner_weight.reshape(inner_weight.shape[0], 2 * ff), 1)
+    outer_parts = gather_over_dp(outer_weight, 2)
+    inner_all = in_order(inner_parts, "dp").reshape(width, 2 * ff)
+    outer_all = in_order(outer_parts, "dp").transpose(1, 0, 2).reshape(ff, width)
+
+    output_all = lax.all_gather(output_weight.T, ("dp", "fsdp"), axis=0, tiled=True)
+    project_all = lax.all_gather(
+        by_head.reshape(shard, count * cols), ("dp", "fsdp"), axis=0, tiled=True
+    )
+
+    tokens_all = gather_tokens(start_low)
+    normed, _, _ = normalize(tokens_all.astype(f32), gain_first)
+    normed_low = normed.astype(low)
+    projected = jnp.dot(normed_low, head_weight, preferred_element_type=f32).astype(low)
+    queries = projected[:, :share]
+    keys = projected[:, share : share + HEAD_SIZE]
+    values = projected[:, share + HEAD_SIZE :]
+    block = rows
+    firsts = segments.reshape(length // block, block)
+    starts = jnp.sum(segments[None, :] < firsts[:, :1], 1) // block
+    wholes = (jnp.sum(segments[None, :] < firsts[:, -1:], 1) + block - 1) // block
+    wholes = jnp.minimum(wholes, jnp.arange(length // block))
+    spans = jnp.stack([starts, wholes]).astype(jnp.int32)
+    seg_row, seg_col = segments.reshape(1, length), segments.reshape(length, 1)
+    mixed_head, mixed_t, totals = attend(spans, queries, keys, values, seg_row, seg_col, block)
+    mixed_low = (
+        all_to_all(mixed_head.reshape(count, rows, share)).transpose(1, 0, 2).reshape(rows, width)
+    )
+
+    start = start_low.astype(f32)
+    middle = start + lax.dot_general(
+        mixed_low, output_all, (((1,), (1,)), ((), ())), preferred_element_type=f32
+    )
+    expert_in, unit_second, factor_second = normalize(middle, gain_second)
+    expert_low = expert_in.astype(low)
+    logits = jnp.dot(expert_low, router, preferred_element_type=f32)
+    chosen = picks.reshape(rows, 2, experts)
+    gates = jax.nn.softmax(jnp.sum(jnp.where(chosen, logits[:, None, :], 0.0), -1), -1)
+
+    def by_slot(source):
+        return [
+            jnp.dot(
+                to_slots[k * capacity : (k + 1) * capacity], source, preferred_element_type=f32
+            ).astype(low)
+            for k in range(experts)
+        ]
+
+    cot_in = jnp.concatenate(swap_blocks(by_slot(cot_low), "fsdp"))
+    rows_in = jnp.concatenate(swap_blocks(by_slot(expert_low), "fsdp"))
+    slot_logits = jnp.dot(rows_in, router, preferred_element_type=f32)
+    own_hot = jnp.arange(experts) == index
+    other_hot = other_expert[:, None] == jnp.arange(experts)[None, :]
+    own_logit = jnp.sum(jnp.where(own_hot[None, :], slot_logits, 0.0), 1)
+    other_logit = jnp.sum(jnp.where(other_hot, slot_logits, 0.0), 1)
+    slot_gates = jax.nn.softmax(jnp.stack([own_logit, other_logit], 1), -1)
+    cot_rows = cot_in.astype(f32)
+    grad_in = (slot_gates[:, :1] * cot_rows).astype(low)
+    hidden, grad_pre, grad_rows = expert_back(inner_all, outer_all, rows_in, grad_in)
+    part = jnp.dot(hidden, outer_all, preferred_element_type=f32).astype(low)
+    grad_gate = jnp.sum(cot_rows * part.astype(f32), 1)
+    slope = slot_gates[:, 0] * slot_gates[:, 1] * grad_gate
+    sides = own_hot[None, :].astype(f32) - other_hot.astype(f32)
+    logit_grads = jnp.concatenate(split_low(slope[:, None] * sides, 2), 1)
+    grad_rows = grad_rows.astype(f32) + jnp.dot(
+        logit_grads, jnp.concatenate([router, router], 1).T, preferred_element_type=f32
+    )
+    grad_rows = grad_rows.astype(low)
+    router_parts = lax.dot_general(
+        rows_in, logit_grads, (((0,), (0,)), ((), ())), preferred_element_type=f32
+    )
+    router_part = router_parts[:, :experts] + router_parts[:, experts:]
+
+    def cut(value, k, size):
+        at = jnp.bitwise_xor(group, k) * size
+        return lax.dynamic_slice_in_dim(value, at, size, 1)
+
+    def pieces(value, blocks):
+        return [value[k * capacity : (k + 1) * capacity] for k in range(blocks)]
+
+    grad_home = jnp.concatenate(swap_blocks(pieces(grad_rows, experts), "fsdp"))
+    part_home = jnp.concatenate(swap_blocks(pieces(part, experts), "fsdp"))
+    size = inner_weight.shape[0]
+    inner_terms = [
+        lax.dot_general(
+            cut(rows_in, k, size), grad_pre, (((0,), (0,)), ((), ())), preferred_element_type=f32
+        )
+        for k in range(4)
+    ]
+    outer_terms = [
+        lax.dot_general(
+            hidden, cut(grad_in, k, size), (((0,), (0,)), ((), ())), preferred_element_type=f32
+        )
+        for k in range(4)
+    ]
+    inner_grad = scatter_over_dp(inner_terms, 1).reshape(size, 2, ff)
+    outer_grad = scatter_over_dp(outer_terms, 2)
+
+    grad_out = cot_low.astype(f32)
+    grad_expert_in = lax.dot_general(
+        to_slots, grad_home, (((0,), (0,)), ((), ())), preferred_element_type=f32
+    )
+    inner_back, middle_part = normalize_back(
+        grad_expert_in, unit_second, factor_second, gain_second
+    )
+    grad_middle = grad_out + inner_back
+    grad_branch = grad_middle.astype(low)
+    mixed_grad = jnp.dot(grad_branch, output_all, preferred_element_type=f32).astype(low)
+    mixed_grad = all_to_all(mixed_grad.reshape(rows, count, share).transpose(1, 0, 2)).reshape(
+        length, share
+    )
+    output_part = lax.dot_general(
+        grad_branch, mixed_low, (((0,), (0,)), ((), ())), preferred_element_type=f32
+    )
+    output_grad = lax.psum_scatter(
+        output_part, ("dp", "fsdp"), scatter_dimension=0, tiled=True
+    ).T
+    gate_terms = split_low(gates, 3)
+    combine = [
+        jnp.where(hit[0], gate[:, 0][None, :], 0) + jnp.where(hit[1], gate[:, 1][None, :], 0)
+        for gate in gate_terms
+    ]
+    mixture = sum(
+        lax.dot_general(term, part_home, (((0,), (0,)), ((), ())), preferred_element_type=f32)
+        for term in combine
+    )
+    block_out = (middle + mixture).astype(low)
+
+    grad_queries, grad_keyvals = attend_backward(
+        spans, queries, mixed_grad, keys, values, seg_row, seg_col, mixed_t, totals, block
+    )
+    grad_heads = jnp.concatenate([grad_queries, grad_keyvals], 1)
+    weight_part = lax.dot_general(
+        normed_low, grad_heads, (((0,), (0,)), ((), ())), preferred_element_type=f32
+    )
+    weight_part = jnp.concatenate([weight_part, middle_part[:, None], router_part], 1)
+    weight_part = jnp.pad(weight_part, ((0, 0), (0, lanes - cols - 1 - experts)))
+    span = count * shard
+    terms = [
+        lax.dynamic_slice_in_dim(weight_part, jnp.bitwise_xor(group, k) * span, span, 0)
+        for k in range(4)
+    ]
+    weight_sum = scatter_over_dp(terms, 1).astype(low)
+    weight_home = all_to_all(weight_sum.reshape(count, shard, lanes)).astype(f32)
+    query_grad = weight_home[:, :, :share].transpose(1, 0, 2).reshape(shard, count * share)
+    key_grad = weight_home[:, :, share : share + HEAD_SIZE].transpose(1, 0, 2)
+    value_grad = weight_home[:, :, share + HEAD_SIZE : cols].transpose(1, 0, 2)
+    keyval_grad = jnp.concatenate(
+        [key_grad.reshape(shard, half), value_grad.reshape(shard, half)], 1
+    )
+    small = jnp.sum(weight_home[:, :, cols : cols + 1 + experts], 0)
+    middle_grad, router_grad = small[:, 0], small[:, 1:]
+    before_grad = (
+        jnp.sum(query_grad * query_weight.astype(f32), 1)
+        + jnp.sum(keyval_grad * key_value_weight.astype(f32), 1)
+    ) / gain_before.astype(f32)
+
+    grad_mine = all_to_all(grad_heads.reshape(count, rows, cols))
+    grad_mine = grad_mine.transpose(1, 0, 2).reshape(rows, count * cols)
+    grad_normed = lax.dot_general(
+        grad_mine, project_all, (((1,), (1,)), ((), ())), preferred_element_type=f32
+    )
+    _, unit_first, factor_first = normalize(start, gain_first)
+    outer_back, _ = normalize_back(grad_normed, unit_first, factor_first, gain_first)
+    tokens_grad = grad_middle + outer_back
+    return (
+        block_out[None],
+        tokens_grad[None],
+        query_grad,
+        keyval_grad,
+        output_grad,
+        router_grad,
+        before_grad,
+        middle_grad,
+        inner_grad,
+        outer_grad,
+    )
+
+
 def solution(mesh):
+    by_heads = (mesh.shape["dp"], mesh.shape["fsdp"]) == (4, KEY_VALUE_HEADS)
     in_specs = (
         P("dp", "fsdp", None),
         P("dp", "fsdp"),
@@ -467,5 +1011,5 @@
         P("fsdp", "dp"),
     )
     return jax.shard_map(
-        per_device, mesh=mesh, in_specs=in_specs, out_specs=out_specs, check_vma=False
-    )
+        per_device_heads if by_heads else per_device, mesh=mesh, in_specs=in_specs, out_specs=out_specs, check_vma=False
+    )

time: 1480 us -> 788 us (0.53)
  blocking collectives: 326 us -> 0 us
  waiting for transfers between devices: 652 us -> 344 us
  local copies, waits for them, and re-layouts: 143 us -> 71.6 us
  starting transfers between devices: 80.6 us -> 150 us
  Pallas kernels: 0 us -> 50.6 us
  matrix products: 154 us -> 108 us
  loops' own time: 29.2 us -> 0 us
  other arithmetic: 60.7 us -> 38.5 us
    reduce_scatter x5 -> x1, waiting for transfers between devices: 396 us -> 0.01 us  [per_device_heads(): lax.psum_scatter(output_part, ('dp', 'fsdp'), scatter_dimension=0, tiled=...]
    ppermute x0 -> x56, waiting for transfers between devices: none -> 330 us  [the longest x50 263 us: flip_exchange(): return lax.ppermute(block, axis, [(i, i ^ flip) for i in range(count)])]
    all_to_all x2 -> x0, blocking collectives: 153 us -> none  [the longest x1 95.8 us: per_device(): lax.all_to_all(sent, 'fsdp', split_axis=0, concat_axis=0, tiled=True)]
    all_to_all x4 -> x5, waiting for transfers between devices: 149 us -> 12.9 us  [all_to_all(): lax.all_to_all(blocks, 'fsdp', split_axis=0, concat_axis=0, tiled=True)]
    ppermute x0 -> x56, starting transfers between devices: none -> 114 us  [the longest x50 101 us: flip_exchange(): return lax.ppermute(block, axis, [(i, i ^ flip) for i in range(count)])]
    all_gather x6 -> x2, waiting for transfers between devices: 104 us -> 0.01 us  [the longest x1 0.01 us: per_device_heads(): lax.all_gather(output_weight.T, ('dp', 'fsdp'), axis=0, tiled=True)]
    all_gather x2 -> x0, blocking collectives: 94.5 us -> none  [the longest x1 83.9 us: layer_weights(): lax.all_gather(router_weight, ('dp', 'fsdp'), axis=0, tiled=True)]
    unnamed x2 -> x0, blocking collectives: 79.2 us -> none
  transfers between devices with their start and end apart: 17 -> 64, of which waited for: 9 -> 25; matrix products, arithmetic and copies ran while one was open for 16% -> 27% of each run, Pallas kernels for 0% -> 7%
where the time goes in v1:
time: 788 us; the launch traced here: 778 us
  waiting for transfers between devices  344 us (44%)
  starting transfers between devices  150 us (19%)
  matrix products  108 us (14%)
  local copies, waits for them, and re-layouts  71.6 us (9%)
  Pallas kernels  50.6 us (6%)
  other arithmetic  38.5 us (5%)
  between operations  15.9 us (2%)
    ppermute x50, waiting for transfers between devices, flip_exchange(): return lax.ppermute(block, axis, [(i, i ^ flip) for i in range(count)])  263 us
    ppermute x50, starting transfers between devices, flip_exchange(): return lax.ppermute(block, axis, [(i, i ^ flip) for i in range(count)])  101 us
    ppermute x3, waiting for transfers between devices, line_gather(): lax.ppermute(downs[-1], 'fsdp', [(i, i - 2) for i in range(2, count - 2 *...  67.5 us
    all_to_all x5, starting transfers between devices, all_to_all(): lax.all_to_all(blocks, 'fsdp', split_axis=0, concat_axis=0, tiled=True)  35.1 us
    unnamed x190, local copies, waits for them, and re-layouts  30.8 us
    pallas_call x1, Pallas kernels, attend_backward(): pl.pallas_call(attend_back_kernel, grid_spec=pltpu.PrefetchScalarGridSpec...  28 us
    pallas_call x1, Pallas kernels, attend(): pl.pallas_call(attend_kernel, grid_spec=pltpu.PrefetchScalarGridSpec(num_...  22.6 us
    dot_general x16, matrix products, by_slot(): jnp.dot(to_slots[k * capacity:(k + 1) * capacity], source, preferred_elem...  18.2 us
  transfers between devices with their start and end apart: 64, of which 25 were waited for; matrix products, arithmetic and copies ran while one was open for 27% of the time, Pallas kernels for 7%

profile of v1, /device:TPU:1, one launch (start us, length us, event | category | flops | bytes accessed | tf_op | source)
XLA Modules:
  0.0 778.1 jit_solution(13041475765832430552)
XLA Ops:
  9.4 6.2 collective-permute-start.1
  19.5 4.6 all-to-all-start
  49.1 4.8 collective-permute-done.34
  58.8 4.2 collective-permute-done.35
  62.9 8.2 %collective-permute-start.37 = (bf16[96,1536]{1,0:T(8,128)(2,1)S(1)}, bf16[96,1536]{1,0:T(8,128)(2,1)S(1)}, u32[]{:S(2)}, u32[]{:S(2)}) collective-permute-start(bf16[96,1536]{1,0:T(8,128)(2,1)S(1)} %copy-done.49), channel_id=1, source_target_pairs={{0,5},{1,4},{2,7},{3,6},{4,1},{5,0},{6,3},{7,2},{8,13},{9,12},{10,... | collective-permute-start | bytes 884744 | tf_op jit(solution)/shard_map/ppermute | solution.py:639
  71.9 13.6 %collective-permute-start.38 = (bf16[96,1536]{1,0:T(8,128)(2,1)S(1)}, bf16[96,1536]{1,0:T(8,128)(2,1)S(1)}, u32[]{:S(2)}, u32[]{:S(2)}) collective-permute-start(bf16[96,1536]{1,0:T(8,128)(2,1)S(1)} %copy-done.48), channel_id=1, source_target_pairs={{0,6},{1,7},{2,4},{3,5},{4,2},{5,3},{6,0},{7,1},{8,14},{9,15},{10,... | collective-permute-start | bytes 884744 | tf_op jit(solution)/shard_map/ppermute | solution.py:639
  87.5 16.9 %collective-permute-done.37 = bf16[96,1536]{1,0:T(8,128)(2,1)S(1)} collective-permute-done((bf16[96,1536]{1,0:T(8,128)(2,1)S(1)}, bf16[96,1536]{1,0:T(8,128)(2,1)S(1)}, u32[]{:S(2)}, u32[]{:S(2)}) %collective-permute-start.37) | collective-permute-done | bytes 294944 | tf_op jit(solution)/shard_map/ppermute | solution.py:639
  107.1 8.5 %collective-permute-done.39 = bf16[96,1536]{1,0:T(8,128)(2,1)S(1)} collective-permute-done((bf16[96,1536]{1,0:T(8,128)(2,1)S(1)}, bf16[96,1536]{1,0:T(8,128)(2,1)S(1)}, u32[]{:S(2)}, u32[]{:S(2)}) %collective-permute-start.39) | collective-permute-done | bytes 294944 | tf_op jit(solution)/shard_map/ppermute | solution.py:639
  118.5 7.9 %collective-permute-done.3 = bf16[256,1536]{1,0:T(8,128)(2,1)S(1)} collective-permute-done((bf16[256,1536]{1,0:T(8,128)(2,1)}, bf16[256,1536]{1,0:T(8,128)(2,1)S(1)}, u32[]{:S(2)}, u32[]{:S(2)}) %collective-permute-start.3) | collective-permute-done | bytes 786464 | tf_op jit(solution)/shard_map/ppermute | solution.py:656
  133.4 59.6 %collective-permute-done.4 = bf16[256,1536]{1,0:T(8,128)(2,1)} collective-permute-done((bf16[256,1536]{1,0:T(8,128)(2,1)S(1)}, bf16[256,1536]{1,0:T(8,128)(2,1)}, u32[]{:S(2)}, u32[]{:S(2)}) %collective-permute-start.4) | collective-permute-done | bytes 786464 | tf_op jit(solution)/shard_map/ppermute | solution.py:656
  198.8 6.5 collective-permute-done.12
  217.2 38.8 %collective-permute-done.24 = bf16[1024,384]{0,1:T(8,128)(2,1)} collective-permute-done((bf16[1024,384]{0,1:T(8,128)(2,1)S(1)}, bf16[1024,384]{0,1:T(8,128)(2,1)}, u32[]{:S(2)}, u32[]{:S(2)}) %collective-permute-start.24) | collective-permute-done | bytes 786464 | tf_op jit(solution)/shard_map/ppermute | solution.py:639
  265.6 8.2 %collective-permute-done.23 = bf16[1024,384]{0,1:T(8,128)(2,1)} collective-permute-done((bf16[1024,384]{0,1:T(8,128)(2,1)S(1)}, bf16[1024,384]{0,1:T(8,128)(2,1)}, u32[]{:S(2)}, u32[]{:S(2)}) %collective-permute-start.23) | collective-permute-done | bytes 786464 | tf_op jit(solution)/shard_map/ppermute | solution.py:639
  273.8 16.9 %collective-permute-done.25 = bf16[1024,384]{0,1:T(8,128)(2,1)} collective-permute-done((bf16[1024,384]{0,1:T(8,128)(2,1)}, bf16[1024,384]{0,1:T(8,128)(2,1)}, u32[]{:S(2)}, u32[]{:S(2)}) %collective-permute-start.25) | collective-permute-done | bytes 786464 | tf_op jit(solution)/shard_map/ppermute | solution.py:639
  296.8 4.1 fusion
  300.9 6.3 convolution_convert_fusion.4
  307.5 22.6 %attend.1 = (bf16[2048,192]{1,0:T(8,128)(2,1)S(1)}, f32[192,2048]{1,0:T(8,128)S(1)}, f32[8,2048]{1,0:T(8,128)S(1)}) custom-call(s32[2,8]{1,0:T(2,128)S(1)} %pad_add_fusion.spans, bf16[2048,192]{1,0:T(8,128)(2,1)S(1)} %slice.267.q_ref, bf16[2048,64]{1,0:T(8,128)(2,1)S(1)} %get-tuple-element.109.k_ref, bf16[2048,64]{1,0:T(8,128)(2,1)S(1)} %get-tuple-element.108.v_ref, ...), custom_call_target="tpu_custom_call" | custom-call | tf_op jit(solution)/shard_map/attend/pallas_call | solution.py:590
  334.5 6.4 all-to-all-start.1
  341.3 3.7 pad_maximum_fusion
  349.4 11.7 %all-to-all-done.1 = bf16[8,256,192]{1,2,0:T(8,128)(2,1)} async-done(((bf16[8,256,192]{1,2,0:T(8,128)(2,1)}), bf16[8,256,192]{1,2,0:T(8,128)(2,1)}, u32[]{:S(2)}, u32[]{:S(2)}) %all-to-all-start.1) | async-done | bytes 786464 | tf_op jit(solution)/shard_map/all_to_all | solution.py:721
  361.1 4.3 multiply_reduce_fusion.2
  394.7 20.5 %collective-permute-done.17 = bf16[96,1536]{1,0:T(8,128)(2,1)} collective-permute-done((bf16[96,1536]{1,0:T(8,128)(2,1)}, bf16[96,1536]{1,0:T(8,128)(2,1)}, u32[]{:S(2)}, u32[]{:S(2)}) %collective-permute-start.17) | collective-permute-done | bytes 294944 | tf_op jit(solution)/shard_map/ppermute | solution.py:639
  418.5 7.1 fusion.158
  428.8 4.0 fusion.4
  433.4 3.6 multiply_convert_fusion.1
  437.1 5.5 convolution_convert_fusion.1
  444.8 11.2 %collective-permute-start.41 = (bf16[96,1536]{1,0:T(8,128)(2,1)S(1)}, bf16[96,1536]{1,0:T(8,128)(2,1)S(1)}, u32[]{:S(2)}, u32[]{:S(2)}) collective-permute-start(bf16[96,1536]{1,0:T(8,128)(2,1)S(1)} %get-tuple-element.97), channel_id=1, source_target_pairs={{0,2},{1,3},{2,0},{3,1},{4,6},{5,7},{6,4},{7,5},{8,10},{9,11},{10,... | collective-permute-start | bytes 884744 | tf_op jit(solution)/shard_map/ppermute | solution.py:639
  460.9 12.6 %collective-permute-done.41 = bf16[96,1536]{1,0:T(8,128)(2,1)S(1)} collective-permute-done((bf16[96,1536]{1,0:T(8,128)(2,1)S(1)}, bf16[96,1536]{1,0:T(8,128)(2,1)S(1)}, u32[]{:S(2)}, u32[]{:S(2)}) %collective-permute-start.41) | collective-permute-done | bytes 294944 | tf_op jit(solution)/shard_map/ppermute | solution.py:639
  476.7 3.7 collective-permute-done.42
  480.5 18.6 %collective-permute-done.44 = bf16[96,1536]{1,0:T(8,128)(2,1)S(1)} collective-permute-done((bf16[96,1536]{1,0:T(8,128)(2,1)S(1)}, bf16[96,1536]{1,0:T(8,128)(2,1)S(1)}, u32[]{:S(2)}, u32[]{:S(2)}) %collective-permute-start.44) | collective-permute-done | bytes 294944 | tf_op jit(solution)/shard_map/ppermute | solution.py:639
  502.4 6.2 fusion.71
  508.6 3.6 convolution_convert_fusion.23
  519.7 12.7 %collective-permute-start.27 = (bf16[96,1536]{1,0:T(8,128)(2,1)}, bf16[96,1536]{1,0:T(8,128)(2,1)}, u32[]{:S(2)}, u32[]{:S(2)}) collective-permute-start(bf16[96,1536]{1,0:T(8,128)(2,1)} %get-tuple-element.105), channel_id=1, source_target_pairs={{0,2},{1,3},{2,0},{3,1},{4,6},{5,7},{6,4},{7,5},{8,10},{9,11},{10,... | collective-permute-start | bytes 884744 | tf_op jit(solution)/shard_map/ppermute | solution.py:639
  546.2 4.5 all-to-all-start.2
  557.9 20.0 %collective-permute-done.28 = bf16[96,1536]{1,0:T(8,128)(2,1)S(1)} collective-permute-done((bf16[96,1536]{1,0:T(8,128)(2,1)}, bf16[96,1536]{1,0:T(8,128)(2,1)S(1)}, u32[]{:S(2)}, u32[]{:S(2)}) %collective-permute-start.28) | collective-permute-done | bytes 294944 | tf_op jit(solution)/shard_map/ppermute | solution.py:639
  579.4 21.0 %collective-permute-done.29 = bf16[96,1536]{1,0:T(8,128)(2,1)S(1)} collective-permute-done((bf16[96,1536]{1,0:T(8,128)(2,1)}, bf16[96,1536]{1,0:T(8,128)(2,1)S(1)}, u32[]{:S(2)}, u32[]{:S(2)}) %collective-permute-start.29) | collective-permute-done | bytes 294944 | tf_op jit(solution)/shard_map/ppermute | solution.py:639
  603.8 23.7 %collective-permute-done.30 = bf16[96,1536]{1,0:T(8,128)(2,1)S(1)} collective-permute-done((bf16[96,1536]{1,0:T(8,128)(2,1)}, bf16[96,1536]{1,0:T(8,128)(2,1)S(1)}, u32[]{:S(2)}, u32[]{:S(2)}) %collective-permute-start.30) | collective-permute-done | bytes 294944 | tf_op jit(solution)/shard_map/ppermute | solution.py:639
  631.0 5.5 collective-permute-done.32
  637.2 3.8 fusion.63
  646.4 28.0 %attend_backward.1 = (bf16[2048,192]{1,0:T(8,128)(2,1)S(1)}, bf16[2048,128]{1,0:T(8,128)(2,1)S(1)}) custom-call(s32[2,8]{1,0:T(2,128)S(1)} %pad_add_fusion.spans, bf16[2048,192]{1,0:T(8,128)(2,1)S(1)} %slice.267.q_ref, bf16[2048,192]{1,0:T(8,128)(2,1)S(1)} %bitcast.147, bf16[2048,64]{1,0:T(8,128)(2,1)S(1)} %get-tuple-element.109.k_ref, ...), custom_call_target="tpu_custom_call" | custom-call | tf_op jit(solution)/shard_map/attend_backward/pallas_call | solution.py:613
  674.5 5.9 fusion.14
  684.9 3.9 collective-permute-done.48
  700.5 14.4 %all-to-all-start.4 = ((bf16[8,48,384]{2,1,0:T(8,128)(2,1)}), bf16[8,48,384]{2,1,0:T(8,128)(2,1)S(1)}, u32[]{:S(2)}, u32[]{:S(2)}) async-start(bf16[8,48,384]{2,1,0:T(8,128)(2,1)} %bitcast.48), calls=%async_computation.4 | async-start | bytes 589824 | tf_op jit(solution)/shard_map/all_to_all | solution.py:721
  714.9 4.8 add_convert_fusion.1
  724.2 5.2 all-to-all-start.3
  735.5 20.5 %collective-permute-done.52 = bf16[384,2048]{1,0:T(8,128)(2,1)} collective-permute-done((bf16[384,2048]{1,0:T(8,128)(2,1)}, bf16[384,2048]{1,0:T(8,128)(2,1)}, u32[]{:S(2)}, u32[]{:S(2)}) %collective-permute-start.52) | collective-permute-done | bytes 1572896 | tf_op jit(solution)/shard_map/ppermute | solution.py:639
  759.5 3.7 reshape.386
  763.3 6.3 fusion.17
  (449 shorter events, 217.8 us)
Async XLA Ops:
  7.2 353.8 %all-gather.3.cloned.1.call-start = ((), (), s32[]{:S(2)}) async-start(), calls=%async_computation.6 | async-start | bytes 4866048 | tf_op jit(solution)/shard_map/all_gather | solution.py:812
  8.0 122.1 %collective-permute-start = (bf16[256,1536]{1,0:T(8,128)(2,1)}, bf16[256,1536]{1,0:T(8,128)(2,1)}, u32[]{:S(2)}, u32[]{:S(2)}) collective-permute-start(bf16[256,1536]{1,0:T(8,128)(2,1)} %bitcast.158), channel_id=1, source_target_pairs={{0,1},{1,0},{2,3},{3,2},{4,5},{5,4},{6,7},{7,6},{8,9},{9,8},{10,11... | collective-permute-start | bytes 2359304 | tf_op jit(solution)/shard_map/ppermute | solution.py:639
  8.1 77.4 %collective-permute-start.2 = (bf16[256,1536]{1,0:T(8,128)(2,1)}, bf16[256,1536]{1,0:T(8,128)(2,1)}, u32[]{:S(2)}, u32[]{:S(2)}) collective-permute-start(bf16[256,1536]{1,0:T(8,128)(2,1)} %bitcast.159), channel_id=1, source_target_pairs={{2,0},{3,1},{4,2},{5,3},{6,4},{7,5},{10,8},{11,9},{12,10},{13,11},... | collective-permute-start | bytes 2359304 | tf_op jit(solution)/shard_map/ppermute | solution.py:656
  9.4 124.0 %collective-permute-start.1 = (bf16[256,1536]{1,0:T(8,128)(2,1)}, bf16[256,1536]{1,0:T(8,128)(2,1)}, u32[]{:S(2)}, u32[]{:S(2)}) collective-permute-start(bf16[256,1536]{1,0:T(8,128)(2,1)} %bitcast.160), channel_id=1, source_target_pairs={{0,2},{1,3},{2,4},{3,5},{4,6},{5,7},{8,10},{9,11},{10,12},{11,13},... | collective-permute-start | bytes 2359304 | tf_op jit(solution)/shard_map/ppermute | solution.py:653
  19.5 96.8 %all-to-all-start = ((bf16[8,64,384]{2,1,0:T(8,128)(2,1)}), bf16[8,64,384]{2,1,0:T(8,128)(2,1)}, u32[]{:S(2)}, u32[]{:S(2)}) async-start(bf16[8,64,384]{2,1,0:T(8,128)(2,1)} %copy.143), calls=%async_computation | async-start | bytes 786432 | tf_op jit(solution)/shard_map/all_to_all | solution.py:721
  24.1 739.1 %all-gather.5.cloned.1.call-start = ((), (), s32[]{:S(2)}) async-start(), calls=%async_computation.7 | async-start | bytes 8110080 | tf_op jit(solution)/shard_map/all_gather | solution.py:813
  26.5 27.3 %collective-permute-start.34 = (bf16[96,1536]{1,0:T(8,128)(2,1)}, bf16[96,1536]{1,0:T(8,128)(2,1)}, u32[]{:S(2)}, u32[]{:S(2)}) collective-permute-start(bf16[96,1536]{1,0:T(8,128)(2,1)} %convolution_convert_fusion.11), channel_id=1, source_target_pairs={{0,2},{1,3},{2,0},{3,1},{4,6},{5,7},{6,4},{7,5},{8,10},{9,11},{10,... | collective-permute-start | bytes 884744 | tf_op jit(solution)/shard_map/ppermute | solution.py:639
  62.9 41.5 %collective-permute-start.37 = (bf16[96,1536]{1,0:T(8,128)(2,1)S(1)}, bf16[96,1536]{1,0:T(8,128)(2,1)S(1)}, u32[]{:S(2)}, u32[]{:S(2)}) collective-permute-start(bf16[96,1536]{1,0:T(8,128)(2,1)S(1)} %copy-done.49), channel_id=1, source_target_pairs={{0,5},{1,4},{2,7},{3,6},{4,1},{5,0},{6,3},{7,2},{8,13},{9,12},{10,... | collective-permute-start | bytes 884744 | tf_op jit(solution)/shard_map/ppermute | solution.py:639
  71.9 33.3 %collective-permute-start.38 = (bf16[96,1536]{1,0:T(8,128)(2,1)S(1)}, bf16[96,1536]{1,0:T(8,128)(2,1)S(1)}, u32[]{:S(2)}, u32[]{:S(2)}) collective-permute-start(bf16[96,1536]{1,0:T(8,128)(2,1)S(1)} %copy-done.48), channel_id=1, source_target_pairs={{0,6},{1,7},{2,4},{3,5},{4,2},{5,3},{6,0},{7,1},{8,14},{9,15},{10,... | collective-permute-start | bytes 884744 | tf_op jit(solution)/shard_map/ppermute | solution.py:639
  85.5 41.0 %collective-permute-start.3 = (bf16[256,1536]{1,0:T(8,128)(2,1)}, bf16[256,1536]{1,0:T(8,128)(2,1)S(1)}, u32[]{:S(2)}, u32[]{:S(2)}) collective-permute-start(bf16[256,1536]{1,0:T(8,128)(2,1)} %collective-permute-done.2), channel_id=1, source_target_pairs={{2,0},{3,1},{4,2},{5,3},{10,8},{11,9},{12,10},{13,11},{18,16},{19,... | collective-permute-start | bytes 2359304 | tf_op jit(solution)/shard_map/ppermute | solution.py:656
  105.2 159.2 %collective-permute-start.20 = (bf16[384,2048]{1,0:T(8,128)(2,1)}, bf16[384,2048]{1,0:T(8,128)(2,1)}, u32[]{:S(2)}, u32[]{:S(2)}) collective-permute-start(bf16[384,2048]{1,0:T(8,128)(2,1)} %bitcast.58), channel_id=1, source_target_pairs={{0,8},{8,0},{16,24},{24,16},{1,9},{9,1},{17,25},{25,17},{2,10},{10... | collective-permute-start | bytes 4718600 | tf_op jit(solution)/shard_map/ppermute | solution.py:639
  117.3 79.9 %collective-permute-start.10 = (bf16[384,384]{1,0:T(8,128)(2,1)S(1)}, bf16[384,384]{1,0:T(8,128)(2,1)S(1)}, u32[]{:S(2)}, u32[]{:S(2)}) collective-permute-start(bf16[384,384]{1,0:T(8,128)(2,1)S(1)} %bitcast.173), channel_id=1, source_target_pairs={{0,8},{8,0},{16,24},{24,16},{1,9},{9,1},{17,25},{25,17},{2,10},{10... | collective-permute-start | bytes 884744 | tf_op jit(solution)/shard_map/ppermute | solution.py:639
  126.5 66.6 %collective-permute-start.4 = (bf16[256,1536]{1,0:T(8,128)(2,1)S(1)}, bf16[256,1536]{1,0:T(8,128)(2,1)}, u32[]{:S(2)}, u32[]{:S(2)}) collective-permute-start(bf16[256,1536]{1,0:T(8,128)(2,1)S(1)} %collective-permute-done.3), channel_id=1, source_target_pairs={{2,0},{3,1},{10,8},{11,9},{18,16},{19,17},{26,24},{27,25}} | collective-permute-start | bytes 2359304 | tf_op jit(solution)/shard_map/ppermute | solution.py:656
  130.1 68.5 %collective-permute-start.11 = (bf16[384,384]{1,0:T(8,128)(2,1)S(1)}, bf16[384,384]{1,0:T(8,128)(2,1)}, u32[]{:S(2)}, u32[]{:S(2)}) collective-permute-start(bf16[384,384]{1,0:T(8,128)(2,1)S(1)} %bitcast.174), channel_id=1, source_target_pairs={{0,16},{8,24},{16,0},{24,8},{1,17},{9,25},{17,1},{25,9},{2,18},{10... | collective-permute-start | bytes 884744 | tf_op jit(solution)/shard_map/ppermute | solution.py:639
  198.6 142.7 %collective-permute-start.21 = (bf16[384,2048]{1,0:T(8,128)(2,1)}, bf16[384,2048]{1,0:T(8,128)(2,1)}, u32[]{:S(2)}, u32[]{:S(2)}) collective-permute-start(bf16[384,2048]{1,0:T(8,128)(2,1)} %bitcast.58), channel_id=1, source_target_pairs={{0,16},{8,24},{16,0},{24,8},{1,17},{9,25},{17,1},{25,9},{2,18},{10... | collective-permute-start | bytes 4718600 | tf_op jit(solution)/shard_map/ppermute | solution.py:639
  205.4 50.7 %collective-permute-start.24 = (bf16[1024,384]{0,1:T(8,128)(2,1)S(1)}, bf16[1024,384]{0,1:T(8,128)(2,1)}, u32[]{:S(2)}, u32[]{:S(2)}) collective-permute-start(bf16[1024,384]{0,1:T(8,128)(2,1)S(1)} %copy.151), channel_id=1, source_target_pairs={{0,16},{8,24},{16,0},{24,8},{1,17},{9,25},{17,1},{25,9},{2,18},{10... | collective-permute-start | bytes 2359304 | tf_op jit(solution)/shard_map/ppermute | solution.py:639
  210.1 46.0 %collective-permute-start.7 = (bf16[256,1536]{1,0:T(8,128)(2,1)}, bf16[256,1536]{1,0:T(8,128)(2,1)}, u32[]{:S(2)}, u32[]{:S(2)}) collective-permute-start(bf16[256,1536]{1,0:T(8,128)(2,1)} %get-tuple-element.77), channel_id=1, source_target_pairs={{0,1},{1,0},{2,3},{3,2},{4,5},{5,4},{6,7},{7,6},{8,9},{9,8},{10,11... | collective-permute-start | bytes 2359304 | tf_op jit(solution)/shard_map/ppermute | solution.py:639
  213.0 46.6 %collective-permute-start.8 = (bf16[256,1536]{1,0:T(8,128)(2,1)}, bf16[256,1536]{1,0:T(8,128)(2,1)}, u32[]{:S(2)}, u32[]{:S(2)}) collective-permute-start(bf16[256,1536]{1,0:T(8,128)(2,1)} %collective-permute-done.6), channel_id=1, source_target_pairs={{4,6},{5,7},{12,14},{13,15},{20,22},{21,23},{28,30},{29,31}} | collective-permute-start | bytes 2359304 | tf_op jit(solution)/shard_map/ppermute | solution.py:653
  256.0 34.6 %collective-permute-start.25 = (bf16[1024,384]{0,1:T(8,128)(2,1)}, bf16[1024,384]{0,1:T(8,128)(2,1)}, u32[]{:S(2)}, u32[]{:S(2)}) collective-permute-start(bf16[1024,384]{0,1:T(8,128)(2,1)} %collective-permute-done.24), channel_id=1, source_target_pairs={{0,8},{8,0},{16,24},{24,16},{1,9},{9,1},{17,25},{25,17},{2,10},{10... | collective-permute-start | bytes 2359304 | tf_op jit(solution)/shard_map/ppermute | solution.py:639
  262.0 32.6 %collective-permute-start.9 = (bf16[256,1536]{1,0:T(8,128)(2,1)}, bf16[256,1536]{1,0:T(8,128)(2,1)}, u32[]{:S(2)}, u32[]{:S(2)}) collective-permute-start(bf16[256,1536]{1,0:T(8,128)(2,1)} %get-tuple-element.75), channel_id=1, source_target_pairs={{0,1},{1,0},{2,3},{3,2},{4,5},{5,4},{6,7},{7,6},{8,9},{9,8},{10,11... | collective-permute-start | bytes 2359304 | tf_op jit(solution)/shard_map/ppermute | solution.py:639
  264.3 77.0 %collective-permute-start.22 = (bf16[384,2048]{1,0:T(8,128)(2,1)}, bf16[384,2048]{1,0:T(8,128)(2,1)}, u32[]{:S(2)}, u32[]{:S(2)}) collective-permute-start(bf16[384,2048]{1,0:T(8,128)(2,1)} %collective-permute-done.20), channel_id=1, source_target_pairs={{0,16},{8,24},{16,0},{24,8},{1,17},{9,25},{17,1},{25,9},{2,18},{10... | collective-permute-start | bytes 4718600 | tf_op jit(solution)/shard_map/ppermute | solution.py:639
  334.5 26.6 %all-to-all-start.1 = ((bf16[8,256,192]{1,2,0:T(8,128)(2,1)}), bf16[8,256,192]{1,2,0:T(8,128)(2,1)}, u32[]{:S(2)}, u32[]{:S(2)}) async-start(bf16[8,256,192]{1,2,0:T(8,128)(2,1)} %copy.147), calls=%async_computation.1 | async-start | bytes 1572864 | tf_op jit(solution)/shard_map/all_to_all | solution.py:721
  340.8 430.3 %reduce-scatter.2.cloned.1.call-start = ((), (), s32[]{:S(2)}) async-start(), calls=%async_computation.8 | async-start | bytes 9732096 | tf_op jit(solution)/shard_map/reduce_scatter | solution.py:920
  370.4 22.4 %collective-permute-start.15 = (bf16[96,1536]{1,0:T(8,128)(2,1)}, bf16[96,1536]{1,0:T(8,128)(2,1)}, u32[]{:S(2)}, u32[]{:S(2)}) collective-permute-start(bf16[96,1536]{1,0:T(8,128)(2,1)} %convolution_convert_fusion.18), channel_id=1, source_target_pairs={{0,3},{1,2},{2,1},{3,0},{4,7},{5,6},{6,5},{7,4},{8,11},{9,10},{10,... | collective-permute-start | bytes 884744 | tf_op jit(solution)/shard_map/ppermute | solution.py:639
  373.9 41.3 %collective-permute-start.17 = (bf16[96,1536]{1,0:T(8,128)(2,1)}, bf16[96,1536]{1,0:T(8,128)(2,1)}, u32[]{:S(2)}, u32[]{:S(2)}) collective-permute-start(bf16[96,1536]{1,0:T(8,128)(2,1)} %convolution_convert_fusion.16), channel_id=1, source_target_pairs={{0,5},{1,4},{2,7},{3,6},{4,1},{5,0},{6,3},{7,2},{8,13},{9,12},{10,... | collective-permute-start | bytes 884744 | tf_op jit(solution)/shard_map/ppermute | solution.py:639
  381.5 34.7 %collective-permute-start.18 = (bf16[96,1536]{1,0:T(8,128)(2,1)S(1)}, bf16[96,1536]{1,0:T(8,128)(2,1)S(1)}, u32[]{:S(2)}, u32[]{:S(2)}) collective-permute-start(bf16[96,1536]{1,0:T(8,128)(2,1)S(1)} %convolution_convert_fusion.15), channel_id=1, source_target_pairs={{0,6},{1,7},{2,4},{3,5},{4,2},{5,3},{6,0},{7,1},{8,14},{9,15},{10,... | collective-permute-start | bytes 884744 | tf_op jit(solution)/shard_map/ppermute | solution.py:639
  386.0 30.2 %collective-permute-start.19 = (bf16[96,1536]{1,0:T(8,128)(2,1)S(1)}, bf16[96,1536]{1,0:T(8,128)(2,1)S(1)}, u32[]{:S(2)}, u32[]{:S(2)}) collective-permute-start(bf16[96,1536]{1,0:T(8,128)(2,1)S(1)} %convolution_convert_fusion.14), channel_id=1, source_target_pairs={{0,7},{1,6},{2,5},{3,4},{4,3},{5,2},{6,1},{7,0},{8,15},{9,14},{10,... | collective-permute-start | bytes 884744 | tf_op jit(solution)/shard_map/ppermute | solution.py:639
  444.8 28.6 %collective-permute-start.41 = (bf16[96,1536]{1,0:T(8,128)(2,1)S(1)}, bf16[96,1536]{1,0:T(8,128)(2,1)S(1)}, u32[]{:S(2)}, u32[]{:S(2)}) collective-permute-start(bf16[96,1536]{1,0:T(8,128)(2,1)S(1)} %get-tuple-element.97), channel_id=1, source_target_pairs={{0,2},{1,3},{2,0},{3,1},{4,6},{5,7},{6,4},{7,5},{8,10},{9,11},{10,... | collective-permute-start | bytes 884744 | tf_op jit(solution)/shard_map/ppermute | solution.py:639
  456.6 23.8 %collective-permute-start.42 = (bf16[96,1536]{1,0:T(8,128)(2,1)S(1)}, bf16[96,1536]{1,0:T(8,128)(2,1)S(1)}, u32[]{:S(2)}, u32[]{:S(2)}) collective-permute-start(bf16[96,1536]{1,0:T(8,128)(2,1)S(1)} %get-tuple-element.96), channel_id=1, source_target_pairs={{0,3},{1,2},{2,1},{3,0},{4,7},{5,6},{6,5},{7,4},{8,11},{9,10},{10,... | collective-permute-start | bytes 884744 | tf_op jit(solution)/shard_map/ppermute | solution.py:639
  456.9 23.5 %collective-permute-start.43 = (bf16[96,1536]{1,0:T(8,128)(2,1)S(1)}, bf16[96,1536]{1,0:T(8,128)(2,1)S(1)}, u32[]{:S(2)}, u32[]{:S(2)}) collective-permute-start(bf16[96,1536]{1,0:T(8,128)(2,1)S(1)} %get-tuple-element.95), channel_id=1, source_target_pairs={{0,4},{1,5},{2,6},{3,7},{4,0},{5,1},{6,2},{7,3},{8,12},{9,13},{10,... | collective-permute-start | bytes 884744 | tf_op jit(solution)/shard_map/ppermute | solution.py:639
  458.5 40.5 %collective-permute-start.44 = (bf16[96,1536]{1,0:T(8,128)(2,1)S(1)}, bf16[96,1536]{1,0:T(8,128)(2,1)S(1)}, u32[]{:S(2)}, u32[]{:S(2)}) collective-permute-start(bf16[96,1536]{1,0:T(8,128)(2,1)S(1)} %get-tuple-element.94), channel_id=1, source_target_pairs={{0,5},{1,4},{2,7},{3,6},{4,1},{5,0},{6,3},{7,2},{8,13},{9,12},{10,... | collective-permute-start | bytes 884744 | tf_op jit(solution)/shard_map/ppermute | solution.py:639
  459.9 39.2 %collective-permute-start.45 = (bf16[96,1536]{1,0:T(8,128)(2,1)S(1)}, bf16[96,1536]{1,0:T(8,128)(2,1)S(1)}, u32[]{:S(2)}, u32[]{:S(2)}) collective-permute-start(bf16[96,1536]{1,0:T(8,128)(2,1)S(1)} %get-tuple-element.93), channel_id=1, source_target_pairs={{0,6},{1,7},{2,4},{3,5},{4,2},{5,3},{6,0},{7,1},{8,14},{9,15},{10,... | collective-permute-start | bytes 884744 | tf_op jit(solution)/shard_map/ppermute | solution.py:639
  473.5 25.6 %collective-permute-start.46 = (bf16[96,1536]{1,0:T(8,128)(2,1)S(1)}, bf16[96,1536]{1,0:T(8,128)(2,1)S(1)}, u32[]{:S(2)}, u32[]{:S(2)}) collective-permute-start(bf16[96,1536]{1,0:T(8,128)(2,1)S(1)} %get-tuple-element.92), channel_id=1, source_target_pairs={{0,7},{1,6},{2,5},{3,4},{4,3},{5,2},{6,1},{7,0},{8,15},{9,14},{10,... | collective-permute-start | bytes 884744 | tf_op jit(solution)/shard_map/ppermute | solution.py:639
  512.2 217.2 %collective-permute-start.53 = (bf16[1024,384]{1,0:T(8,128)(2,1)}, bf16[1024,384]{1,0:T(8,128)(2,1)}, u32[]{:S(2)}, u32[]{:S(2)}) collective-permute-start(bf16[1024,384]{1,0:T(8,128)(2,1)} %convolution_convert_fusion.23), channel_id=1, source_target_pairs={{0,16},{8,24},{16,0},{24,8},{1,17},{9,25},{17,1},{25,9},{2,18},{10... | collective-permute-start | bytes 2359304 | tf_op jit(solution)/shard_map/ppermute | solution.py:639
  515.4 175.3 %collective-permute-start.54 = (bf16[1024,384]{1,0:T(8,128)(2,1)}, bf16[1024,384]{1,0:T(8,128)(2,1)}, u32[]{:S(2)}, u32[]{:S(2)}) collective-permute-start(bf16[1024,384]{1,0:T(8,128)(2,1)} %convolution_convert_fusion.22), channel_id=1, source_target_pairs={{0,16},{8,24},{16,0},{24,8},{1,17},{9,25},{17,1},{25,9},{2,18},{10... | collective-permute-start | bytes 2359304 | tf_op jit(solution)/shard_map/ppermute | solution.py:639
  518.3 217.2 %collective-permute-start.50 = (bf16[384,2048]{1,0:T(8,128)(2,1)}, bf16[384,2048]{1,0:T(8,128)(2,1)}, u32[]{:S(2)}, u32[]{:S(2)}) collective-permute-start(bf16[384,2048]{1,0:T(8,128)(2,1)} %convolution_convert_fusion.3), channel_id=1, source_target_pairs={{0,8},{8,0},{16,24},{24,16},{1,9},{9,1},{17,25},{25,17},{2,10},{10... | collective-permute-start | bytes 4718600 | tf_op jit(solution)/shard_map/ppermute | solution.py:639
  519.7 31.0 %collective-permute-start.26 = (bf16[96,1536]{1,0:T(8,128)(2,1)}, bf16[96,1536]{1,0:T(8,128)(2,1)}, u32[]{:S(2)}, u32[]{:S(2)}) collective-permute-start(bf16[96,1536]{1,0:T(8,128)(2,1)} %get-tuple-element.106), channel_id=1, source_target_pairs={{0,1},{1,0},{2,3},{3,2},{4,5},{5,4},{6,7},{7,6},{8,9},{9,8},{10,11... | collective-permute-start | bytes 884744 | tf_op jit(solution)/shard_map/ppermute | solution.py:639
  519.7 34.5 %collective-permute-start.27 = (bf16[96,1536]{1,0:T(8,128)(2,1)}, bf16[96,1536]{1,0:T(8,128)(2,1)}, u32[]{:S(2)}, u32[]{:S(2)}) collective-permute-start(bf16[96,1536]{1,0:T(8,128)(2,1)} %get-tuple-element.105), channel_id=1, source_target_pairs={{0,2},{1,3},{2,0},{3,1},{4,6},{5,7},{6,4},{7,5},{8,10},{9,11},{10,... | collective-permute-start | bytes 884744 | tf_op jit(solution)/shard_map/ppermute | solution.py:639
  546.2 96.7 %all-to-all-start.2 = ((bf16[8,256,192]{1,2,0:T(8,128)(2,1)}), bf16[8,256,192]{1,2,0:T(8,128)(2,1)}, u32[]{:S(2)}, u32[]{:S(2)}) async-start(bf16[8,256,192]{1,2,0:T(8,128)(2,1)} %bitcast.172), calls=%async_computation.2 | async-start | bytes 1572864 | tf_op jit(solution)/shard_map/all_to_all | solution.py:721
  550.7 27.2 %collective-permute-start.28 = (bf16[96,1536]{1,0:T(8,128)(2,1)}, bf16[96,1536]{1,0:T(8,128)(2,1)S(1)}, u32[]{:S(2)}, u32[]{:S(2)}) collective-permute-start(bf16[96,1536]{1,0:T(8,128)(2,1)} %get-tuple-element.104), channel_id=1, source_target_pairs={{0,3},{1,2},{2,1},{3,0},{4,7},{5,6},{6,5},{7,4},{8,11},{9,10},{10,... | collective-permute-start | bytes 884744 | tf_op jit(solution)/shard_map/ppermute | solution.py:639
  554.1 46.2 %collective-permute-start.29 = (bf16[96,1536]{1,0:T(8,128)(2,1)}, bf16[96,1536]{1,0:T(8,128)(2,1)S(1)}, u32[]{:S(2)}, u32[]{:S(2)}) collective-permute-start(bf16[96,1536]{1,0:T(8,128)(2,1)} %get-tuple-element.103), channel_id=1, source_target_pairs={{0,4},{1,5},{2,6},{3,7},{4,0},{5,1},{6,2},{7,3},{8,12},{9,13},{10,... | collective-permute-start | bytes 884744 | tf_op jit(solution)/shard_map/ppermute | solution.py:639
  577.9 49.6 %collective-permute-start.30 = (bf16[96,1536]{1,0:T(8,128)(2,1)}, bf16[96,1536]{1,0:T(8,128)(2,1)S(1)}, u32[]{:S(2)}, u32[]{:S(2)}) collective-permute-start(bf16[96,1536]{1,0:T(8,128)(2,1)} %get-tuple-element.102), channel_id=1, source_target_pairs={{0,5},{1,4},{2,7},{3,6},{4,1},{5,0},{6,3},{7,2},{8,13},{9,12},{10,... | collective-permute-start | bytes 884744 | tf_op jit(solution)/shard_map/ppermute | solution.py:639
  600.3 27.9 %collective-permute-start.31 = (bf16[96,1536]{1,0:T(8,128)(2,1)}, bf16[96,1536]{1,0:T(8,128)(2,1)S(1)}, u32[]{:S(2)}, u32[]{:S(2)}) collective-permute-start(bf16[96,1536]{1,0:T(8,128)(2,1)} %get-tuple-element.101), channel_id=1, source_target_pairs={{0,6},{1,7},{2,4},{3,5},{4,2},{5,3},{6,0},{7,1},{8,14},{9,15},{10,... | collective-permute-start | bytes 884744 | tf_op jit(solution)/shard_map/ppermute | solution.py:639
  628.3 86.6 %collective-permute-start.51 = (bf16[384,2048]{1,0:T(8,128)(2,1)}, bf16[384,2048]{1,0:T(8,128)(2,1)}, u32[]{:S(2)}, u32[]{:S(2)}) collective-permute-start(bf16[384,2048]{1,0:T(8,128)(2,1)} %convolution_convert_fusion.2), channel_id=1, source_target_pairs={{0,8},{8,0},{16,24},{24,16},{1,9},{9,1},{17,25},{25,17},{2,10},{10... | collective-permute-start | bytes 4718600 | tf_op jit(solution)/shard_map/ppermute | solution.py:639
  698.0 31.5 %collective-permute-start.55 = (bf16[1024,384]{1,0:T(8,128)(2,1)}, bf16[1024,384]{1,0:T(8,128)(2,1)}, u32[]{:S(2)}, u32[]{:S(2)}) collective-permute-start(bf16[1024,384]{1,0:T(8,128)(2,1)} %add_convert_fusion.2), channel_id=1, source_target_pairs={{0,8},{8,0},{16,24},{24,16},{1,9},{9,1},{17,25},{25,17},{2,10},{10... | collective-permute-start | bytes 2359304 | tf_op jit(solution)/shard_map/ppermute | solution.py:639
  700.5 23.7 %all-to-all-start.4 = ((bf16[8,48,384]{2,1,0:T(8,128)(2,1)}), bf16[8,48,384]{2,1,0:T(8,128)(2,1)S(1)}, u32[]{:S(2)}, u32[]{:S(2)}) async-start(bf16[8,48,384]{2,1,0:T(8,128)(2,1)} %bitcast.48), calls=%async_computation.4 | async-start | bytes 589824 | tf_op jit(solution)/shard_map/all_to_all | solution.py:721
  719.7 36.3 %collective-permute-start.52 = (bf16[384,2048]{1,0:T(8,128)(2,1)}, bf16[384,2048]{1,0:T(8,128)(2,1)}, u32[]{:S(2)}, u32[]{:S(2)}) collective-permute-start(bf16[384,2048]{1,0:T(8,128)(2,1)} %add_convert_fusion.1), channel_id=1, source_target_pairs={{0,16},{8,24},{16,0},{24,8},{1,17},{9,25},{17,1},{25,9},{2,18},{10... | collective-permute-start | bytes 4718600 | tf_op jit(solution)/shard_map/ppermute | solution.py:639
  724.2 39.0 %all-to-all-start.3 = ((bf16[8,256,320]{1,2,0:T(8,128)(2,1)}), bf16[8,256,320]{1,2,0:T(8,128)(2,1)}, u32[]{:S(2)}, u32[]{:S(2)}) async-start(bf16[8,256,320]{1,2,0:T(8,128)(2,1)} %copy.157), calls=%async_computation.3 | async-start | bytes 2621440 | tf_op jit(solution)/shard_map/all_to_all | solution.py:721
  (94 other events, 1234.8 us)
Sparse Core Ops, SparseCore 0:
  11.1 87.6 all-gather.2
  101.8 92.2 all-gather.4
  508.7 179.6 reduce-scatter.1

commit v2 on v0

--- a/solution.py
+++ b/solution.py
@@ -1,6 +1,10 @@
+import functools
+
 import jax
 import jax.numpy as jnp
 from jax import lax
+from jax.experimental import pallas as pl
+from jax.experimental.pallas import tpu as pltpu
 from jax.sharding import PartitionSpec as P
 
 QUERY_HEADS = 24
@@ -439,7 +443,964 @@
     )
 
 
+def contract(left, right, left_axis, right_axis):
+    return lax.dot_general(
+        left, right, (((left_axis,), (right_axis,)), ((), ())), preferred_element_type=jnp.float32
+    )
+
+
+def unit_of(rows):
+    factor = lax.rsqrt(jnp.mean(rows * rows, -1, keepdims=True) + EPSILON)
+    return (rows * factor, factor)
+
+
+def column_as_row(table, lane):
+    pick = (lax.broadcasted_iota(jnp.int32, (8, table.shape[1]), 1) == lane).astype(jnp.bfloat16)
+    return contract(pick, table, 1, 1)[:1]
+
+
+def split_low(value):
+    high = value.astype(jnp.bfloat16)
+    return (high, (value - high.astype(jnp.float32)).astype(jnp.bfloat16))
+
+
+def project_kernel(lane, rows_ref, weight_ref, table_ref, normed_ref, heads_ref, gain):
+    @pl.when(pl.program_id(0) == 0)
+    def _():
+        gain[...] = column_as_row(table_ref[...], lane)
+
+    unit, _ = unit_of(rows_ref[...].astype(jnp.float32))
+    normed = (unit * gain[...]).astype(jnp.bfloat16)
+    normed_ref[...] = normed
+    heads = jnp.dot(normed, weight_ref[...], preferred_element_type=jnp.float32)
+    heads_ref[0] = heads.T[: heads_ref.shape[1]].astype(jnp.bfloat16)
+
+
+def project(rows, head_weights, wide, lane, block):
+    length, width = rows.shape
+    lanes = head_weights.shape[1]
+    blocks = length // block
+    return pl.pallas_call(
+        functools.partial(project_kernel, lane),
+        grid=(blocks,),
+        in_specs=[
+            pl.BlockSpec((block, width), lambda i: (i, 0)),
+            pl.BlockSpec((width, lanes), lambda i: (0, 0)),
+            pl.BlockSpec((width, 128), lambda i: (0, lanes // 128 - 1)),
+        ],
+        out_specs=[
+            pl.BlockSpec((block, width), lambda i: (i, 0)),
+            pl.BlockSpec((1, wide, block), lambda i: (i, 0, 0)),
+        ],
+        out_shape=[
+            jax.ShapeDtypeStruct((length, width), jnp.bfloat16),
+            jax.ShapeDtypeStruct((blocks, wide, block), jnp.bfloat16),
+        ],
+        scratch_shapes=[pltpu.VMEM((1, width), jnp.float32)],
+        compiler_params=pltpu.CompilerParams(vmem_limit_bytes=40 * 2**20),
+        name="project",
+    )(rows, head_weights, head_weights)
+
+
+def beside(rows, block, heads):
+    return jnp.concatenate([rows[h * HEAD_SIZE : (h + 1) * HEAD_SIZE] for h in range(heads)], 1)
+
+
+def attend_kernel(spans, q_ref, heads_ref, segr_ref, segc_ref, low_ref, mixed_ref, totals_ref):
+    step = pl.program_id(0)
+    block = q_ref.shape[2]
+    heads = QUERY_HEADS // KEY_VALUE_HEADS
+    share = heads * HEAD_SIZE
+    queries = beside(q_ref[0, :share, :] * jnp.bfloat16(HEAD_SIZE ** (-0.5)), block, heads)
+    seg_row = segr_ref[...]
+
+    def scores_of(j):
+        return contract(heads_ref[j, share : share + HEAD_SIZE, :], queries, 0, 0)
+
+    def same_doc(j):
+        return segc_ref[pl.ds(pl.multiple_of(j * block, block), block), :] == seg_row
+
+    def fold(j, scores, carry):
+        top, total, out = carry
+        values = heads_ref[j, share + HEAD_SIZE : share + 2 * HEAD_SIZE, :]
+        new_top = jnp.maximum(top, jnp.max(scores, 0, keepdims=True))
+        probs = jnp.exp(scores - new_top)
+        decay = jnp.exp(top - new_top)
+        total = total * decay + jnp.sum(probs, 0, keepdims=True)
+        out = out * decay + jnp.dot(
+            values, probs.astype(jnp.bfloat16), preferred_element_type=jnp.float32
+        )
+        return (new_top, total, out)
+
+    def masked(j, carry):
+        allowed = jnp.concatenate([same_doc(j)] * heads, 1)
+        return fold(j, jnp.where(allowed, scores_of(j), NEGATIVE_LARGE), carry)
+
+    columns = heads * block
+    carry = (
+        jnp.full((1, columns), NEGATIVE_LARGE, jnp.float32),
+        jnp.zeros((1, columns), jnp.float32),
+        jnp.zeros((HEAD_SIZE, columns), jnp.float32),
+    )
+    first, full = spans[0, step], spans[1, step]
+    carry = lax.fori_loop(first, full, masked, carry)
+    carry = lax.fori_loop(full, step, lambda j, kept: fold(j, scores_of(j), kept), carry)
+    key_spot = lax.broadcasted_iota(jnp.int32, (block, block), 0)
+    query_spot = lax.broadcasted_iota(jnp.int32, (block, block), 1)
+    allowed = same_doc(step) & (key_spot <= query_spot)
+    allowed = jnp.concatenate([allowed] * heads, 1)
+    top, total, out = fold(step, jnp.where(allowed, scores_of(step), NEGATIVE_LARGE), carry)
+    out = out / total
+    totals = top + jnp.log(total)
+    for h in range(heads):
+        part = out[:, h * block : (h + 1) * block]
+        mixed_ref[0, h * HEAD_SIZE : (h + 1) * HEAD_SIZE, :] = part
+        low_ref[0, h * HEAD_SIZE : (h + 1) * HEAD_SIZE, :] = part.astype(jnp.bfloat16)
+        totals_ref[0, h : h + 1, :] = totals[:, h * block : (h + 1) * block]
+
+
+def attend(spans, projected, seg_row, seg_col):
+    blocks, wide, block = projected.shape
+    share = wide - 2 * HEAD_SIZE
+    length = blocks * block
+    each = lambda height: pl.BlockSpec((1, height, block), lambda i, spans: (i, 0, 0))
+    return pl.pallas_call(
+        attend_kernel,
+        grid_spec=pltpu.PrefetchScalarGridSpec(
+            num_scalar_prefetch=1,
+            grid=(blocks,),
+            in_specs=[
+                pl.BlockSpec((1, wide, block), lambda i, spans: (i, 0, 0)),
+                pl.BlockSpec((blocks, wide, block), lambda i, spans: (0, 0, 0)),
+                pl.BlockSpec((1, block), lambda i, spans: (0, i)),
+                pl.BlockSpec((length, 1), lambda i, spans: (0, 0)),
+            ],
+            out_specs=[each(share), each(share), each(8)],
+        ),
+        out_shape=[
+            jax.ShapeDtypeStruct((blocks, share, block), jnp.bfloat16),
+            jax.ShapeDtypeStruct((blocks, share, block), jnp.float32),
+            jax.ShapeDtypeStruct((blocks, 8, block), jnp.float32),
+        ],
+        compiler_params=pltpu.CompilerParams(vmem_limit_bytes=40 * 2**20),
+        name="attend",
+    )(spans, projected, projected, seg_row, seg_col)
+
+
+def attend_back_kernel(
+    spans, q_ref, g_ref, heads_ref, segr_ref, segc_ref, mixed_ref, totals_ref,
+    blocks_ref, line_ref, dk_sum, dv_sum,
+):
+    step = pl.program_id(0)
+    blocks, _, block = heads_ref.shape
+    heads = QUERY_HEADS // KEY_VALUE_HEADS
+    share = heads * HEAD_SIZE
+    queries = beside(q_ref[0, :share, :] * jnp.bfloat16(HEAD_SIZE ** (-0.5)), block, heads)
+    grads = beside(g_ref[0], block, heads)
+    delta = jnp.sum(
+        grads.astype(jnp.float32) * beside(mixed_ref[0], block, heads), 0, keepdims=True
+    )
+    totals = jnp.concatenate([totals_ref[0, h : h + 1, :] for h in range(heads)], 1)
+    seg_row = segr_ref[...]
+
+    @pl.when(step == 0)
+    def _():
+        dk_sum[...] = jnp.zeros_like(dk_sum)
+        dv_sum[...] = jnp.zeros_like(dv_sum)
+
+    def turn(j, query_sum, allowed):
+        keys = heads_ref[j, share : share + HEAD_SIZE, :]
+        values = heads_ref[j, share + HEAD_SIZE : share + 2 * HEAD_SIZE, :]
+        probs = jnp.exp(contract(keys, queries, 0, 0) - totals)
+        if allowed is not None:
+            probs = jnp.where(jnp.concatenate([allowed] * heads, 1), probs, 0.0)
+        grad_scores = (probs * (contract(values, grads, 0, 0) - delta)).astype(jnp.bfloat16)
+        dv_sum[j] += contract(grads, probs.astype(jnp.bfloat16), 1, 1)
+        dk_sum[j] += contract(queries, grad_scores, 1, 1)
+        return query_sum + jnp.dot(keys, grad_scores, preferred_element_type=jnp.float32)
+
+    def same_doc(j):
+        return segc_ref[pl.ds(pl.multiple_of(j * block, block), block), :] == seg_row
+
+    query_sum = jnp.zeros((HEAD_SIZE, heads * block), jnp.float32)
+    first, full = spans[0, step], spans[1, step]
+    query_sum = lax.fori_loop(first, full, lambda j, c: turn(j, c, same_doc(j)), query_sum)
+    query_sum = lax.fori_loop(full, step, lambda j, c: turn(j, c, None), query_sum)
+    key_spot = lax.broadcasted_iota(jnp.int32, (block, block), 0)
+    query_spot = lax.broadcasted_iota(jnp.int32, (block, block), 1)
+    query_sum = turn(step, query_sum, same_doc(step) & (key_spot <= query_spot))
+    query_sum = (query_sum * HEAD_SIZE ** (-0.5)).astype(jnp.bfloat16)
+
+    def spread(j, at, size, value):
+        blocks_ref[j, at : at + size, :] = value
+        there = pl.ds(pl.multiple_of(j * block, block), block)
+        line_ref[at : at + size, there] = value
+
+    for h in range(heads):
+        spread(step, h * HEAD_SIZE, HEAD_SIZE, query_sum[:, h * block : (h + 1) * block])
+
+    @pl.when(step == pl.num_programs(0) - 1)
+    def _():
+        for j in range(blocks):
+            spread(j, share, HEAD_SIZE, dk_sum[j].astype(jnp.bfloat16))
+            spread(j, share + HEAD_SIZE, HEAD_SIZE, dv_sum[j].astype(jnp.bfloat16))
+
+
+def attend_backward(spans, projected, grads, seg_row, seg_col, mixed, totals):
+    blocks, wide, block = projected.shape
+    share = wide - 2 * HEAD_SIZE
+    length = blocks * block
+    each = lambda height: pl.BlockSpec((1, height, block), lambda i, spans: (i, 0, 0))
+    return pl.pallas_call(
+        attend_back_kernel,
+        grid_spec=pltpu.PrefetchScalarGridSpec(
+            num_scalar_prefetch=1,
+            grid=(blocks,),
+            in_specs=[
+                pl.BlockSpec((1, wide, block), lambda i, spans: (i, 0, 0)),
+                each(share),
+                pl.BlockSpec((blocks, wide, block), lambda i, spans: (0, 0, 0)),
+                pl.BlockSpec((1, block), lambda i, spans: (0, i)),
+                pl.BlockSpec((length, 1), lambda i, spans: (0, 0)),
+                each(share),
+                each(8),
+            ],
+            out_specs=[
+                pl.BlockSpec((blocks, wide, block), lambda i, spans: (0, 0, 0)),
+                pl.BlockSpec((wide, length), lambda i, spans: (0, 0)),
+            ],
+            scratch_shapes=[
+                pltpu.VMEM((blocks, HEAD_SIZE, block), jnp.float32),
+                pltpu.VMEM((blocks, HEAD_SIZE, block), jnp.float32),
+            ],
+        ),
+        out_shape=[
+            jax.ShapeDtypeStruct((blocks, wide, block), jnp.bfloat16),
+            jax.ShapeDtypeStruct((wide, length), jnp.bfloat16),
+        ],
+        compiler_params=pltpu.CompilerParams(vmem_limit_bytes=40 * 2**20),
+        name="attend_backward",
+    )(spans, projected, grads, projected, seg_row, seg_col, mixed, totals)
+
+
+def hits(slots, height):
+    spot = lax.broadcasted_iota(jnp.int32, (height, slots.shape[1]), 0)
+    return (spot == slots[0:1, :], spot == slots[1:2, :])
+
+
+def spread_kernel(slots_ref, rows_ref, *out_refs):
+    size = out_refs[0].shape[0]
+    first, second = hits(slots_ref[...], size * len(out_refs))
+    chosen = (first | second).astype(jnp.bfloat16)
+    for k, out_ref in enumerate(out_refs):
+        out_ref[...] = jnp.dot(
+            chosen[k * size : (k + 1) * size], rows_ref[...], preferred_element_type=jnp.float32
+        ).astype(jnp.bfloat16)
+
+
+def spread_rows(slots, rows, size, blocks):
+    return pl.pallas_call(
+        spread_kernel,
+        out_shape=[jax.ShapeDtypeStruct((size, rows.shape[1]), jnp.bfloat16)] * blocks,
+        compiler_params=pltpu.CompilerParams(vmem_limit_bytes=40 * 2**20),
+        name="spread_rows",
+    )(slots, rows)
+
+
+def middle_kernel(
+    lane, router_lane, start_ref, mixed_ref, weight_ref, table_ref, slots_ref, routes_ref,
+    middle_ref, sent_ref, gates_ref,
+):
+    table = table_ref[...]
+    middle = start_ref[...].astype(jnp.float32) + contract(mixed_ref[...].T, weight_ref[...], 1, 1)
+    middle_ref[...] = middle
+    unit, _ = unit_of(middle)
+    expert_low = (unit * column_as_row(table, lane)).astype(jnp.bfloat16)
+    first, second = hits(slots_ref[...], sent_ref.shape[0])
+    sent_ref[...] = jnp.dot(
+        (first | second).astype(jnp.bfloat16), expert_low, preferred_element_type=jnp.float32
+    ).astype(jnp.bfloat16)
+    logits = jnp.dot(expert_low, table, preferred_element_type=jnp.float32).T
+    spot = lax.broadcasted_iota(jnp.int32, logits.shape, 0) - router_lane
+    chosen = [
+        jnp.sum(jnp.where(spot == routes_ref[c : c + 1, :], logits, 0.0), 0, keepdims=True)
+        for c in range(2)
+    ]
+    top = jnp.maximum(chosen[0], chosen[1])
+    parts = [jnp.exp(value - top) for value in chosen]
+    gates_ref[...] = jnp.concatenate([part / (parts[0] + parts[1]) for part in parts], 0)
+
+
+def middle_part(start, mixed, weight, head_weights, slots, routes, lane, router_lane, height):
+    rows, width = start.shape
+    lanes = head_weights.shape[1]
+    whole = lambda shape: pl.BlockSpec(shape, lambda i: (0, 0))
+    return pl.pallas_call(
+        functools.partial(middle_kernel, lane, router_lane),
+        grid=(1,),
+        in_specs=[
+            whole(start.shape),
+            whole(mixed.shape),
+            whole(weight.shape),
+            pl.BlockSpec((width, 128), lambda i: (0, lanes // 128 - 1)),
+            whole(slots.shape),
+            whole(routes.shape),
+        ],
+        out_specs=[whole((rows, width)), whole((height, width)), whole((2, rows))],
+        out_shape=[
+            jax.ShapeDtypeStruct((rows, width), jnp.float32),
+            jax.ShapeDtypeStruct((height, width), jnp.bfloat16),
+            jax.ShapeDtypeStruct((2, rows), jnp.float32),
+        ],
+        compiler_params=pltpu.CompilerParams(vmem_limit_bytes=40 * 2**20),
+        name="middle",
+    )(start, mixed, weight, head_weights, slots, routes)
+
+
+def block_place(own_ref, axis, k, size):
+    return pl.ds(pl.multiple_of(jnp.bitwise_xor(own_ref[axis], k) * size, size), size)
+
+
+def assemble_weights(own_ref, part_refs, gate, up, outer):
+    count = len(part_refs) // 3
+    for k in range(count):
+        size = part_refs[k].shape[0]
+        place = block_place(own_ref, 1, k, size)
+        gate[place, :] = part_refs[k][...]
+        up[place, :] = part_refs[count + k][...]
+        outer[:, place] = part_refs[2 * count + k][...]
+
+
+def expert_kernel(router_lane, blocks, own_ref, rows_ref, *refs):
+    weight_refs, (table_ref, other_ref) = refs[:12], refs[12:14]
+    pre_gate_ref, pre_up_ref, hidden_ref, gates_ref = refs[14:18]
+    part_refs, (part_sum, gate, up, outer) = refs[18 : 18 + blocks], refs[18 + blocks :]
+    step = pl.program_id(0)
+    size = part_refs[0].shape[0]
+    rows = rows_ref[...]
+    assemble_weights(own_ref, weight_refs, gate, up, outer)
+
+    @pl.when(step == 0)
+    def _():
+        lane = lax.broadcasted_iota(jnp.int32, (rows.shape[0], 128), 1) - router_lane
+        logits = jnp.dot(rows, table_ref[...], preferred_element_type=jnp.float32)
+        own = jnp.sum(jnp.where(lane == own_ref[0], logits, 0.0), 1, keepdims=True)
+        other = jnp.sum(jnp.where(lane == other_ref[...], logits, 0.0), 1, keepdims=True)
+        top = jnp.maximum(own, other)
+        own, other = jnp.exp(own - top), jnp.exp(other - top)
+        gates_ref[:, 0:1] = own / (own + other)
+        gates_ref[:, 1:2] = other / (own + other)
+        part_sum[...] = jnp.zeros_like(part_sum)
+
+    gate_pre = jnp.dot(rows, gate[...], preferred_element_type=jnp.float32)
+    up_pre = jnp.dot(rows, up[...], preferred_element_type=jnp.float32)
+    pre_gate_ref[...] = gate_pre
+    pre_up_ref[...] = up_pre
+    hidden = (gate_pre / (1.0 + jnp.exp(-gate_pre)) * up_pre).astype(jnp.bfloat16)
+    hidden_ref[...] = hidden
+    part_sum[...] += jnp.dot(hidden, outer[...], preferred_element_type=jnp.float32)
+
+    @pl.when(step == pl.num_programs(0) - 1)
+    def _():
+        for k, ref in enumerate(part_refs):
+            ref[...] = part_sum[block_place(own_ref, 0, k, size), :].astype(jnp.bfloat16)
+
+
+def weight_specs(inner, outer, tile, steps):
+    size = inner[0].shape[0]
+    return (
+        [pl.BlockSpec((size, tile), lambda i, own: (0, i))] * len(inner)
+        + [pl.BlockSpec((size, tile), lambda i, own: (0, steps + i))] * len(inner)
+        + [pl.BlockSpec((tile, size), lambda i, own: (i, 0))] * len(outer)
+    )
+
+
+def expert_forward_pass(own, rows, inner, outer, head_weights, other, router_lane, tile, blocks):
+    height, width = rows.shape
+    units = outer[0].shape[0]
+    steps = units // tile
+    lanes = head_weights.shape[1]
+    whole = lambda shape: pl.BlockSpec(shape, lambda i, own: (0, 0))
+    tiled = lambda rows, off: pl.BlockSpec((rows, tile), lambda i, own: (0, off + i))
+    shape = jax.ShapeDtypeStruct
+    low, f32 = jnp.bfloat16, jnp.float32
+    outcome = pl.pallas_call(
+        functools.partial(expert_kernel, router_lane, blocks),
+        grid_spec=pltpu.PrefetchScalarGridSpec(
+            num_scalar_prefetch=1,
+            grid=(steps,),
+            in_specs=[whole(rows.shape)]
+            + weight_specs(inner, outer, tile, steps)
+            + [
+                pl.BlockSpec((width, 128), lambda i, own: (0, lanes // 128 - 1)),
+                whole(other.shape),
+            ],
+            out_specs=[tiled(height, 0)] * 3
+            + [whole((height, 128))]
+            + [whole((height // blocks, width))] * blocks,
+            scratch_shapes=[
+                pltpu.VMEM((height, width), f32),
+                pltpu.VMEM((width, tile), low),
+                pltpu.VMEM((width, tile), low),
+                pltpu.VMEM((tile, width), low),
+            ],
+        ),
+        out_shape=[shape((height, units), f32)] * 2
+        + [shape((height, units), low), shape((height, 128), f32)]
+        + [shape((height // blocks, width), low)] * blocks,
+        compiler_params=pltpu.CompilerParams(vmem_limit_bytes=56 * 2**20),
+        name="expert",
+    )(own, rows, *inner, *inner, *outer, head_weights, other)
+    return outcome[:4], list(outcome[4:])
+
+
+def expert_back_kernel(router_lane, blocks, own_ref, *refs):
+    cot_refs, part_refs, refs = refs[:blocks], refs[blocks : 2 * blocks], refs[2 * blocks :]
+    rows_ref, gates_ref, pre_gate_ref, pre_up_ref = refs[:4]
+    weight_refs, refs = refs[4:16], refs[16:]
+    table_ref, other_ref, pre_ref, grad_ref, back_ref, router_ref = refs[:6]
+    cot, back_sum, gate, up, outer = refs[6:]
+    step = pl.program_id(0)
+    tile = gate.shape[1]
+    assemble_weights(own_ref, weight_refs, gate, up, outer)
+    units = tile * pl.num_programs(0)
+    size = cot_refs[0].shape[0]
+    gates = gates_ref[...]
+
+    @pl.when(step == 0)
+    def _():
+        for k, ref in enumerate(cot_refs):
+            cot[block_place(own_ref, 0, k, size), :] = ref[...]
+        grad_ref[...] = (gates[:, 0:1] * cot[...].astype(jnp.float32)).astype(jnp.bfloat16)
+        back_sum[...] = jnp.zeros_like(back_sum)
+
+    gate_pre, up_pre = pre_gate_ref[...], pre_up_ref[...]
+    grad_hidden = contract(grad_ref[...], outer[...], 1, 1)
+    sigma = 1.0 / (1.0 + jnp.exp(-gate_pre))
+    grad_gate = grad_hidden * up_pre * sigma * (1.0 + gate_pre * (1.0 - sigma))
+    grad_gate = grad_gate.astype(jnp.bfloat16)
+    grad_up = (grad_hidden * (gate_pre * sigma)).astype(jnp.bfloat16)
+    at = pl.multiple_of(step * tile, tile)
+    pre_ref[:, pl.ds(at, tile)] = grad_gate
+    pre_ref[:, pl.ds(pl.multiple_of(units + at, tile), tile)] = grad_up
+    back_sum[...] += contract(grad_gate, gate[...], 1, 1) + contract(grad_up, up[...], 1, 1)
+
+    @pl.when(step == pl.num_programs(0) - 1)
+    def _():
+        table = table_ref[...]
+        total = jnp.zeros(router_ref.shape, jnp.float32)
+        for k in range(blocks):
+            place = block_place(own_ref, 0, k, size)
+            grad_gates = jnp.sum(
+                cot_refs[k][...].astype(jnp.float32) * part_refs[k][...].astype(jnp.float32),
+                1,
+                keepdims=True,
+            )
+            gates_k = gates_ref[place, :]
+            lane_k = lax.broadcasted_iota(jnp.int32, (size, 128), 1) - router_lane
+            sides_k = (lane_k == own_ref[0]).astype(jnp.float32) - (
+                lane_k == other_ref[place, :]
+            ).astype(jnp.float32)
+            high, rest = split_low(gates_k[:, 0:1] * gates_k[:, 1:2] * grad_gates * sides_k)
+            routed = contract(high, table, 1, 1) + contract(rest, table, 1, 1)
+            back = back_sum[place, :].astype(jnp.bfloat16).astype(jnp.float32)
+            back_ref[place, :] = (back + routed).astype(jnp.bfloat16)
+            rows_k = rows_ref[place, :]
+            total = total + contract(high, rows_k, 0, 0) + contract(rest, rows_k, 0, 0)
+        router_ref[...] = total
+
+
+def expert_backward_pass(
+    own, cot_blocks, part_blocks, rows, gates, pre_gate, pre_up, inner, outer, head_weights, other,
+    router_lane, tile,
+):
+    height, width = rows.shape
+    units = outer[0].shape[0]
+    steps = units // tile
+    lanes = head_weights.shape[1]
+    blocks = len(cot_blocks)
+    whole = lambda shape: pl.BlockSpec(shape, lambda i, own: (0, 0))
+    tiled = lambda rows, off: pl.BlockSpec((rows, tile), lambda i, own: (0, off + i))
+    low, f32 = jnp.bfloat16, jnp.float32
+    return pl.pallas_call(
+        functools.partial(expert_back_kernel, router_lane, blocks),
+        grid_spec=pltpu.PrefetchScalarGridSpec(
+            num_scalar_prefetch=1,
+            grid=(steps,),
+            in_specs=[whole((height // blocks, width))] * (2 * blocks)
+            + [
+                whole(rows.shape),
+                whole(gates.shape),
+                tiled(height, 0),
+                tiled(height, 0),
+            ]
+            + weight_specs(inner, outer, tile, steps)
+            + [
+                pl.BlockSpec((width, 128), lambda i, own: (0, lanes // 128 - 1)),
+                whole(other.shape),
+            ],
+            out_specs=[
+                whole((height, 2 * units)),
+                whole((height, width)),
+                whole((height, width)),
+                whole((128, width)),
+            ],
+            scratch_shapes=[
+                pltpu.VMEM((height, width), low),
+                pltpu.VMEM((height, width), f32),
+                pltpu.VMEM((width, tile), low),
+                pltpu.VMEM((width, tile), low),
+                pltpu.VMEM((tile, width), low),
+            ],
+        ),
+        out_shape=[
+            jax.ShapeDtypeStruct((height, 2 * units), low),
+            jax.ShapeDtypeStruct((height, width), low),
+            jax.ShapeDtypeStruct((height, width), low),
+            jax.ShapeDtypeStruct((128, width), f32),
+        ],
+        compiler_params=pltpu.CompilerParams(vmem_limit_bytes=56 * 2**20),
+        name="expert_backward",
+    )(
+        own, *cot_blocks, *part_blocks, rows, gates, pre_gate, pre_up, *inner, *inner, *outer,
+        head_weights, other,
+    )
+
+
+def back_kernel(
+    lane, middle_ref, cot_ref, home_ref, weight_ref, table_ref, slots_ref,
+    grad_ref, branch_ref, gain_ref, mixed_ref,
+):
+    first, second = hits(slots_ref[...], home_ref.shape[0])
+    grad_in = contract((first | second).astype(jnp.bfloat16), home_ref[...], 0, 0)
+    unit, factor = unit_of(middle_ref[...])
+    gain_ref[...] = jnp.sum(grad_in * unit, 0, keepdims=True)
+    scaled = grad_in * column_as_row(table_ref[...], lane)
+    inner_part = factor * (scaled - unit * jnp.mean(scaled * unit, -1, keepdims=True))
+    grad_middle = cot_ref[...].astype(jnp.float32) + inner_part
+    grad_ref[...] = grad_middle
+    branch = grad_middle.astype(jnp.bfloat16)
+    branch_ref[...] = branch
+    mixed = jnp.dot(branch, weight_ref[...], preferred_element_type=jnp.float32)
+    mixed_ref[...] = mixed.T.astype(jnp.bfloat16)
+
+
+def back_part(middle, cot, home, weight, head_weights, slots, lane):
+    rows, width = middle.shape
+    lanes = head_weights.shape[1]
+    whole = lambda shape: pl.BlockSpec(shape, lambda i: (0, 0))
+    return pl.pallas_call(
+        functools.partial(back_kernel, lane),
+        grid=(1,),
+        in_specs=[
+            whole((rows, width)),
+            whole((rows, width)),
+            whole(home.shape),
+            whole(weight.shape),
+            pl.BlockSpec((width, 128), lambda i: (0, lanes // 128 - 1)),
+            whole(slots.shape),
+        ],
+        out_specs=[
+            whole((rows, width)),
+            whole((rows, width)),
+            whole((1, width)),
+            whole((weight.shape[1], rows)),
+        ],
+        out_shape=[
+            jax.ShapeDtypeStruct((rows, width), jnp.float32),
+            jax.ShapeDtypeStruct((rows, width), jnp.bfloat16),
+            jax.ShapeDtypeStruct((1, width), jnp.float32),
+            jax.ShapeDtypeStruct((weight.shape[1], rows), jnp.bfloat16),
+        ],
+        compiler_params=pltpu.CompilerParams(vmem_limit_bytes=48 * 2**20),
+        name="back",
+    )(middle, cot, home, weight, head_weights, slots)
+
+
+def weight_kernel(place, normed_ref, grads_ref, extra_ref, out_ref):
+    total = jnp.dot(grads_ref[...], normed_ref[...], preferred_element_type=jnp.float32)
+    out_ref[0] = jnp.concatenate([total, extra_ref[...]], 0).T.astype(jnp.bfloat16)
+
+
+def weight_terms(place, normed, grads, extra, parts):
+    length, width = normed.shape
+    wide = grads.shape[0]
+    span = width // parts
+    lanes = wide + extra.shape[0]
+    near = lambda k, place: (0, jnp.bitwise_xor(place[0], k))
+    return pl.pallas_call(
+        weight_kernel,
+        grid_spec=pltpu.PrefetchScalarGridSpec(
+            num_scalar_prefetch=1,
+            grid=(parts,),
+            in_specs=[
+                pl.BlockSpec((length, span), near),
+                pl.BlockSpec((wide, length), lambda k, place: (0, 0)),
+                pl.BlockSpec((extra.shape[0], span), near),
+            ],
+            out_specs=pl.BlockSpec((1, span, lanes), lambda k, place: (k, 0, 0)),
+        ),
+        out_shape=jax.ShapeDtypeStruct((parts, span, lanes), jnp.bfloat16),
+        compiler_params=pltpu.CompilerParams(vmem_limit_bytes=40 * 2**20),
+        name="weight_terms",
+    )(place, normed, grads, extra)
+
+
+def mixture_kernel(slots_ref, gates_ref, middle_ref, *refs):
+    part_refs, out_ref = refs[:-1], refs[-1]
+    size = part_refs[0].shape[0]
+    first, second = hits(slots_ref[...], size * len(part_refs))
+    total = middle_ref[...]
+    shares = gates_ref[...]
+    for _ in range(3):
+        piece = shares.astype(jnp.bfloat16)
+        shares = shares - piece.astype(jnp.float32)
+        piece = piece.astype(jnp.float32)
+        weights = jnp.where(first, piece[0:1], 0.0) + jnp.where(second, piece[1:2], 0.0)
+        weights = weights.astype(jnp.bfloat16)
+        for k, ref in enumerate(part_refs):
+            total = total + contract(weights[k * size : (k + 1) * size], ref[...], 0, 0)
+    out_ref[...] = total.astype(jnp.bfloat16)
+
+
+def mixture(slots, gates, middle, parts):
+    return pl.pallas_call(
+        mixture_kernel,
+        out_shape=jax.ShapeDtypeStruct(middle.shape, jnp.bfloat16),
+        compiler_params=pltpu.CompilerParams(vmem_limit_bytes=40 * 2**20),
+        name="mixture",
+    )(slots, gates, middle, *parts)
+
+
+def weight_grads_kernel(
+    share, home_ref, query_weight_ref, keyval_weight_ref, gain_ref,
+    query_ref, keyval_ref, router_ref, gains_ref,
+):
+    count = home_ref.shape[0]
+    cols = share + 2 * HEAD_SIZE
+    half = count * HEAD_SIZE
+    experts = router_ref.shape[1]
+    small = jnp.zeros((home_ref.shape[1], home_ref.shape[2] - cols), jnp.float32)
+    for e in range(count):
+        part = home_ref[e].astype(jnp.float32)
+        query_ref[:, e * share : (e + 1) * share] = part[:, :share]
+        at = e * HEAD_SIZE
+        keyval_ref[:, at : at + HEAD_SIZE] = part[:, share : share + HEAD_SIZE]
+        keyval_ref[:, half + at : half + at + HEAD_SIZE] = part[:, share + HEAD_SIZE : cols]
+        small = small + part[:, cols:]
+    router_ref[...] = small[:, :experts]
+    products = jnp.sum(
+        query_ref[...] * query_weight_ref[...].astype(jnp.float32), 1, keepdims=True
+    ) + jnp.sum(keyval_ref[...] * keyval_weight_ref[...].astype(jnp.float32), 1, keepdims=True)
+    gains_ref[:, 0:1] = products / gain_ref[...].astype(jnp.float32)
+    gains_ref[:, 1:2] = small[:, experts : experts + 1]
+
+
+def weight_grads(home, query_weight, keyval_weight, gain, share, experts):
+    shape = lambda width: jax.ShapeDtypeStruct((query_weight.shape[0], width), jnp.float32)
+    return pl.pallas_call(
+        functools.partial(weight_grads_kernel, share),
+        out_shape=[
+            shape(query_weight.shape[1]),
+            shape(keyval_weight.shape[1]),
+            shape(experts),
+            shape(2),
+        ],
+        compiler_params=pltpu.CompilerParams(vmem_limit_bytes=40 * 2**20),
+        name="weight_grads",
+    )(home, query_weight, keyval_weight, gain)
+
+
+def after(values, *earlier):
+    return lax.optimization_barrier((values, earlier))[0]
+
+
+def flip_exchange(block, axis, flip):
+    count = lax.axis_size(axis)
+    return lax.ppermute(block, axis, [(i, i ^ flip) for i in range(count)])
+
+
+def swap_near_blocks(blocks, flips):
+    return [flip_exchange(blocks[flip], "fsdp", flip) for flip in flips]
+
+
+def swap_near(block, axis, flips):
+    return [flip_exchange(block, axis, flip) for flip in flips]
+
+
+def in_order(parts, axis):
+    stacked = jnp.stack(parts)
+    index = lax.axis_index(axis)
+    return jnp.stack(
+        [
+            lax.dynamic_index_in_dim(stacked, jnp.bitwise_xor(index, j), 0, keepdims=False)
+            for j in range(len(parts))
+        ]
+    )
+
+
+def all_to_all(blocks):
+    return lax.all_to_all(blocks, "fsdp", split_axis=0, concat_axis=0, tiled=True)
+
+
+def gather(block, axis):
+    return lax.all_gather(block, axis, axis=0, tiled=True)
+
+
+def per_device_heads(
+    tokens,
+    segment_ids,
+    routes,
+    query_weight,
+    key_value_weight,
+    output_weight,
+    router_weight,
+    gain_before,
+    gain_middle,
+    inner_weight,
+    outer_weight,
+    cotangent,
+):
+    f32, low = jnp.float32, jnp.bfloat16
+    _, rows, width = tokens.shape
+    count = lax.axis_size("fsdp")
+    experts = router_weight.shape[1]
+    index, group = lax.axis_index("fsdp"), lax.axis_index("dp")
+    core = index % 2
+    capacity = 3 * rows // 8
+    height = experts * capacity
+    length = count * rows
+    shard = query_weight.shape[0]
+    share = QUERY_HEADS // KEY_VALUE_HEADS * HEAD_SIZE
+    cols = share + 2 * HEAD_SIZE
+    half = KEY_VALUE_HEADS * HEAD_SIZE
+    ff = outer_weight.shape[0]
+    size = inner_weight.shape[0]
+
+    start_low = tokens.reshape(rows, width)
+    cot_low = cotangent.reshape(rows, width)
+
+    route = routes.reshape(rows, 2)
+    route_flat = route.reshape(rows * 2)
+    picks = route_flat[:, None] == jnp.arange(experts, dtype=jnp.int32)[None, :]
+    before = jnp.dot(
+        jnp.tril(jnp.ones((rows * 2, rows * 2), low), -1),
+        picks.astype(low),
+        preferred_element_type=f32,
+    )
+    rank = jnp.sum(jnp.where(picks, before, 0.0), 1).astype(jnp.int32).reshape(rows, 2)
+    route_lines = route.T
+    slots = (route * capacity + rank).T
+    slots_near = (jnp.bitwise_xor(route, index) * capacity + rank).T
+    spots = jnp.arange(height, dtype=jnp.int32)[:, None]
+    other_route = jnp.sum(
+        jnp.where(slots[0:1] == spots, route_lines[1:2], 0)
+        + jnp.where(slots[1:2] == spots, route_lines[0:1], 0),
+        1,
+    )
+
+    by_head = jnp.concatenate(
+        [
+            query_weight.reshape(shard, count, share),
+            key_value_weight[:, :half].reshape(shard, count, HEAD_SIZE),
+            key_value_weight[:, half:].reshape(shard, count, HEAD_SIZE),
+        ],
+        2,
+    )
+    lanes = 128 * -(-(cols + 2 + experts) // 128)
+    table_lane = lanes - 128
+    router_lane = cols - table_lane
+    first_lane, second_lane = router_lane + experts, router_lane + experts + 1
+    extras = jnp.concatenate([router_weight, gain_before[:, None], gain_middle[:, None]], 1)
+    extras = jnp.broadcast_to(extras[None], (count, shard, 2 + experts))
+    head_block = jnp.concatenate([by_head.transpose(1, 0, 2), extras], 2)
+    head_block = jnp.pad(head_block, ((0, 0), (0, 0), (0, lanes - cols - 2 - experts)))
+    seg_line = jnp.broadcast_to(segment_ids.reshape(1, 1, rows), (count, 1, rows)).astype(low)
+    seg_line = jnp.pad(seg_line, ((0, 0), (0, 0), (0, lanes - rows)))
+    other_line = other_route.reshape(experts, 1, capacity).astype(low)
+    other_line = jnp.pad(other_line, ((0, 0), (0, 14), (0, lanes - capacity)))
+    head_block = jnp.concatenate([head_block, seg_line, other_line], 1)
+    chip = index // 2
+    tokens_all = gather(start_low, "fsdp")
+    arrived = all_to_all(head_block)
+
+    inner_own = inner_weight.reshape(size, 2 * ff)
+    inner_x, inner_y = swap_near(inner_own, "dp", (1, 2))
+    outer_x, outer_y = swap_near(outer_weight, "dp", (1, 2))
+    arrived, inner_x, inner_y, outer_x, outer_y = after(
+        (arrived, inner_x, inner_y, outer_x, outer_y)
+    )
+    inner_far = flip_exchange(inner_x, "dp", 2)
+    outer_far = flip_exchange(outer_y, "dp", 1)
+    segments = arrived[:, shard, :rows].reshape(length).astype(jnp.int32)
+    other_expert = arrived[:, shard + 1, :capacity].reshape(height, 1).astype(jnp.int32)
+    head_rows = arrived[:, :shard].reshape(count * shard, lanes)
+    head_near = swap_near(head_rows, "dp", (1, 2, 3))
+    head_weights = in_order([head_rows] + head_near, "dp").reshape(width, lanes)
+    cot_sent = spread_rows(slots_near, cot_low, capacity, experts)
+
+    by_head_line = by_head.reshape(shard, count * cols)
+    tokens_all, cot_sent, head_weights, by_head_line, output_own = after(
+        (tokens_all, cot_sent, head_weights, by_head_line, output_weight.T)
+    )
+    output_all = gather(output_own, ("dp", "fsdp"))
+    normed, projected = project(tokens_all, head_weights, cols, first_lane, rows)
+    cot_first = swap_near_blocks(cot_sent, (4, 6, 2))
+    firsts = segments.reshape(count, rows)
+    starts = jnp.sum(segments[None, :] < firsts[:, :1], 1) // rows
+    wholes = (jnp.sum(segments[None, :] < firsts[:, -1:], 1) + rows - 1) // rows
+    wholes = jnp.minimum(wholes, jnp.arange(count))
+    spans = jnp.stack([starts, wholes]).astype(jnp.int32)
+    seg_row, seg_col = segments.reshape(1, length), segments.reshape(length, 1)
+    mixed_head, mixed_exact, totals = attend(spans, projected, seg_row, seg_col)
+    mixed_head, cot_first, inner_far, outer_far, by_head_line = after(
+        (mixed_head, cot_first, inner_far, outer_far, by_head_line)
+    )
+    project_line = gather(by_head_line, "fsdp")
+    inner_parts = [inner_own, inner_x, inner_y, inner_far]
+    outer_parts = [outer_weight, outer_x, outer_y, outer_far]
+    mixed = all_to_all(mixed_head).reshape(count * share, rows)
+
+    middle, sent, gates = middle_part(
+        start_low, mixed, output_all, head_weights, slots, route_lines,
+        second_lane, router_lane, height,
+    )
+
+    rows_in = all_to_all(sent)
+    rows_in, cot_sent, project_line = after((rows_in, cot_sent, project_line))
+    project_all = gather(project_line, "dp")
+    cot_last = swap_near_blocks(cot_sent, (5, 7, 3, 1))
+    own_expert = jnp.stack([index, group]).astype(jnp.int32)
+    (pre_gate, pre_up, hidden, slot_gates), parts = expert_forward_pass(
+        own_expert, rows_in, inner_parts, outer_parts, head_weights, other_expert,
+        router_lane, 256, experts,
+    )
+    hidden, parts, cot_last = after((hidden, parts, cot_last))
+    part_first = swap_near_blocks(parts, (4, 6, 2, 1))
+    cot_in = [cot_sent[0], cot_last[3], cot_first[2], cot_last[2]]
+    cot_in = cot_in + [cot_first[0], cot_last[0], cot_first[1], cot_last[1]]
+    grad_pre, grad_in, grad_rows, router_part = expert_backward_pass(
+        own_expert, cot_in, parts, rows_in, slot_gates, pre_gate, pre_up, inner_parts, outer_parts,
+        head_weights, other_expert, router_lane, 256,
+    )
+    grad_rows, part_first, grad_pre, grad_in = after((grad_rows, part_first, grad_pre, grad_in))
+    grad_home = all_to_all(grad_rows)
+
+    def cut(value, k):
+        return lax.dynamic_slice_in_dim(value, jnp.bitwise_xor(group, k) * size, size, 1)
+
+    inner_terms = [contract(cut(rows_in, k), grad_pre, 0, 0).astype(low) for k in range(4)]
+    outer_term = contract(grad_in, hidden, 0, 0).astype(low)
+    half_size = size // 2
+    inner_a = [term[:half_size] for term in inner_terms]
+    inner_b = [term[half_size:] for term in inner_terms]
+    near_a, far_a = [flip_exchange(inner_a[k], "dp", 1) for k in (1, 3)]
+    near_b, far_b = [flip_exchange(inner_b[k], "dp", 2) for k in (2, 3)]
+    grad_home, outer_term, near_a, far_a, near_b, far_b, project_all = after(
+        (grad_home, outer_term, near_a, far_a, near_b, far_b, project_all)
+    )
+    passed_a = (inner_a[2].astype(f32) + far_a.astype(f32)).astype(low)
+    passed_b = (inner_b[1].astype(f32) + far_b.astype(f32)).astype(low)
+    side_a, side_b = flip_exchange(passed_a, "dp", 2), flip_exchange(passed_b, "dp", 1)
+
+    grad_middle, grad_branch, gain_part, mixed_grad = back_part(
+        middle, cot_low, grad_home, output_all, head_weights, slots, second_lane
+    )
+    mixed_grad = all_to_all(mixed_grad.reshape(count, share, rows))
+
+    branch_near = jnp.concatenate([cut(grad_branch, k) for k in range(4)], 1)
+    half_width = width // 2
+
+    def half_terms(side):
+        heads = lax.dynamic_slice_in_dim(mixed, side * half_width, half_width, 0)
+        return contract(branch_near, heads, 0, 1).astype(low)
+
+    from_core = flip_exchange(half_terms(1 - core), "fsdp", 1)
+    output_part = half_terms(core).astype(f32) + from_core.astype(f32)
+    output_part = output_part.astype(low).reshape(4, size, half_width)
+    mixed_grad, output_part, parts, side_a, side_b, outer_term = after(
+        (mixed_grad, output_part, parts, side_a, side_b, outer_term)
+    )
+    outer_sum = lax.psum_scatter(outer_term, "dp", scatter_dimension=0, tiled=True)
+    part_last = swap_near_blocks(parts, (5, 7, 3))
+    output_near = [flip_exchange(output_part[k], "dp", k) for k in (1, 2)]
+
+    grads_blocks, grads_line = attend_backward(
+        spans, projected, mixed_grad, seg_row, seg_col, mixed_exact, totals
+    )
+    grads_blocks, grads_line, output_part, output_near, part_last = after(
+        (grads_blocks, grads_line, output_part, output_near, part_last)
+    )
+    part_home = [parts[0], part_first[3], part_first[2], part_last[2]]
+    part_home = part_home + [part_first[0], part_last[0], part_first[1], part_last[1]]
+    grad_mine = all_to_all(grads_blocks).reshape(count * cols, rows)
+    extra = jnp.concatenate(
+        [router_part[router_lane : router_lane + experts], gain_part,
+         jnp.zeros((lanes - cols - experts - 1, width), f32)]
+    )
+    output_near = output_near + [flip_exchange(output_part[3], "dp", 3)]
+    own_group = group.reshape(1).astype(jnp.int32)
+    terms = weight_terms(own_group, normed, grads_line, extra, 4)
+    weight_sum = terms[0].astype(f32)
+    for k in range(1, 4):
+        weight_sum = weight_sum + flip_exchange(terms[k], "dp", k).astype(f32)
+    inner_grad = jnp.concatenate(
+        [
+            inner_a[0].astype(f32) + near_a.astype(f32) + side_a.astype(f32),
+            inner_b[0].astype(f32) + near_b.astype(f32) + side_b.astype(f32),
+        ]
+    ).reshape(size, 2, ff)
+    outer_grad = outer_sum.astype(f32).T
+    block_out = mixture(slots_near, gates, middle, part_home)
+    output_sum = output_part[0].astype(f32)
+    for near in output_near:
+        output_sum = output_sum + near.astype(f32)
+    weight_sum, output_sum = after((weight_sum.astype(low), output_sum), grad_mine)
+    weight_home = all_to_all(weight_sum.reshape(count, shard, lanes))
+    query_grad, keyval_grad, router_grad, gains = weight_grads(
+        weight_home, query_weight, key_value_weight, gain_before[:, None], share, experts
+    )
+    before_grad, middle_grad = gains[:, 0], gains[:, 1]
+    chips, pair = count // 2, 2 * shard
+    output_low = output_sum.astype(low)
+
+    def line_part(value, k):
+        at = jnp.bitwise_xor(index // 2, k) * pair
+        return lax.dynamic_slice_in_dim(value, at, pair, 0)
+
+    output_grad = line_part(output_sum, 0)
+    for k in range(1, chips):
+        output_grad = output_grad + flip_exchange(line_part(output_low, k), "fsdp", 2 * k).astype(f32)
+    own_half = lax.dynamic_slice_in_dim(output_grad, core * shard, shard, 0)
+    other_half = flip_exchange(
+        lax.dynamic_slice_in_dim(output_grad, (1 - core) * shard, shard, 0), "fsdp", 1
+    )
+    output_grad = jnp.where(
+        core == 0,
+        jnp.concatenate([own_half, other_half], 1),
+        jnp.concatenate([other_half, own_half], 1),
+    ).T
+    grad_normed = contract(grad_mine, project_all, 0, 1)
+    gain_first = head_weights[:, table_lane + first_lane]
+    _, unit_first, factor_first = normalize(start_low.astype(f32), gain_first)
+    outer_back, _ = normalize_back(grad_normed, unit_first, factor_first, gain_first)
+    tokens_grad = grad_middle + outer_back
+    return (
+        block_out[None],
+        tokens_grad[None],
+        query_grad,
+        keyval_grad,
+        output_grad,
+        router_grad,
+        before_grad,
+        middle_grad,
+        inner_grad,
+        outer_grad,
+    )
+
+
 def solution(mesh):
+    by_heads = (mesh.shape["dp"], mesh.shape["fsdp"]) == (4, KEY_VALUE_HEADS)
     in_specs = (
         P("dp", "fsdp", None),
         P("dp", "fsdp"),
@@ -467,5 +1428,5 @@
         P("fsdp", "dp"),
     )
     return jax.shard_map(
-        per_device, mesh=mesh, in_specs=in_specs, out_specs=out_specs, check_vma=False
-    )
+        per_device_heads if by_heads else per_device, mesh=mesh, in_specs=in_specs, out_specs=out_specs, check_vma=False
+    )

time: 1480 us -> 565 us (0.38)
  waiting for transfers between devices: 652 us -> 165 us
  blocking collectives: 326 us -> 64.9 us
  Pallas kernels: 0 us -> 125 us
  matrix products: 154 us -> 32.8 us
  local copies, waits for them, and re-layouts: 143 us -> 53.6 us
  other arithmetic: 60.7 us -> 22.1 us
  loops' own time: 29.2 us -> 0 us
    reduce_scatter x5 -> x1, waiting for transfers between devices: 396 us -> 0.01 us  [per_device_heads(): lax.psum_scatter(outer_term, 'dp', scatter_dimension=0, tiled=True)]
    all_to_all x4 -> x5, waiting for transfers between devices: 149 us -> 13.3 us  [all_to_all(): lax.all_to_all(blocks, 'fsdp', split_axis=0, concat_axis=0, tiled=True)]
    pallas_call x0 -> x11, Pallas kernels: none -> 125 us  [the longest x1 27.9 us: expert_backward_pass(): pl.pallas_call(functools.partial(expert_back_kernel, router_lane, blocks)...]
    dot_general x41 -> x9, matrix products: 152 us -> 32.8 us  [the longest x8 32.5 us: contract(): lax.dot_general(left, right, (((left_axis,), (right_axis,)), ((), ())), p...]
    all_gather x2 -> x0, blocking collectives: 94.5 us -> none  [the longest x1 83.9 us: layer_weights(): lax.all_gather(router_weight, ('dp', 'fsdp'), axis=0, tiled=True)]
    all_to_all x2, blocking collectives: 153 us -> 64.9 us  [all_to_all(): lax.all_to_all(blocks, 'fsdp', split_axis=0, concat_axis=0, tiled=True)]
    ppermute x0 -> x40, waiting for transfers between devices: none -> 82.6 us  [flip_exchange(): return lax.ppermute(block, axis, [(i, i ^ flip) for i in range(count)])]
    unnamed x2 -> x0, blocking collectives: 79.2 us -> none
  transfers between devices with their start and end apart: 17 -> 50, of which waited for: 9 -> 16; matrix products, arithmetic and copies ran while one was open for 16% -> 13% of each run, Pallas kernels for 0% -> 21%
where the time goes in v2:
time: 565 us; the launch traced here: 556 us
  waiting for transfers between devices  165 us (29%)
  Pallas kernels  125 us (22%)
  starting transfers between devices  77.5 us (14%)
  blocking collectives  64.9 us (11%)
  local copies, waits for them, and re-layouts  53.6 us (9%)
  matrix products  32.8 us (6%)
  other arithmetic  22.1 us (4%)
  between operations  15.1 us (3%)
    ppermute x40, waiting for transfers between devices, flip_exchange(): return lax.ppermute(block, axis, [(i, i ^ flip) for i in range(count)])  82.6 us
    all_gather x4, waiting for transfers between devices, gather(): return lax.all_gather(block, axis, axis=0, tiled=True)  67.3 us
    all_to_all x2, blocking collectives, all_to_all(): lax.all_to_all(blocks, 'fsdp', split_axis=0, concat_axis=0, tiled=True)  64.9 us
    ppermute x40, starting transfers between devices, flip_exchange(): return lax.ppermute(block, axis, [(i, i ^ flip) for i in range(count)])  42.1 us
    all_to_all x5, starting transfers between devices, all_to_all(): lax.all_to_all(blocks, 'fsdp', split_axis=0, concat_axis=0, tiled=True)  35 us
    unnamed x155, local copies, waits for them, and re-layouts  33.7 us
    dot_general x8, matrix products, contract(): lax.dot_general(left, right, (((left_axis,), (right_axis,)), ((), ())), p...  32.5 us
    pallas_call x1, Pallas kernels, expert_backward_pass(): pl.pallas_call(functools.partial(expert_back_kernel, router_lane, blocks)...  27.9 us
  transfers between devices with their start and end apart: 50, of which 16 were waited for; matrix products, arithmetic and copies ran while one was open for 13% of the time, Pallas kernels for 21%

profile of v2, /device:TPU:1, one launch (start us, length us, event | category | flops | bytes accessed | tf_op | source)
XLA Modules:
  0.0 555.6 jit_solution(422366687300144468)
XLA Ops:
  10.0 2.1 collective-permute-start
  15.9 27.9 %all_to_all.49 = bf16[8,64,384]{2,1,0:T(8,128)(2,1)S(1)} all-to-all(bf16[8,64,384]{2,1,0:T(8,128)(2,1)S(1)} %copy.74), channel_id=1, replica_groups=mesh['dp'=4,'fsdp'=8] {'fsdp'}, dimensions={0} | all-to-all | bytes 786432 | tf_op jit(solution)/shard_map/all_to_all | solution.py:1143
  43.8 19.4 %collective-permute-done.2.refs_9_.refs_29_ = bf16[1024,384]{1,0:T(8,128)(2,1)} collective-permute-done((bf16[1024,384]{1,0:T(8,128)(2,1)S(1)}, bf16[1024,384]{1,0:T(8,128)(2,1)}, u32[]{:S(2)}, u32[]{:S(2)}) %collective-permute-start.2) | collective-permute-done | bytes 786464 | tf_op jit(solution)/shard_map/ppermute | solution.py:1120
  73.2 7.2 %collective-permute-done.5 = bf16[384,384]{1,0:T(8,128)(2,1)S(1)} collective-permute-done((bf16[384,384]{1,0:T(8,128)(2,1)S(1)}, bf16[384,384]{1,0:T(8,128)(2,1)S(1)}, u32[]{:S(2)}, u32[]{:S(2)}) %collective-permute-start.5) | collective-permute-done | bytes 294944 | tf_op jit(solution)/shard_map/ppermute | solution.py:1120
  80.9 4.3 all-gather.12.cloned.1.call-done
  92.0 9.1 %project.1 = (bf16[2048,1536]{1,0:T(8,128)(2,1)S(1)}, bf16[8,320,256]{2,1,0:T(8,128)(2,1)S(1)}) custom-call(bf16[2048,1536]{1,0:T(8,128)(2,1)} %bitcast.141, bf16[1536,384]{1,0:T(8,128)(2,1)S(1)} %bitcast.112, bf16[1536,384]{1,0:T(8,128)(2,1)S(1)} %bitcast.113), custom_call_target="tpu_custom_call" | custom-call | tf_op jit(solution)/shard_map/project/pallas_call | solution.py:483
  101.1 2.6 copy-done.6
  103.8 21.4 %attend.1 = (bf16[8,192,256]{2,1,0:T(8,128)(2,1)S(1)}, f32[8,192,256]{2,1,0:T(8,128)S(1)}, f32[8,8,256]{2,1,0:T(8,128)S(1)}) custom-call(s32[2,8]{1,0:T(2,128)S(1)} %pad_add_fusion.spans, bf16[8,320,256]{2,1,0:T(8,128)(2,1)S(1)} %get-tuple-element.140.q_ref.heads_ref, bf16[8,320,256]{2,1,0:T(8,128)(2,1)S(1)} %get-tuple-element.140.q_ref.heads_ref, ...), custom_call_target="tpu_custom_call" | custom-call | tf_op jit(solution)/shard_map/attend/pallas_call | solution.py:567
  127.0 37.0 %all_to_all.50 = bf16[8,192,256]{2,1,0:T(8,128)(2,1)} all-to-all(bf16[8,192,256]{2,1,0:T(8,128)(2,1)S(1)} %get-tuple-element.148), channel_id=1, replica_groups=mesh['dp'=4,'fsdp'=8] {'fsdp'}, dimensions={0} | all-to-all | bytes 1572864 | tf_op jit(solution)/shard_map/all_to_all | solution.py:1143
  164.0 3.9 all-gather.6.cloned.1.call-done.weight_ref
  167.9 2.3 copy-done.2
  171.3 2.6 middle.1
  176.5 4.5 all-to-all-start.2
  182.1 59.1 %all-gather.8.cloned.1.call-done = bf16[384,2560]{1,0:T(8,128)(2,1)} async-done(((bf16[48,2560]{1,0:T(8,128)(2,1)}), bf16[384,2560]{1,0:T(8,128)(2,1)}) %all-gather.8.cloned.1.call-update) | async-done | bytes 1966096 | tf_op jit(solution)/shard_map/all_gather | solution.py:1147
  241.2 9.6 %all-to-all-done.2 = bf16[8,96,1536]{2,1,0:T(8,128)(2,1)} async-done(((bf16[8,96,1536]{2,1,0:T(8,128)(2,1)}), bf16[8,96,1536]{2,1,0:T(8,128)(2,1)}, u32[]{:S(2)}, u32[]{:S(2)}) %all-to-all-start.2) | async-done | bytes 2359328 | tf_op jit(solution)/shard_map/all_to_all | solution.py:1143
  257.0 18.0 %expert.1 = (f32[768,1024]{1,0:T(8,128)}, f32[768,1024]{1,0:T(8,128)}, bf16[768,1024]{1,0:T(8,128)(2,1)}, f32[768,128]{1,0:T(8,128)}, bf16[96,1536]{1,0:T(8,128)...) custom-call(s32[2]{0:T(128)} %pad_add_fusion.1.own_ref, ...), custom_call_target="tpu_custom_call" | custom-call | tf_op jit(solution)/shard_map/expert/pallas_call | solution.py:827
  275.0 4.9 collective-permute-start.16
  282.3 27.9 %expert_backward.1 = (bf16[768,2048]{1,0:T(8,128)(2,1)}, bf16[768,1536]{1,0:T(8,128)(2,1)}, bf16[768,1536]{1,0:T(8,128)(2,1)}, f32[128,1536]{1,0:T(8,128)}) custom-call(s32[2]{0:T(128)} %pad_add_fusion.1.own_ref, bf16[96,1536]{1,0:T(8,128)(2,1)} %copy-done.42, bf16[96,1536]{1,0:T(8,128)(2,1)} %collective-permute-done.15.refs_1_, ...), custom_call_target="tpu_custom_call" | custom-call | tf_op jit(solution)/shard_map/expert_backward/pallas_call | solution.py:925
  313.1 15.5 %all-to-all-start.3 = ((bf16[8,96,1536]{2,1,0:T(8,128)(2,1)}), bf16[8,96,1536]{2,1,0:T(8,128)(2,1)}, u32[]{:S(2)}, u32[]{:S(2)}) async-start(bf16[8,96,1536]{2,1,0:T(8,128)(2,1)} %bitcast.145), calls=%async_computation.3 | async-start | bytes 4718592 | tf_op jit(solution)/shard_map/all_to_all | solution.py:1143
  328.6 3.7 convolution_convert_fusion.6
  334.1 2.5 convolution_convert_fusion.5
  338.9 2.5 convolution_convert_fusion.4
  345.0 6.5 %convolution_convert_fusion = bf16[1536,1024]{1,0:T(8,128)(2,1)} fusion(bf16[768,1536]{1,0:T(8,128)(2,1)} %get-tuple-element.200, bf16[768,1024]{1,0:T(8,128)(2,1)} %get-tuple-element.201), kind=kOutput, calls=%fused_computation.1 | convolution fusion | flops 2417491968 | bytes 7077888 | tf_op jit(solution)/shard_map/dot_general | solution.py:447
  353.1 16.9 %collective-permute-done.21 = bf16[192,2048]{1,0:T(8,128)(2,1)} collective-permute-done((bf16[192,2048]{1,0:T(8,128)(2,1)}, bf16[192,2048]{1,0:T(8,128)(2,1)}, u32[]{:S(2)}, u32[]{:S(2)}) %collective-permute-start.21) | collective-permute-done | bytes 786464 | tf_op jit(solution)/shard_map/ppermute | solution.py:1120
  369.9 9.2 %collective-permute-done.23 = bf16[192,2048]{1,0:T(8,128)(2,1)} collective-permute-done((bf16[192,2048]{1,0:T(8,128)(2,1)}, bf16[192,2048]{1,0:T(8,128)(2,1)}, u32[]{:S(2)}, u32[]{:S(2)}) %collective-permute-start.23) | collective-permute-done | bytes 786464 | tf_op jit(solution)/shard_map/ppermute | solution.py:1120
  379.1 3.8 all-to-all-done.3
  384.0 6.3 %back.1 = (f32[256,1536]{1,0:T(8,128)S(1)}, bf16[256,1536]{1,0:T(8,128)(2,1)S(1)}, f32[1,1536]{1,0:T(1,128)S(1)}, bf16[1536,256]{1,0:T(8,128)(2,1)S(1)}) custom-call(f32[256,1536]{1,0:T(8,128)} %copy-done.7, bf16[256,1536]{1,0:T(8,128)(2,1)S(1)} %bitcast.123, bf16[768,1536]{1,0:T(8,128)(2,1)} %bitcast.33.home_ref, ...), custom_call_target="tpu_custom_call" | custom-call | tf_op jit(solution)/shard_map/back/pallas_call | solution.py:992
  392.1 2.3 convolution_convert_fusion.1
  395.0 4.2 all-to-all-start.4
  399.2 2.6 add_convert_fusion.2
  402.8 2.3 add_convert_fusion.1
  405.4 4.3 add_convert_fusion
  409.7 11.6 %collective-permute-done.25 = bf16[192,2048]{1,0:T(8,128)(2,1)} collective-permute-done((bf16[192,2048]{1,0:T(8,128)(2,1)}, bf16[192,2048]{1,0:T(8,128)(2,1)}, u32[]{:S(2)}, u32[]{:S(2)}) %collective-permute-start.25) | collective-permute-done | bytes 786464 | tf_op jit(solution)/shard_map/ppermute | solution.py:1120
  421.3 2.9 collective-permute-done.26
  424.5 2.3 slice_bitcast_fusion.1
  429.2 3.9 collective-permute-start.29
  434.0 4.6 convolution_convert_fusion.3
  438.7 26.5 %attend_backward.1 = (bf16[8,320,256]{2,1,0:T(8,128)(2,1)S(1)}, bf16[320,2048]{1,0:T(8,128)(2,1)S(1)}) custom-call(s32[2,8]{1,0:T(2,128)S(1)} %copy-done.49, bf16[8,320,256]{2,1,0:T(8,128)(2,1)S(1)} %get-tuple-element.140.q_ref.heads_ref, bf16[8,192,256]{2,1,0:T(8,128)(2,1)} %all-to-all-done.4.g_ref, ...), custom_call_target="tpu_custom_call" | custom-call | tf_op jit(solution)/shard_map/attend_backward/pallas_call | solution.py:654
  468.5 5.2 all-to-all-start.5
  473.8 3.4 convert_add_fusion.1
  480.8 4.5 weight_terms.1
  491.1 5.7 %reshape.293 = f32[384,2,1024]{2,1,0:T(2,128)} reshape(f32[384,2048]{1,0:T(8,128)} %pad_maximum_fusion) | data formatting | bytes 6291456 | tf_op jit(solution)/shard_map/reshape | solution.py:1352
  501.6 6.0 %mixture.1 = bf16[256,1536]{1,0:T(8,128)(2,1)} custom-call(s32[2,256]{1,0:T(2,128)S(1)} %copy-done.47, f32[2,256]{1,0:T(2,128)S(1)} %get-tuple-element.150.gates_ref, f32[256,1536]{1,0:T(8,128)S(1)} %copy-done.8, bf16[96,1536]{1,0:T(8,128)(2,1)S(1)} %copy-done.22, bf16[96,1536]{1,0:T(8,128)(2,1)S(1)} %copy-done.35, bf16[96,1536]{1,0:T(8,128)(2,1)S(1)} %copy-done.33, ...), custom_call_target="tpu_custom_call" | custom-call | tf_op jit(solution)/shard_map/mixture/pallas_call | solution.py:1067
  512.2 5.6 %all-to-all-start.6 = ((bf16[8,48,384]{2,1,0:T(8,128)(2,1)}), bf16[8,48,384]{2,1,0:T(8,128)(2,1)S(1)}, u32[]{:S(2)}, u32[]{:S(2)}) async-start(bf16[8,48,384]{2,1,0:T(8,128)(2,1)} %bitcast.47), calls=%async_computation.6 | async-start | bytes 589824 | tf_op jit(solution)/shard_map/all_to_all | solution.py:1143
  518.0 3.3 collective-permute-start.38
  521.6 6.1 %fusion.2 = (f32[256]{0:T(256)S(1)}, f32[256,1536]{1,0:T(8,128)S(1)}) fusion(f32[256]{0:T(256)S(1)} %add_rsqrt_fusion, bf16[1,256,1536]{2,1,0:T(8,128)(2,1)S(1)} %copy-done.3, f32[1536]{0:T(1024)S(1)} %convert_reduce_fusion, bf16[2560,256]{1,0:T(8,128)(2,1)} %bitcast.39, bf16[1536,2560]{1,0:T(8,128)(2,1)} %all-gather.10.cloned.1.call-done), kind=kOutput, calls=%fused_computation.14 | convolution fusion | flops 2015231744 | bytes 11542528 | tf_op jit(solution)/shard_map/dot_general | solution.py:447
  527.7 2.3 collective-permute-done.38
  530.0 10.1 %collective-permute-done.37 = bf16[96,768]{1,0:T(8,128)(2,1)S(1)} collective-permute-done((bf16[96,768]{1,0:T(8,128)(2,1)S(1)}, bf16[96,768]{1,0:T(8,128)(2,1)S(1)}, u32[]{:S(2)}, u32[]{:S(2)}) %collective-permute-start.37) | collective-permute-done | bytes 147488 | tf_op jit(solution)/shard_map/ppermute | solution.py:1120
  (306 shorter events, 90.2 us)
Async XLA Ops:
  7.2 78.0 %all-gather.12.cloned.1.call-start = ((), (), s32[]{:S(2)}) async-start(), calls=%async_computation.12 | async-start | bytes 7077888 | tf_op jit(solution)/shard_map/all_gather | solution.py:1147
  7.9 160.0 %all-gather.6.cloned.1.call-start = ((), (), s32[]{:S(2)}) async-start(), calls=%async_computation.8 | async-start | bytes 4866048 | tf_op jit(solution)/shard_map/all_gather | solution.py:1147
  10.0 54.0 %collective-permute-start = (bf16[384,2048]{1,0:T(8,128)(2,1)S(1)}, bf16[384,2048]{1,0:T(8,128)(2,1)}, u32[]{:S(2)}, u32[]{:S(2)}) collective-permute-start(bf16[384,2048]{1,0:T(8,128)(2,1)S(1)} %bitcast.135), channel_id=1, source_target_pairs={{0,8},{8,0},{16,24},{24,16},{1,9},{9,1},{17,25},{25,17},{2,10},{10... | collective-permute-start | bytes 4718600 | tf_op jit(solution)/shard_map/ppermute | solution.py:1120
  12.1 51.9 %collective-permute-start.1 = (bf16[384,2048]{1,0:T(8,128)(2,1)S(1)}, bf16[384,2048]{1,0:T(8,128)(2,1)}, u32[]{:S(2)}, u32[]{:S(2)}) collective-permute-start(bf16[384,2048]{1,0:T(8,128)(2,1)S(1)} %bitcast.136), channel_id=1, source_target_pairs={{0,16},{8,24},{16,0},{24,8},{1,17},{9,25},{17,1},{25,9},{2,18},{10... | collective-permute-start | bytes 4718600 | tf_op jit(solution)/shard_map/ppermute | solution.py:1120
  13.3 49.8 %collective-permute-start.2 = (bf16[1024,384]{1,0:T(8,128)(2,1)S(1)}, bf16[1024,384]{1,0:T(8,128)(2,1)}, u32[]{:S(2)}, u32[]{:S(2)}) collective-permute-start(bf16[1024,384]{1,0:T(8,128)(2,1)S(1)} %copy-done.63), channel_id=1, source_target_pairs={{0,8},{8,0},{16,24},{24,16},{1,9},{9,1},{17,25},{25,17},{2,10},{10... | collective-permute-start | bytes 2359304 | tf_op jit(solution)/shard_map/ppermute | solution.py:1120
  13.6 50.4 %collective-permute-start.3 = (bf16[1024,384]{1,0:T(8,128)(2,1)S(1)}, bf16[1024,384]{1,0:T(8,128)(2,1)}, u32[]{:S(2)}, u32[]{:S(2)}) collective-permute-start(bf16[1024,384]{1,0:T(8,128)(2,1)S(1)} %copy-done.63), channel_id=1, source_target_pairs={{0,16},{8,24},{16,0},{24,8},{1,17},{9,25},{17,1},{25,9},{2,18},{10... | collective-permute-start | bytes 2359304 | tf_op jit(solution)/shard_map/ppermute | solution.py:1120
  65.4 15.0 %collective-permute-start.5 = (bf16[384,384]{1,0:T(8,128)(2,1)S(1)}, bf16[384,384]{1,0:T(8,128)(2,1)S(1)}, u32[]{:S(2)}, u32[]{:S(2)}) collective-permute-start(bf16[384,384]{1,0:T(8,128)(2,1)S(1)} %bitcast.148), channel_id=1, source_target_pairs={{0,16},{8,24},{16,0},{24,8},{1,17},{9,25},{17,1},{25,9},{2,18},{10... | collective-permute-start | bytes 884744 | tf_op jit(solution)/shard_map/ppermute | solution.py:1120
  65.7 14.7 %collective-permute-start.4 = (bf16[384,384]{1,0:T(8,128)(2,1)S(1)}, bf16[384,384]{1,0:T(8,128)(2,1)S(1)}, u32[]{:S(2)}, u32[]{:S(2)}) collective-permute-start(bf16[384,384]{1,0:T(8,128)(2,1)S(1)} %bitcast.149), channel_id=1, source_target_pairs={{0,8},{8,0},{16,24},{24,16},{1,9},{9,1},{17,25},{25,17},{2,10},{10... | collective-permute-start | bytes 884744 | tf_op jit(solution)/shard_map/ppermute | solution.py:1120
  85.2 41.7 %collective-permute-start.10 = (bf16[384,2048]{1,0:T(8,128)(2,1)}, bf16[384,2048]{1,0:T(8,128)(2,1)}, u32[]{:S(2)}, u32[]{:S(2)}) collective-permute-start(bf16[384,2048]{1,0:T(8,128)(2,1)} %collective-permute-done.refs_1_.refs_5_.refs_21_.refs_25_), channel_id=1, source_target_pairs={{0,16},{8,24},{16,0},{24,8},{1,17},{9,25},{17,1},{25,9},{2,18},{10... | collective-permute-start | bytes 4718600 | tf_op jit(solution)/shard_map/ppermute | solution.py:1120
  86.5 40.5 %collective-permute-start.11 = (bf16[1024,384]{1,0:T(8,128)(2,1)}, bf16[1024,384]{1,0:T(8,128)(2,1)}, u32[]{:S(2)}, u32[]{:S(2)}) collective-permute-start(bf16[1024,384]{1,0:T(8,128)(2,1)} %collective-permute-done.3.refs_10_.refs_30_), channel_id=1, source_target_pairs={{0,8},{8,0},{16,24},{24,16},{1,9},{9,1},{17,25},{25,17},{2,10},{10... | collective-permute-start | bytes 2359304 | tf_op jit(solution)/shard_map/ppermute | solution.py:1120
  89.2 37.7 %collective-permute-start.7 = (bf16[96,1536]{1,0:T(8,128)(2,1)}, bf16[96,1536]{1,0:T(8,128)(2,1)}, u32[]{:S(2)}, u32[]{:S(2)}) collective-permute-start(bf16[96,1536]{1,0:T(8,128)(2,1)} %get-tuple-element.142), channel_id=1, source_target_pairs={{0,4},{1,5},{2,6},{3,7},{4,0},{5,1},{6,2},{7,3},{8,12},{9,13},{10,... | collective-permute-start | bytes 884744 | tf_op jit(solution)/shard_map/ppermute | solution.py:1120
  89.3 37.6 %collective-permute-start.8 = (bf16[96,1536]{1,0:T(8,128)(2,1)}, bf16[96,1536]{1,0:T(8,128)(2,1)}, u32[]{:S(2)}, u32[]{:S(2)}) collective-permute-start(bf16[96,1536]{1,0:T(8,128)(2,1)} %get-tuple-element.143), channel_id=1, source_target_pairs={{0,6},{1,7},{2,4},{3,5},{4,2},{5,3},{6,0},{7,1},{8,14},{9,15},{10,... | collective-permute-start | bytes 884744 | tf_op jit(solution)/shard_map/ppermute | solution.py:1120
  90.0 36.9 %collective-permute-start.9 = (bf16[96,1536]{1,0:T(8,128)(2,1)}, bf16[96,1536]{1,0:T(8,128)(2,1)}, u32[]{:S(2)}, u32[]{:S(2)}) collective-permute-start(bf16[96,1536]{1,0:T(8,128)(2,1)} %get-tuple-element.144), channel_id=1, source_target_pairs={{0,2},{1,3},{2,0},{3,1},{4,6},{5,7},{6,4},{7,5},{8,10},{9,11},{10,... | collective-permute-start | bytes 884744 | tf_op jit(solution)/shard_map/ppermute | solution.py:1120
  176.5 74.3 %all-to-all-start.2 = ((bf16[8,96,1536]{2,1,0:T(8,128)(2,1)}), bf16[8,96,1536]{2,1,0:T(8,128)(2,1)}, u32[]{:S(2)}, u32[]{:S(2)}) async-start(bf16[8,96,1536]{2,1,0:T(8,128)(2,1)} %bitcast.127), calls=%async_computation.2 | async-start | bytes 4718592 | tf_op jit(solution)/shard_map/all_to_all | solution.py:1143
  181.1 60.1 %all-gather.8.cloned.1.call-start = ((), (), s32[]{:S(2)}) async-start(), calls=%async_computation.9 | async-start | bytes 2211840 | tf_op jit(solution)/shard_map/all_gather | solution.py:1147
  181.8 201.1 %all-gather.10.cloned.1.call-start = ((), (), s32[]{:S(2)}) async-start(), calls=%async_computation.10 | async-start | bytes 9830400 | tf_op jit(solution)/shard_map/all_gather | solution.py:1147
  250.8 24.2 %collective-permute-start.12 = (bf16[96,1536]{1,0:T(8,128)(2,1)S(1)}, bf16[96,1536]{1,0:T(8,128)(2,1)}, u32[]{:S(2)}, u32[]{:S(2)}) collective-permute-start(bf16[96,1536]{1,0:T(8,128)(2,1)S(1)} %copy-done.57), channel_id=1, source_target_pairs={{0,5},{1,4},{2,7},{3,6},{4,1},{5,0},{6,3},{7,2},{8,13},{9,12},{10,... | collective-permute-start | bytes 884744 | tf_op jit(solution)/shard_map/ppermute | solution.py:1120
  250.9 24.1 %collective-permute-start.13 = (bf16[96,1536]{1,0:T(8,128)(2,1)S(1)}, bf16[96,1536]{1,0:T(8,128)(2,1)}, u32[]{:S(2)}, u32[]{:S(2)}) collective-permute-start(bf16[96,1536]{1,0:T(8,128)(2,1)S(1)} %copy-done.55), channel_id=1, source_target_pairs={{0,7},{1,6},{2,5},{3,4},{4,3},{5,2},{6,1},{7,0},{8,15},{9,14},{10,... | collective-permute-start | bytes 884744 | tf_op jit(solution)/shard_map/ppermute | solution.py:1120
  252.7 22.3 %collective-permute-start.14 = (bf16[96,1536]{1,0:T(8,128)(2,1)S(1)}, bf16[96,1536]{1,0:T(8,128)(2,1)}, u32[]{:S(2)}, u32[]{:S(2)}) collective-permute-start(bf16[96,1536]{1,0:T(8,128)(2,1)S(1)} %copy-done.53), channel_id=1, source_target_pairs={{0,3},{1,2},{2,1},{3,0},{4,7},{5,6},{6,5},{7,4},{8,11},{9,10},{10,... | collective-permute-start | bytes 884744 | tf_op jit(solution)/shard_map/ppermute | solution.py:1120
  254.6 20.4 %collective-permute-start.15 = (bf16[96,1536]{1,0:T(8,128)(2,1)S(1)}, bf16[96,1536]{1,0:T(8,128)(2,1)}, u32[]{:S(2)}, u32[]{:S(2)}) collective-permute-start(bf16[96,1536]{1,0:T(8,128)(2,1)S(1)} %copy-done.51), channel_id=1, source_target_pairs={{0,1},{1,0},{2,3},{3,2},{4,5},{5,4},{6,7},{7,6},{8,9},{9,8},{10,11... | collective-permute-start | bytes 884744 | tf_op jit(solution)/shard_map/ppermute | solution.py:1120
  275.0 35.1 %collective-permute-start.16 = (bf16[96,1536]{1,0:T(8,128)(2,1)}, bf16[96,1536]{1,0:T(8,128)(2,1)S(1)}, u32[]{:S(2)}, u32[]{:S(2)}) collective-permute-start(bf16[96,1536]{1,0:T(8,128)(2,1)} %get-tuple-element.189.refs_12_), channel_id=1, source_target_pairs={{0,4},{1,5},{2,6},{3,7},{4,0},{5,1},{6,2},{7,3},{8,12},{9,13},{10,... | collective-permute-start | bytes 884744 | tf_op jit(solution)/shard_map/ppermute | solution.py:1120
  280.0 30.9 %collective-permute-start.17 = (bf16[96,1536]{1,0:T(8,128)(2,1)}, bf16[96,1536]{1,0:T(8,128)(2,1)S(1)}, u32[]{:S(2)}, u32[]{:S(2)}) collective-permute-start(bf16[96,1536]{1,0:T(8,128)(2,1)} %get-tuple-element.191.refs_14_), channel_id=1, source_target_pairs={{0,6},{1,7},{2,4},{3,5},{4,2},{5,3},{6,0},{7,1},{8,14},{9,15},{10,... | collective-permute-start | bytes 884744 | tf_op jit(solution)/shard_map/ppermute | solution.py:1120
  281.3 30.3 %collective-permute-start.18 = (bf16[96,1536]{1,0:T(8,128)(2,1)}, bf16[96,1536]{1,0:T(8,128)(2,1)S(1)}, u32[]{:S(2)}, u32[]{:S(2)}) collective-permute-start(bf16[96,1536]{1,0:T(8,128)(2,1)} %get-tuple-element.187.refs_10_), channel_id=1, source_target_pairs={{0,2},{1,3},{2,0},{3,1},{4,6},{5,7},{6,4},{7,5},{8,10},{9,11},{10,... | collective-permute-start | bytes 884744 | tf_op jit(solution)/shard_map/ppermute | solution.py:1120
  281.3 31.0 %collective-permute-start.19 = (bf16[96,1536]{1,0:T(8,128)(2,1)}, bf16[96,1536]{1,0:T(8,128)(2,1)S(1)}, u32[]{:S(2)}, u32[]{:S(2)}) collective-permute-start(bf16[96,1536]{1,0:T(8,128)(2,1)} %get-tuple-element.186.refs_9_), channel_id=1, source_target_pairs={{0,1},{1,0},{2,3},{3,2},{4,5},{5,4},{6,7},{7,6},{8,9},{9,8},{10,11... | collective-permute-start | bytes 884744 | tf_op jit(solution)/shard_map/ppermute | solution.py:1120
  313.1 69.8 %all-to-all-start.3 = ((bf16[8,96,1536]{2,1,0:T(8,128)(2,1)}), bf16[8,96,1536]{2,1,0:T(8,128)(2,1)}, u32[]{:S(2)}, u32[]{:S(2)}) async-start(bf16[8,96,1536]{2,1,0:T(8,128)(2,1)} %bitcast.145), calls=%async_computation.3 | async-start | bytes 4718592 | tf_op jit(solution)/shard_map/all_to_all | solution.py:1143
  333.6 19.4 %collective-permute-start.20 = (bf16[192,2048]{1,0:T(8,128)(2,1)}, bf16[192,2048]{1,0:T(8,128)(2,1)}, u32[]{:S(2)}, u32[]{:S(2)}) collective-permute-start(bf16[192,2048]{1,0:T(8,128)(2,1)} %slice.130), channel_id=1, source_target_pairs={{0,8},{8,0},{16,24},{24,16},{1,9},{9,1},{17,25},{25,17},{2,10},{10... | collective-permute-start | bytes 2359304 | tf_op jit(solution)/shard_map/ppermute | solution.py:1120
  337.9 32.0 %collective-permute-start.21 = (bf16[192,2048]{1,0:T(8,128)(2,1)}, bf16[192,2048]{1,0:T(8,128)(2,1)}, u32[]{:S(2)}, u32[]{:S(2)}) collective-permute-start(bf16[192,2048]{1,0:T(8,128)(2,1)} %get-tuple-element.309), channel_id=1, source_target_pairs={{0,8},{8,0},{16,24},{24,16},{1,9},{9,1},{17,25},{25,17},{2,10},{10... | collective-permute-start | bytes 2359304 | tf_op jit(solution)/shard_map/ppermute | solution.py:1120
  343.5 26.4 %collective-permute-start.22 = (bf16[192,2048]{1,0:T(8,128)(2,1)}, bf16[192,2048]{1,0:T(8,128)(2,1)}, u32[]{:S(2)}, u32[]{:S(2)}) collective-permute-start(bf16[192,2048]{1,0:T(8,128)(2,1)} %slice.132), channel_id=1, source_target_pairs={{0,16},{8,24},{16,0},{24,8},{1,17},{9,25},{17,1},{25,9},{2,18},{10... | collective-permute-start | bytes 2359304 | tf_op jit(solution)/shard_map/ppermute | solution.py:1120
  344.4 34.7 %collective-permute-start.23 = (bf16[192,2048]{1,0:T(8,128)(2,1)}, bf16[192,2048]{1,0:T(8,128)(2,1)}, u32[]{:S(2)}, u32[]{:S(2)}) collective-permute-start(bf16[192,2048]{1,0:T(8,128)(2,1)} %get-tuple-element.308), channel_id=1, source_target_pairs={{0,16},{8,24},{16,0},{24,8},{1,17},{9,25},{17,1},{25,9},{2,18},{10... | collective-permute-start | bytes 2359304 | tf_op jit(solution)/shard_map/ppermute | solution.py:1120
  394.4 11.1 %collective-permute-start.24 = (bf16[1536,768]{1,0:T(8,128)(2,1)}, bf16[1536,768]{1,0:T(8,128)(2,1)}, u32[]{:S(2)}, u32[]{:S(2)}) collective-permute-start(bf16[1536,768]{1,0:T(8,128)(2,1)} %convolution_convert_fusion.1), channel_id=1, source_target_pairs={{0,1},{1,0},{2,3},{3,2},{4,5},{5,4},{6,7},{7,6},{8,9},{9,8},{10,11... | collective-permute-start | bytes 7077896 | tf_op jit(solution)/shard_map/ppermute | solution.py:1120
  395.0 29.2 %all-to-all-start.4 = ((bf16[8,192,256]{2,1,0:T(8,128)(2,1)}), bf16[8,192,256]{2,1,0:T(8,128)(2,1)}, u32[]{:S(2)}, u32[]{:S(2)}) async-start(bf16[8,192,256]{2,1,0:T(8,128)(2,1)} %bitcast.128), calls=%async_computation.4 | async-start | bytes 1572864 | tf_op jit(solution)/shard_map/all_to_all | solution.py:1143
  399.2 146.6 %reduce-scatter.2.cloned.1.call-start = ((), (), s32[]{:S(2)}) async-start(), calls=%async_computation.11 | async-start | bytes 3932160 | tf_op jit(solution)/shard_map/reduce_scatter | solution.py:1324
  401.9 19.4 %collective-permute-start.25 = (bf16[192,2048]{1,0:T(8,128)(2,1)}, bf16[192,2048]{1,0:T(8,128)(2,1)}, u32[]{:S(2)}, u32[]{:S(2)}) collective-permute-start(bf16[192,2048]{1,0:T(8,128)(2,1)} %add_convert_fusion.2), channel_id=1, source_target_pairs={{0,16},{8,24},{16,0},{24,8},{1,17},{9,25},{17,1},{25,9},{2,18},{10... | collective-permute-start | bytes 2359304 | tf_op jit(solution)/shard_map/ppermute | solution.py:1120
  405.1 19.1 %collective-permute-start.26 = (bf16[192,2048]{1,0:T(8,128)(2,1)}, bf16[192,2048]{1,0:T(8,128)(2,1)}, u32[]{:S(2)}, u32[]{:S(2)}) collective-permute-start(bf16[192,2048]{1,0:T(8,128)(2,1)} %add_convert_fusion.1), channel_id=1, source_target_pairs={{0,8},{8,0},{16,24},{24,16},{1,9},{9,1},{17,25},{25,17},{2,10},{10... | collective-permute-start | bytes 2359304 | tf_op jit(solution)/shard_map/ppermute | solution.py:1120
  426.8 41.7 %collective-permute-start.27 = (bf16[384,768]{1,0:T(8,128)(2,1)}, bf16[384,768]{1,0:T(8,128)(2,1)}, u32[]{:S(2)}, u32[]{:S(2)}) collective-permute-start(bf16[384,768]{1,0:T(8,128)(2,1)} %get-tuple-element.305), channel_id=1, source_target_pairs={{0,8},{8,0},{16,24},{24,16},{1,9},{9,1},{17,25},{25,17},{2,10},{10... | collective-permute-start | bytes 1769480 | tf_op jit(solution)/shard_map/ppermute | solution.py:1120
  427.1 41.4 %collective-permute-start.28 = (bf16[384,768]{1,0:T(8,128)(2,1)}, bf16[384,768]{1,0:T(8,128)(2,1)}, u32[]{:S(2)}, u32[]{:S(2)}) collective-permute-start(bf16[384,768]{1,0:T(8,128)(2,1)} %get-tuple-element.304), channel_id=1, source_target_pairs={{0,16},{8,24},{16,0},{24,8},{1,17},{9,25},{17,1},{25,9},{2,18},{10... | collective-permute-start | bytes 1769480 | tf_op jit(solution)/shard_map/ppermute | solution.py:1120
  429.2 37.2 %collective-permute-start.29 = (bf16[96,1536]{1,0:T(8,128)(2,1)}, bf16[96,1536]{1,0:T(8,128)(2,1)S(1)}, u32[]{:S(2)}, u32[]{:S(2)}) collective-permute-start(bf16[96,1536]{1,0:T(8,128)(2,1)} %get-tuple-element.219.refs_13_), channel_id=1, source_target_pairs={{0,5},{1,4},{2,7},{3,6},{4,1},{5,0},{6,3},{7,2},{8,13},{9,12},{10,... | collective-permute-start | bytes 884744 | tf_op jit(solution)/shard_map/ppermute | solution.py:1120
  433.1 34.0 %collective-permute-start.30 = (bf16[96,1536]{1,0:T(8,128)(2,1)}, bf16[96,1536]{1,0:T(8,128)(2,1)S(1)}, u32[]{:S(2)}, u32[]{:S(2)}) collective-permute-start(bf16[96,1536]{1,0:T(8,128)(2,1)} %get-tuple-element.220.refs_15_), channel_id=1, source_target_pairs={{0,7},{1,6},{2,5},{3,4},{4,3},{5,2},{6,1},{7,0},{8,15},{9,14},{10,... | collective-permute-start | bytes 884744 | tf_op jit(solution)/shard_map/ppermute | solution.py:1120
  434.0 33.7 %collective-permute-start.31 = (bf16[96,1536]{1,0:T(8,128)(2,1)}, bf16[96,1536]{1,0:T(8,128)(2,1)S(1)}, u32[]{:S(2)}, u32[]{:S(2)}) collective-permute-start(bf16[96,1536]{1,0:T(8,128)(2,1)} %get-tuple-element.221.refs_11_), channel_id=1, source_target_pairs={{0,3},{1,2},{2,1},{3,0},{4,7},{5,6},{6,5},{7,4},{8,11},{9,10},{10,... | collective-permute-start | bytes 884744 | tf_op jit(solution)/shard_map/ppermute | solution.py:1120
  468.5 43.7 %all-to-all-start.5 = ((bf16[8,320,256]{2,1,0:T(8,128)(2,1)}), bf16[8,320,256]{2,1,0:T(8,128)(2,1)}, u32[]{:S(2)}, u32[]{:S(2)}) async-start(bf16[8,320,256]{2,1,0:T(8,128)(2,1)} %copy-done.21), calls=%async_computation.5 | async-start | bytes 2621440 | tf_op jit(solution)/shard_map/all_to_all | solution.py:1143
  479.1 31.2 %collective-permute-start.35 = (bf16[384,768]{1,0:T(8,128)(2,1)}, bf16[384,768]{1,0:T(8,128)(2,1)}, u32[]{:S(2)}, u32[]{:S(2)}) collective-permute-start(bf16[384,768]{1,0:T(8,128)(2,1)} %slice_bitcast_fusion), channel_id=1, source_target_pairs={{0,24},{8,16},{16,8},{24,0},{1,25},{9,17},{17,9},{25,1},{2,26},{10... | collective-permute-start | bytes 1769480 | tf_op jit(solution)/shard_map/ppermute | solution.py:1120
  486.3 21.3 %collective-permute-start.34 = (bf16[384,384]{1,0:T(8,128)(2,1)}, bf16[384,384]{1,0:T(8,128)(2,1)}, u32[]{:S(2)}, u32[]{:S(2)}) collective-permute-start(bf16[384,384]{1,0:T(8,128)(2,1)} %get-tuple-element.311), channel_id=1, source_target_pairs={{0,24},{8,16},{16,8},{24,0},{1,25},{9,17},{17,9},{25,1},{2,26},{10... | collective-permute-start | bytes 884744 | tf_op jit(solution)/shard_map/ppermute | solution.py:1120
  487.1 21.1 %collective-permute-start.33 = (bf16[384,384]{1,0:T(8,128)(2,1)}, bf16[384,384]{1,0:T(8,128)(2,1)}, u32[]{:S(2)}, u32[]{:S(2)}) collective-permute-start(bf16[384,384]{1,0:T(8,128)(2,1)} %get-tuple-element.312), channel_id=1, source_target_pairs={{0,16},{8,24},{16,0},{24,8},{1,17},{9,25},{17,1},{25,9},{2,18},{10... | collective-permute-start | bytes 884744 | tf_op jit(solution)/shard_map/ppermute | solution.py:1120
  487.8 20.4 %collective-permute-start.32 = (bf16[384,384]{1,0:T(8,128)(2,1)}, bf16[384,384]{1,0:T(8,128)(2,1)}, u32[]{:S(2)}, u32[]{:S(2)}) collective-permute-start(bf16[384,384]{1,0:T(8,128)(2,1)} %get-tuple-element.310), channel_id=1, source_target_pairs={{0,8},{8,0},{16,24},{24,16},{1,9},{9,1},{17,25},{25,17},{2,10},{10... | collective-permute-start | bytes 884744 | tf_op jit(solution)/shard_map/ppermute | solution.py:1120
  512.2 31.2 %all-to-all-start.6 = ((bf16[8,48,384]{2,1,0:T(8,128)(2,1)}), bf16[8,48,384]{2,1,0:T(8,128)(2,1)S(1)}, u32[]{:S(2)}, u32[]{:S(2)}) async-start(bf16[8,48,384]{2,1,0:T(8,128)(2,1)} %bitcast.47), calls=%async_computation.6 | async-start | bytes 589824 | tf_op jit(solution)/shard_map/all_to_all | solution.py:1143
  518.0 12.0 %collective-permute-start.38 = (bf16[96,768]{1,0:T(8,128)(2,1)S(1)}, bf16[96,768]{1,0:T(8,128)(2,1)S(1)}, u32[]{:S(2)}, u32[]{:S(2)}) collective-permute-start(bf16[96,768]{1,0:T(8,128)(2,1)S(1)} %get-tuple-element.322), channel_id=1, source_target_pairs={{0,6},{1,7},{2,4},{3,5},{4,2},{5,3},{6,0},{7,1},{8,14},{9,15},{10,... | collective-permute-start | bytes 442376 | tf_op jit(solution)/shard_map/ppermute | solution.py:1120
  521.2 18.9 %collective-permute-start.37 = (bf16[96,768]{1,0:T(8,128)(2,1)S(1)}, bf16[96,768]{1,0:T(8,128)(2,1)S(1)}, u32[]{:S(2)}, u32[]{:S(2)}) collective-permute-start(bf16[96,768]{1,0:T(8,128)(2,1)S(1)} %get-tuple-element.323), channel_id=1, source_target_pairs={{0,4},{1,5},{2,6},{3,7},{4,0},{5,1},{6,2},{7,3},{8,12},{9,13},{10,... | collective-permute-start | bytes 442376 | tf_op jit(solution)/shard_map/ppermute | solution.py:1120
  521.2 18.9 %collective-permute-start.36 = (bf16[96,768]{1,0:T(8,128)(2,1)S(1)}, bf16[96,768]{1,0:T(8,128)(2,1)S(1)}, u32[]{:S(2)}, u32[]{:S(2)}) collective-permute-start(bf16[96,768]{1,0:T(8,128)(2,1)S(1)} %get-tuple-element.321), channel_id=1, source_target_pairs={{0,2},{1,3},{2,0},{3,1},{4,6},{5,7},{6,4},{7,5},{8,10},{9,11},{10,... | collective-permute-start | bytes 442376 | tf_op jit(solution)/shard_map/ppermute | solution.py:1120
  (77 other events, 850.5 us)
Sparse Core Ops, SparseCore 0:
  9.7 75.4 all-gather.11
  88.2 79.6 all-gather.5
  183.6 57.6 all-gather.7
  251.0 81.1 all-gather.9
  424.3 53.3 reduce-scatter.1

commit v3 on v2

--- a/solution.py
+++ b/solution.py
@@ -497,7 +497,7 @@
             jax.ShapeDtypeStruct((blocks, wide, block), jnp.bfloat16),
         ],
         scratch_shapes=[pltpu.VMEM((1, width), jnp.float32)],
-        compiler_params=pltpu.CompilerParams(vmem_limit_bytes=40 * 2**20),
+        compiler_params=pltpu.CompilerParams(vmem_limit_bytes=60 * 2**20),
         name="project",
     )(rows, head_weights, head_weights)
 
@@ -752,7 +752,7 @@
             jax.ShapeDtypeStruct((height, width), jnp.bfloat16),
             jax.ShapeDtypeStruct((2, rows), jnp.float32),
         ],
-        compiler_params=pltpu.CompilerParams(vmem_limit_bytes=40 * 2**20),
+        compiler_params=pltpu.CompilerParams(vmem_limit_bytes=60 * 2**20),
         name="middle",
     )(start, mixed, weight, head_weights, slots, routes)
 
@@ -858,12 +858,10 @@
     cot_refs, part_refs, refs = refs[:blocks], refs[blocks : 2 * blocks], refs[2 * blocks :]
     rows_ref, gates_ref, pre_gate_ref, pre_up_ref = refs[:4]
     weight_refs, refs = refs[4:16], refs[16:]
-    table_ref, other_ref, pre_ref, grad_ref, back_ref, router_ref = refs[:6]
-    cot, back_sum, gate, up, outer = refs[6:]
+    table_ref, other_ref, grad_gate_ref, grad_up_ref, grad_ref, back_ref, router_ref = refs[:7]
+    cot, back_sum, gate, up, outer = refs[7:]
     step = pl.program_id(0)
-    tile = gate.shape[1]
     assemble_weights(own_ref, weight_refs, gate, up, outer)
-    units = tile * pl.num_programs(0)
     size = cot_refs[0].shape[0]
     gates = gates_ref[...]
 
@@ -880,9 +878,8 @@
     grad_gate = grad_hidden * up_pre * sigma * (1.0 + gate_pre * (1.0 - sigma))
     grad_gate = grad_gate.astype(jnp.bfloat16)
     grad_up = (grad_hidden * (gate_pre * sigma)).astype(jnp.bfloat16)
-    at = pl.multiple_of(step * tile, tile)
-    pre_ref[:, pl.ds(at, tile)] = grad_gate
-    pre_ref[:, pl.ds(pl.multiple_of(units + at, tile), tile)] = grad_up
+    grad_gate_ref[...] = grad_gate
+    grad_up_ref[...] = grad_up
     back_sum[...] += contract(grad_gate, gate[...], 1, 1) + contract(grad_up, up[...], 1, 1)
 
     @pl.when(step == pl.num_programs(0) - 1)
@@ -940,7 +937,8 @@
                 whole(other.shape),
             ],
             out_specs=[
-                whole((height, 2 * units)),
+                tiled(height, 0),
+                tiled(height, 0),
                 whole((height, width)),
                 whole((height, width)),
                 whole((128, width)),
@@ -954,7 +952,8 @@
             ],
         ),
         out_shape=[
-            jax.ShapeDtypeStruct((height, 2 * units), low),
+            jax.ShapeDtypeStruct((height, units), low),
+            jax.ShapeDtypeStruct((height, units), low),
             jax.ShapeDtypeStruct((height, width), low),
             jax.ShapeDtypeStruct((height, width), low),
             jax.ShapeDtypeStruct((128, width), f32),
@@ -1111,6 +1110,27 @@
     )(home, query_weight, keyval_weight, gain)
 
 
+def sum_pairs_kernel(*refs):
+    out_ref = refs[-1]
+    count = len(refs) // 2
+    for side in range(2):
+        total = sum(ref[...].astype(jnp.float32) for ref in refs[side * count : (side + 1) * count])
+        out_ref[:, side, :] = total
+
+
+def sum_pairs(first, second, tile):
+    rows, width = first[0].shape
+    return pl.pallas_call(
+        sum_pairs_kernel,
+        grid=(rows // tile,),
+        in_specs=[pl.BlockSpec((tile, width), lambda i: (i, 0))] * (len(first) + len(second)),
+        out_specs=pl.BlockSpec((tile, 2, width), lambda i: (i, 0, 0)),
+        out_shape=jax.ShapeDtypeStruct((rows, 2, width), jnp.float32),
+        compiler_params=pltpu.CompilerParams(vmem_limit_bytes=40 * 2**20),
+        name="sum_pairs",
+    )(*first, *second)
+
+
 def after(values, *earlier):
     return lax.optimization_barrier((values, earlier))[0]
 
@@ -1230,8 +1250,6 @@
     arrived, inner_x, inner_y, outer_x, outer_y = after(
         (arrived, inner_x, inner_y, outer_x, outer_y)
     )
-    inner_far = flip_exchange(inner_x, "dp", 2)
-    outer_far = flip_exchange(outer_y, "dp", 1)
     segments = arrived[:, shard, :rows].reshape(length).astype(jnp.int32)
     other_expert = arrived[:, shard + 1, :capacity].reshape(height, 1).astype(jnp.int32)
     head_rows = arrived[:, :shard].reshape(count * shard, lanes)
@@ -1253,12 +1271,8 @@
     spans = jnp.stack([starts, wholes]).astype(jnp.int32)
     seg_row, seg_col = segments.reshape(1, length), segments.reshape(length, 1)
     mixed_head, mixed_exact, totals = attend(spans, projected, seg_row, seg_col)
-    mixed_head, cot_first, inner_far, outer_far, by_head_line = after(
-        (mixed_head, cot_first, inner_far, outer_far, by_head_line)
-    )
+    mixed_head, cot_first, by_head_line = after((mixed_head, cot_first, by_head_line))
     project_line = gather(by_head_line, "fsdp")
-    inner_parts = [inner_own, inner_x, inner_y, inner_far]
-    outer_parts = [outer_weight, outer_x, outer_y, outer_far]
     mixed = all_to_all(mixed_head).reshape(count * share, rows)
 
     middle, sent, gates = middle_part(
@@ -1267,7 +1281,13 @@
     )
 
     rows_in = all_to_all(sent)
-    rows_in, cot_sent, project_line = after((rows_in, cot_sent, project_line))
+    inner_far = flip_exchange(after(inner_x, sent), "dp", 2)
+    outer_far = flip_exchange(after(outer_y, sent), "dp", 1)
+    rows_in, cot_sent, project_line, inner_far, outer_far = after(
+        (rows_in, cot_sent, project_line, inner_far, outer_far)
+    )
+    inner_parts = [inner_own, inner_x, inner_y, inner_far]
+    outer_parts = [outer_weight, outer_x, outer_y, outer_far]
     project_all = gather(project_line, "dp")
     cot_last = swap_near_blocks(cot_sent, (5, 7, 3, 1))
     own_expert = jnp.stack([index, group]).astype(jnp.int32)
@@ -1276,31 +1296,37 @@
         router_lane, 256, experts,
     )
     hidden, parts, cot_last = after((hidden, parts, cot_last))
-    part_first = swap_near_blocks(parts, (4, 6, 2, 1))
+    part_first = swap_near_blocks(parts, (4, 6, 2, 1, 3))
     cot_in = [cot_sent[0], cot_last[3], cot_first[2], cot_last[2]]
     cot_in = cot_in + [cot_first[0], cot_last[0], cot_first[1], cot_last[1]]
-    grad_pre, grad_in, grad_rows, router_part = expert_backward_pass(
+    grad_gate, grad_up, grad_in, grad_rows, router_part = expert_backward_pass(
         own_expert, cot_in, parts, rows_in, slot_gates, pre_gate, pre_up, inner_parts, outer_parts,
-        head_weights, other_expert, router_lane, 256,
-    )
-    grad_rows, part_first, grad_pre, grad_in = after((grad_rows, part_first, grad_pre, grad_in))
+        head_weights, other_expert, router_lane, 512,
+    )
+    grad_rows, part_first, grad_gate, grad_up, grad_in = after(
+        (grad_rows, part_first, grad_gate, grad_up, grad_in)
+    )
     grad_home = all_to_all(grad_rows)
 
     def cut(value, k):
         return lax.dynamic_slice_in_dim(value, jnp.bitwise_xor(group, k) * size, size, 1)
 
-    inner_terms = [contract(cut(rows_in, k), grad_pre, 0, 0).astype(low) for k in range(4)]
-    outer_term = contract(grad_in, hidden, 0, 0).astype(low)
-    half_size = size // 2
-    inner_a = [term[:half_size] for term in inner_terms]
-    inner_b = [term[half_size:] for term in inner_terms]
-    near_a, far_a = [flip_exchange(inner_a[k], "dp", 1) for k in (1, 3)]
-    near_b, far_b = [flip_exchange(inner_b[k], "dp", 2) for k in (2, 3)]
-    grad_home, outer_term, near_a, far_a, near_b, far_b, project_all = after(
-        (grad_home, outer_term, near_a, far_a, near_b, far_b, project_all)
-    )
-    passed_a = (inner_a[2].astype(f32) + far_a.astype(f32)).astype(low)
-    passed_b = (inner_b[1].astype(f32) + far_b.astype(f32)).astype(low)
+    rows_near = [cut(rows_in, k) for k in range(4)]
+    gate_terms = [contract(near, grad_gate, 0, 0).astype(low) for near in rows_near]
+    up_terms = [contract(near, grad_up, 0, 0).astype(low) for near in rows_near]
+    near_a, far_a = [flip_exchange(gate_terms[k], "dp", 1) for k in (1, 3)]
+    near_b, far_b = [flip_exchange(up_terms[k], "dp", 2) for k in (2, 3)]
+    passed_a = (gate_terms[2].astype(f32) + far_a.astype(f32)).astype(low)
+    passed_b = (up_terms[1].astype(f32) + far_b.astype(f32)).astype(low)
+    outer_term = jnp.concatenate(
+        [contract(hidden, grad_in[:, k * size : (k + 1) * size], 0, 0) for k in range(4)]
+    ).astype(low)
+    grad_home, outer_term, passed_a, passed_b, gate_terms, up_terms, near_a, near_b, project_all = after(
+        (
+            grad_home, outer_term, passed_a, passed_b, gate_terms, up_terms, near_a, near_b,
+            project_all,
+        )
+    )
     side_a, side_b = flip_exchange(passed_a, "dp", 2), flip_exchange(passed_b, "dp", 1)
 
     grad_middle, grad_branch, gain_part, mixed_grad = back_part(
@@ -1322,8 +1348,8 @@
         (mixed_grad, output_part, parts, side_a, side_b, outer_term)
     )
     outer_sum = lax.psum_scatter(outer_term, "dp", scatter_dimension=0, tiled=True)
-    part_last = swap_near_blocks(parts, (5, 7, 3))
-    output_near = [flip_exchange(output_part[k], "dp", k) for k in (1, 2)]
+    output_near = flip_exchange(output_part[2:], "dp", 2)
+    part_last = swap_near_blocks(parts, (5, 7))
 
     grads_blocks, grads_line = attend_backward(
         spans, projected, mixed_grad, seg_row, seg_col, mixed_exact, totals
@@ -1331,36 +1357,33 @@
     grads_blocks, grads_line, output_part, output_near, part_last = after(
         (grads_blocks, grads_line, output_part, output_near, part_last)
     )
-    part_home = [parts[0], part_first[3], part_first[2], part_last[2]]
+    part_home = [parts[0], part_first[3], part_first[2], part_first[4]]
     part_home = part_home + [part_first[0], part_last[0], part_first[1], part_last[1]]
     grad_mine = all_to_all(grads_blocks).reshape(count * cols, rows)
     extra = jnp.concatenate(
         [router_part[router_lane : router_lane + experts], gain_part,
          jnp.zeros((lanes - cols - experts - 1, width), f32)]
     )
-    output_near = output_near + [flip_exchange(output_part[3], "dp", 3)]
+    output_sum = output_part[:2].astype(f32) + output_near.astype(f32)
+    output_passed = output_sum[1].astype(low)
+    output_side = flip_exchange(output_passed, "dp", 1)
+    grads_line = after(grads_line, output_passed)
     own_group = group.reshape(1).astype(jnp.int32)
     terms = weight_terms(own_group, normed, grads_line, extra, 4)
     weight_sum = terms[0].astype(f32)
     for k in range(1, 4):
         weight_sum = weight_sum + flip_exchange(terms[k], "dp", k).astype(f32)
-    inner_grad = jnp.concatenate(
-        [
-            inner_a[0].astype(f32) + near_a.astype(f32) + side_a.astype(f32),
-            inner_b[0].astype(f32) + near_b.astype(f32) + side_b.astype(f32),
-        ]
-    ).reshape(size, 2, ff)
-    outer_grad = outer_sum.astype(f32).T
     block_out = mixture(slots_near, gates, middle, part_home)
-    output_sum = output_part[0].astype(f32)
-    for near in output_near:
-        output_sum = output_sum + near.astype(f32)
-    weight_sum, output_sum = after((weight_sum.astype(low), output_sum), grad_mine)
+    inner_grad = sum_pairs(
+        [gate_terms[0], near_a, side_a], [up_terms[0], near_b, side_b], size // 4
+    )
+    outer_grad = outer_sum.astype(f32)
+    grad_normed = contract(
+        after(grad_mine, inner_grad, outer_grad, block_out), project_all, 0, 1
+    )
+    output_sum = output_sum[0] + output_side.astype(f32)
+    weight_sum = after(weight_sum.astype(low), grad_mine)
     weight_home = all_to_all(weight_sum.reshape(count, shard, lanes))
-    query_grad, keyval_grad, router_grad, gains = weight_grads(
-        weight_home, query_weight, key_value_weight, gain_before[:, None], share, experts
-    )
-    before_grad, middle_grad = gains[:, 0], gains[:, 1]
     chips, pair = count // 2, 2 * shard
     output_low = output_sum.astype(low)
 
@@ -1368,9 +1391,17 @@
         at = jnp.bitwise_xor(index // 2, k) * pair
         return lax.dynamic_slice_in_dim(value, at, pair, 0)
 
+    output_line = [
+        flip_exchange(line_part(output_low, k), "fsdp", 2 * k) for k in range(1, chips)
+    ]
+    output_line, weight_home = after((output_line, weight_home), block_out, outer_grad)
+    query_grad, keyval_grad, router_grad, gains = weight_grads(
+        weight_home, query_weight, key_value_weight, gain_before[:, None], share, experts
+    )
+    before_grad, middle_grad = gains[:, 0], gains[:, 1]
     output_grad = line_part(output_sum, 0)
-    for k in range(1, chips):
-        output_grad = output_grad + flip_exchange(line_part(output_low, k), "fsdp", 2 * k).astype(f32)
+    for near in output_line:
+        output_grad = output_grad + near.astype(f32)
     own_half = lax.dynamic_slice_in_dim(output_grad, core * shard, shard, 0)
     other_half = flip_exchange(
         lax.dynamic_slice_in_dim(output_grad, (1 - core) * shard, shard, 0), "fsdp", 1
@@ -1380,7 +1411,6 @@
         jnp.concatenate([own_half, other_half], 1),
         jnp.concatenate([other_half, own_half], 1),
     ).T
-    grad_normed = contract(grad_mine, project_all, 0, 1)
     gain_first = head_weights[:, table_lane + first_lane]
     _, unit_first, factor_first = normalize(start_low.astype(f32), gain_first)
     outer_back, _ = normalize_back(grad_normed, unit_first, factor_first, gain_first)

time: 565 us -> 536 us (0.949)
  local copies, waits for them, and re-layouts: 53.6 us -> 29.5 us
  waiting for transfers between devices: 165 us -> 141 us
  other arithmetic: 22.1 us -> 33.7 us
  starting transfers between devices: 77.5 us -> 65.9 us
  matrix products: 32.8 us -> 41.1 us
  Pallas kernels: 125 us -> 132 us
    ppermute x40 -> x39, waiting for transfers between devices: 82.6 us -> 61.1 us  [flip_exchange(): return lax.ppermute(block, axis, [(i, i ^ flip) for i in range(count)])]
    unnamed x155 -> x140, local copies, waits for them, and re-layouts: 33.7 us -> 18.9 us
    all_to_all x5, starting transfers between devices: 35 us -> 25.7 us  [all_to_all(): lax.all_to_all(blocks, 'fsdp', split_axis=0, concat_axis=0, tiled=True)]
    concatenate x1, other arithmetic: 2.04 us -> 11 us  [per_device_heads(): jnp.concatenate([contract(hidden, grad_in[:, k * size:(k + 1) * size], 0,...]
    dot_general x8 -> x15, matrix products: 32.5 us -> 40.7 us  [contract(): lax.dot_general(left, right, (((left_axis,), (right_axis,)), ((), ())), p...]
    reshape x1 -> x0, local copies, waits for them, and re-layouts: 5.73 us -> none  [per_device_heads(): inner_grad = jnp.concatenate([inner_a[0].astype(f32) + near_a.astype(f32)...]
    ppermute x40 -> x39, starting transfers between devices: 42.1 us -> 40 us  [flip_exchange(): return lax.ppermute(block, axis, [(i, i ^ flip) for i in range(count)])]
  transfers between devices with their start and end apart: 50 -> 49, of which waited for: 16 -> 16; matrix products, arithmetic and copies ran while one was open for 13% -> 16% of each run, Pallas kernels for 21% -> 23%
where the time goes in v3:
time: 536 us; the launch traced here: 526 us
  waiting for transfers between devices  141 us (26%)
  Pallas kernels  132 us (25%)
  blocking collectives  67.1 us (13%)
  starting transfers between devices  65.9 us (12%)
  matrix products  41.1 us (8%)
  other arithmetic  33.7 us (6%)
  local copies, waits for them, and re-layouts  29.5 us (6%)
  between operations  15.3 us (3%)
    all_to_all x2, blocking collectives, all_to_all(): lax.all_to_all(blocks, 'fsdp', split_axis=0, concat_axis=0, tiled=True)  67.1 us
    all_gather x4, waiting for transfers between devices, gather(): return lax.all_gather(block, axis, axis=0, tiled=True)  62.5 us
    ppermute x39, waiting for transfers between devices, flip_exchange(): return lax.ppermute(block, axis, [(i, i ^ flip) for i in range(count)])  61.1 us
    dot_general x15, matrix products, contract(): lax.dot_general(left, right, (((left_axis,), (right_axis,)), ((), ())), p...  40.7 us
    ppermute x39, starting transfers between devices, flip_exchange(): return lax.ppermute(block, axis, [(i, i ^ flip) for i in range(count)])  40 us
    all_to_all x5, starting transfers between devices, all_to_all(): lax.all_to_all(blocks, 'fsdp', split_axis=0, concat_axis=0, tiled=True)  25.7 us
    pallas_call x1, Pallas kernels, attend_backward(): pl.pallas_call(attend_back_kernel, grid_spec=pltpu.PrefetchScalarGridSpec...  25.6 us
    pallas_call x1, Pallas kernels, expert_backward_pass(): pl.pallas_call(functools.partial(expert_back_kernel, router_lane, blocks)...  25 us
  transfers between devices with their start and end apart: 49, of which 16 were waited for; matrix products, arithmetic and copies ran while one was open for 16% of the time, Pallas kernels for 23%

profile of v3, /device:TPU:1, one launch (start us, length us, event | category | flops | bytes accessed | tf_op | source)
XLA Modules:
  0.0 526.1 jit_solution(838774042982671359)
XLA Ops:
  8.0 3.1 copy.78
  17.0 29.4 %all_to_all.49 = bf16[8,64,384]{2,1,0:T(8,128)(2,1)S(1)} all-to-all(bf16[8,64,384]{2,1,0:T(8,128)(2,1)S(1)} %copy.70), channel_id=1, replica_groups=mesh['dp'=4,'fsdp'=8] {'fsdp'}, dimensions={0} | all-to-all | bytes 786432 | tf_op jit(solution)/shard_map/all_to_all | solution.py:1163
  46.4 18.0 %collective-permute-done.2.refs_9_.refs_29_ = bf16[1024,384]{1,0:T(8,128)(2,1)S(1)} collective-permute-done((bf16[1024,384]{1,0:T(8,128)(2,1)S(1)}, bf16[1024,384]{1,0:T(8,128)(2,1)S(1)}, u32[]{:S(2)}, u32[]{:S(2)}) %collective-permute-start.2) | collective-permute-done | bytes 786464 | tf_op jit(solution)/shard_map/ppermute | solution.py:1140
  73.1 8.5 %collective-permute-done.5 = bf16[384,384]{1,0:T(8,128)(2,1)} collective-permute-done((bf16[384,384]{1,0:T(8,128)(2,1)S(1)}, bf16[384,384]{1,0:T(8,128)(2,1)}, u32[]{:S(2)}, u32[]{:S(2)}) %collective-permute-start.5) | collective-permute-done | bytes 294944 | tf_op jit(solution)/shard_map/ppermute | solution.py:1140
  89.6 10.4 %project.1 = (bf16[2048,1536]{1,0:T(8,128)(2,1)}, bf16[8,320,256]{2,1,0:T(8,128)(2,1)}) custom-call(bf16[2048,1536]{1,0:T(8,128)(2,1)} %bitcast.129, bf16[1536,384]{1,0:T(8,128)(2,1)} %bitcast.114, bf16[1536,384]{1,0:T(8,128)(2,1)} %bitcast.115), custom_call_target="tpu_custom_call" | custom-call | tf_op jit(solution)/shard_map/project/pallas_call | solution.py:483
  101.4 21.4 %attend.1 = (bf16[8,192,256]{2,1,0:T(8,128)(2,1)S(1)}, f32[8,192,256]{2,1,0:T(8,128)S(1)}, f32[8,8,256]{2,1,0:T(8,128)S(1)}) custom-call(s32[2,8]{1,0:T(2,128)S(1)} %pad_add_fusion.spans, bf16[8,320,256]{2,1,0:T(8,128)(2,1)S(1)} %copy-done.1, bf16[8,320,256]{2,1,0:T(8,128)(2,1)S(1)} %copy-done.1, s32[1,2048]{1,0:T(1,128)S(1)} %bitcast.126, ...), custom_call_target="tpu_custom_call" | custom-call | tf_op jit(solution)/shard_map/attend/pallas_call | solution.py:567
  124.6 37.7 %all_to_all.50 = bf16[8,192,256]{2,1,0:T(8,128)(2,1)} all-to-all(bf16[8,192,256]{2,1,0:T(8,128)(2,1)S(1)} %get-tuple-element.155), channel_id=1, replica_groups=mesh['dp'=4,'fsdp'=8] {'fsdp'}, dimensions={0} | all-to-all | bytes 1572864 | tf_op jit(solution)/shard_map/all_to_all | solution.py:1163
  162.3 3.6 all-gather.6.cloned.1.call-done.weight_ref
  165.9 6.7 %middle.1 = (f32[256,1536]{1,0:T(8,128)}, bf16[768,1536]{1,0:T(8,128)(2,1)}, f32[2,256]{1,0:T(2,128)}) custom-call(bf16[256,1536]{1,0:T(8,128)(2,1)} %bitcast.128, bf16[1536,256]{1,0:T(8,128)(2,1)} %bitcast.130, bf16[1536,1536]{1,0:T(8,128)(2,1)} %all-gather.6.cloned.1.call-done.weight_ref, bf16[1536,384]{1,0:T(8,128)(2,1)} %bitcast.116, ...), custom_call_target="tpu_custom_call" | custom-call | tf_op jit(solution)/shard_map/middle/pallas_call | solution.py:738
  172.6 4.5 all-to-all-start.2
  179.5 58.0 %all-gather.8.cloned.1.call-done = bf16[384,2560]{1,0:T(8,128)(2,1)} async-done(((bf16[48,2560]{1,0:T(8,128)(2,1)}), bf16[384,2560]{1,0:T(8,128)(2,1)}) %all-gather.8.cloned.1.call-update) | async-done | bytes 1966096 | tf_op jit(solution)/shard_map/all_gather | solution.py:1167
  237.4 9.4 %all-to-all-done.2 = bf16[8,96,1536]{2,1,0:T(8,128)(2,1)} async-done(((bf16[8,96,1536]{2,1,0:T(8,128)(2,1)}), bf16[8,96,1536]{2,1,0:T(8,128)(2,1)}, u32[]{:S(2)}, u32[]{:S(2)}) %all-to-all-start.2) | async-done | bytes 2359328 | tf_op jit(solution)/shard_map/all_to_all | solution.py:1163
  253.1 18.4 %expert.1 = (f32[768,1024]{1,0:T(8,128)}, f32[768,1024]{1,0:T(8,128)}, bf16[768,1024]{1,0:T(8,128)(2,1)}, f32[768,128]{1,0:T(8,128)}, bf16[96,1536]{1,0:T(8,128)...) custom-call(s32[2]{0:T(128)} %pad_add_fusion.1.own_ref, ...), custom_call_target="tpu_custom_call" | custom-call | tf_op jit(solution)/shard_map/expert/pallas_call | solution.py:827
  271.5 4.5 collective-permute-start.16
  280.0 25.0 %expert_backward.1 = (bf16[768,1024]{1,0:T(8,128)(2,1)}, bf16[768,1024]{1,0:T(8,128)(2,1)}, bf16[768,1536]{1,0:T(8,128)(2,1)}, bf16[768,1536]{1,0:T(8,128)(2,1)}, f32[128,1536]{1,0:T(8,128)}) custom-call(s32[2]{0:T(128)} %pad_add_fusion.1.own_ref, bf16[96,1536]{1,0:T(8,128)(2,1)} %copy-done.33, bf16[96,1536]{1,0:T(8,128)(2,1)} %collective-permute-done.15.refs_1_, ...), custom_call_target="tpu_custom_call" | custom-call | tf_op jit(solution)/shard_map/expert_backward/pallas_call | solution.py:922
  306.1 5.0 all-to-all-start.3
  311.1 3.4 convolution_convert_fusion.8
  314.5 2.9 convolution_convert_fusion.6
  318.4 2.7 convolution_convert_fusion.4
  322.5 2.7 convolution_convert_fusion.2
  325.7 3.0 convolution_convert_fusion.9
  332.7 11.0 %pad_maximum_fusion = bf16[4096,384]{1,0:T(8,128)(2,1)} fusion(bf16[1024,384]{1,0:T(8,128)(2,1)S(1)} %convolution_convert_fusion.10, bf16[1024,384]{1,0:T(8,128)(2,1)S(1)} %convolution_convert_fusion.11, bf16[1024,384]{1,0:T(8,128)(2,1)S(1)} %convolution_convert_fusion.12, bf16[1024,384]{1,0:T(8,128)(2,1)S(1)} %convolution_convert_fusion.13), kind=kLoop, calls=%fused_computation.3 | loop fusion | flops 12582912 | bytes 6291456 | tf_op jit(solution)/shard_map/concatenate | solution.py:1321
  343.8 2.5 convolution_convert_fusion.7
  346.3 2.9 convolution_convert_fusion.5.refs_0_
  349.2 2.8 convolution_convert_fusion.3.refs_3_
  353.3 2.4 add_convert_fusion.1
  355.8 6.3 %collective-permute-done.23.refs_1_ = bf16[384,1024]{1,0:T(8,128)(2,1)} collective-permute-done((bf16[384,1024]{1,0:T(8,128)(2,1)}, bf16[384,1024]{1,0:T(8,128)(2,1)}, u32[]{:S(2)}, u32[]{:S(2)}) %collective-permute-start.23) | collective-permute-done | bytes 786464 | tf_op jit(solution)/shard_map/ppermute | solution.py:1140
  362.0 2.9 all-to-all-done.3
  365.0 6.3 %back.1 = (f32[256,1536]{1,0:T(8,128)S(1)}, bf16[256,1536]{1,0:T(8,128)(2,1)S(1)}, f32[1,1536]{1,0:T(1,128)S(1)}, bf16[1536,256]{1,0:T(8,128)(2,1)S(1)}) custom-call(f32[256,1536]{1,0:T(8,128)} %get-tuple-element.158.middle_ref, bf16[256,1536]{1,0:T(8,128)(2,1)S(1)} %bitcast.122, bf16[768,1536]{1,0:T(8,128)(2,1)} %bitcast.33.home_ref, ...), custom_call_target="tpu_custom_call" | custom-call | tf_op jit(solution)/shard_map/back/pallas_call | solution.py:991
  373.0 2.3 convolution_convert_fusion
  376.2 3.5 all-to-all-start.4
  380.9 4.3 add_convert_fusion
  385.2 14.1 %collective-permute-done.26.refs_2_ = bf16[384,1024]{1,0:T(8,128)(2,1)} collective-permute-done((bf16[384,1024]{1,0:T(8,128)(2,1)}, bf16[384,1024]{1,0:T(8,128)(2,1)}, u32[]{:S(2)}, u32[]{:S(2)}) %collective-permute-start.26) | collective-permute-done | bytes 786464 | tf_op jit(solution)/shard_map/ppermute | solution.py:1140
  400.9 2.5 slice.97
  404.3 3.0 collective-permute-start.29
  417.1 25.6 %attend_backward.1 = (bf16[8,320,256]{2,1,0:T(8,128)(2,1)S(1)}, bf16[320,2048]{1,0:T(8,128)(2,1)S(1)}) custom-call(s32[2,8]{1,0:T(2,128)S(1)} %pad_add_fusion.spans, bf16[8,320,256]{2,1,0:T(8,128)(2,1)S(1)} %copy-done.2, bf16[8,192,256]{2,1,0:T(8,128)(2,1)S(1)} %copy-done.7, bf16[8,320,256]{2,1,0:T(8,128)(2,1)S(1)} %copy-done.2, s32[1,2048]{1,0:T(1,128)S(1)} %bitcast.127, ...), custom_call_target="tpu_custom_call" | custom-call | tf_op jit(solution)/shard_map/attend_backward/pallas_call | solution.py:654
  443.7 3.1 collective-permute-done.28
  446.8 6.7 %all-to-all-start.5 = ((bf16[8,320,256]{2,1,0:T(8,128)(2,1)}), bf16[8,320,256]{2,1,0:T(8,128)(2,1)}, u32[]{:S(2)}, u32[]{:S(2)}) async-start(bf16[8,320,256]{2,1,0:T(8,128)(2,1)} %copy-done.14), calls=%async_computation.5 | async-start | bytes 2621440 | tf_op jit(solution)/shard_map/all_to_all | solution.py:1163
  455.9 2.8 copy-done.3
  458.7 4.5 weight_terms.1
  466.5 4.9 sum_pairs.1
  471.4 7.0 %mixture.1 = bf16[256,1536]{1,0:T(8,128)(2,1)} custom-call(s32[2,256]{1,0:T(2,128)S(1)} %get-tuple-element.343.slots_ref, f32[2,256]{1,0:T(2,128)S(1)} %copy-done.41, f32[256,1536]{1,0:T(8,128)S(1)} %copy-done.4, bf16[96,1536]{1,0:T(8,128)(2,1)S(1)} %copy-done.15, bf16[96,1536]{1,0:T(8,128)(2,1)S(1)} %copy-done.30, bf16[96,1536]{1,0:T(8,128)(2,1)S(1)} %copy-done.28, ...), custom_call_target="tpu_custom_call" | custom-call | tf_op jit(solution)/shard_map/mixture/pallas_call | solution.py:1066
  480.3 5.4 %collective-permute-done.35 = bf16[384,384]{1,0:T(8,128)(2,1)S(1)} collective-permute-done((bf16[384,384]{1,0:T(8,128)(2,1)S(1)}, bf16[384,384]{1,0:T(8,128)(2,1)S(1)}, u32[]{:S(2)}, u32[]{:S(2)}) %collective-permute-start.35) | collective-permute-done | bytes 294944 | tf_op jit(solution)/shard_map/ppermute | solution.py:1140
  491.5 6.0 %all-to-all-start.6 = ((bf16[8,48,384]{2,1,0:T(8,128)(2,1)}), bf16[8,48,384]{2,1,0:T(8,128)(2,1)S(1)}, u32[]{:S(2)}, u32[]{:S(2)}) async-start(bf16[8,48,384]{2,1,0:T(8,128)(2,1)} %bitcast.45), calls=%async_computation.7 | async-start | bytes 589824 | tf_op jit(solution)/shard_map/all_to_all | solution.py:1163
  497.4 2.4 convert_element_type.239
  499.8 7.2 %fusion.2 = (f32[256]{0:T(256)S(1)}, f32[256,1536]{1,0:T(8,128)}) fusion(f32[256]{0:T(256)S(1)} %add_rsqrt_fusion, bf16[1,256,1536]{2,1,0:T(8,128)(2,1)S(1)} %copy-done.44, f32[1536]{0:T(1024)S(1)} %convert_reduce_fusion, bf16[2560,256]{1,0:T(8,128)(2,1)} %bitcast.37, bf16[1536,2560]{1,0:T(8,128)(2,1)} %all-gather.10.cloned.1.call-done), kind=kOutput, calls=%fused_computation.10 | convolution fusion | flops 2015231744 | bytes 11542528 | tf_op jit(solution)/shard_map/dot_general | solution.py:447
  507.0 3.9 all-to-all-done.6.home_ref
  513.2 3.0 fusion.6
  (291 shorter events, 83.2 us)
Async XLA Ops:
  7.2 78.1 %all-gather.12.cloned.1.call-start = ((), (), s32[]{:S(2)}) async-start(), calls=%async_computation.12 | async-start | bytes 7077888 | tf_op jit(solution)/shard_map/all_gather | solution.py:1167
  7.9 158.0 %all-gather.6.cloned.1.call-start = ((), (), s32[]{:S(2)}) async-start(), calls=%async_computation.8 | async-start | bytes 4866048 | tf_op jit(solution)/shard_map/all_gather | solution.py:1167
  11.1 54.2 %collective-permute-start = (bf16[384,2048]{1,0:T(8,128)(2,1)}, bf16[384,2048]{1,0:T(8,128)(2,1)}, u32[]{:S(2)}, u32[]{:S(2)}) collective-permute-start(bf16[384,2048]{1,0:T(8,128)(2,1)} %bitcast.50.refs_0_.refs_4_.refs_20_.refs_24_), channel_id=1, source_target_pairs={{0,8},{8,0},{16,24},{24,16},{1,9},{9,1},{17,25},{25,17},{2,10},{10... | collective-permute-start | bytes 4718600 | tf_op jit(solution)/shard_map/ppermute | solution.py:1140
  13.1 52.1 %collective-permute-start.1 = (bf16[384,2048]{1,0:T(8,128)(2,1)}, bf16[384,2048]{1,0:T(8,128)(2,1)}, u32[]{:S(2)}, u32[]{:S(2)}) collective-permute-start(bf16[384,2048]{1,0:T(8,128)(2,1)} %bitcast.50.refs_0_.refs_4_.refs_20_.refs_24_), channel_id=1, source_target_pairs={{0,16},{8,24},{16,0},{24,8},{1,17},{9,25},{17,1},{25,9},{2,18},{10... | collective-permute-start | bytes 4718600 | tf_op jit(solution)/shard_map/ppermute | solution.py:1140
  14.4 50.0 %collective-permute-start.2 = (bf16[1024,384]{1,0:T(8,128)(2,1)S(1)}, bf16[1024,384]{1,0:T(8,128)(2,1)S(1)}, u32[]{:S(2)}, u32[]{:S(2)}) collective-permute-start(bf16[1024,384]{1,0:T(8,128)(2,1)S(1)} %copy-done.45), channel_id=1, source_target_pairs={{0,8},{8,0},{16,24},{24,16},{1,9},{9,1},{17,25},{25,17},{2,10},{10... | collective-permute-start | bytes 2359304 | tf_op jit(solution)/shard_map/ppermute | solution.py:1140
  14.6 50.6 %collective-permute-start.3 = (bf16[1024,384]{1,0:T(8,128)(2,1)S(1)}, bf16[1024,384]{1,0:T(8,128)(2,1)}, u32[]{:S(2)}, u32[]{:S(2)}) collective-permute-start(bf16[1024,384]{1,0:T(8,128)(2,1)S(1)} %copy-done.45), channel_id=1, source_target_pairs={{0,16},{8,24},{16,0},{24,8},{1,17},{9,25},{17,1},{25,9},{2,18},{10... | collective-permute-start | bytes 2359304 | tf_op jit(solution)/shard_map/ppermute | solution.py:1140
  65.3 7.8 %collective-permute-start.6 = (bf16[384,384]{1,0:T(8,128)(2,1)S(1)}, bf16[384,384]{1,0:T(8,128)(2,1)}, u32[]{:S(2)}, u32[]{:S(2)}) collective-permute-start(bf16[384,384]{1,0:T(8,128)(2,1)S(1)} %bitcast.138), channel_id=1, source_target_pairs={{0,24},{8,16},{16,8},{24,0},{1,25},{9,17},{17,9},{25,1},{2,26},{10... | collective-permute-start | bytes 884744 | tf_op jit(solution)/shard_map/ppermute | solution.py:1140
  66.7 15.0 %collective-permute-start.5 = (bf16[384,384]{1,0:T(8,128)(2,1)S(1)}, bf16[384,384]{1,0:T(8,128)(2,1)}, u32[]{:S(2)}, u32[]{:S(2)}) collective-permute-start(bf16[384,384]{1,0:T(8,128)(2,1)S(1)} %bitcast.139), channel_id=1, source_target_pairs={{0,16},{8,24},{16,0},{24,8},{1,17},{9,25},{17,1},{25,9},{2,18},{10... | collective-permute-start | bytes 884744 | tf_op jit(solution)/shard_map/ppermute | solution.py:1140
  66.9 14.7 %collective-permute-start.4 = (bf16[384,384]{1,0:T(8,128)(2,1)S(1)}, bf16[384,384]{1,0:T(8,128)(2,1)}, u32[]{:S(2)}, u32[]{:S(2)}) collective-permute-start(bf16[384,384]{1,0:T(8,128)(2,1)S(1)} %bitcast.140), channel_id=1, source_target_pairs={{0,8},{8,0},{16,24},{24,16},{1,9},{9,1},{17,25},{25,17},{2,10},{10... | collective-permute-start | bytes 884744 | tf_op jit(solution)/shard_map/ppermute | solution.py:1140
  86.8 37.0 %collective-permute-start.7 = (bf16[96,1536]{1,0:T(8,128)(2,1)}, bf16[96,1536]{1,0:T(8,128)(2,1)S(1)}, u32[]{:S(2)}, u32[]{:S(2)}) collective-permute-start(bf16[96,1536]{1,0:T(8,128)(2,1)} %copy-done.43), channel_id=1, source_target_pairs={{0,4},{1,5},{2,6},{3,7},{4,0},{5,1},{6,2},{7,3},{8,12},{9,13},{10,... | collective-permute-start | bytes 884744 | tf_op jit(solution)/shard_map/ppermute | solution.py:1140
  88.3 35.6 %collective-permute-start.8 = (bf16[96,1536]{1,0:T(8,128)(2,1)}, bf16[96,1536]{1,0:T(8,128)(2,1)}, u32[]{:S(2)}, u32[]{:S(2)}) collective-permute-start(bf16[96,1536]{1,0:T(8,128)(2,1)} %copy-done.42), channel_id=1, source_target_pairs={{0,6},{1,7},{2,4},{3,5},{4,2},{5,3},{6,0},{7,1},{8,14},{9,15},{10,... | collective-permute-start | bytes 884744 | tf_op jit(solution)/shard_map/ppermute | solution.py:1140
  89.4 34.5 %collective-permute-start.9 = (bf16[96,1536]{1,0:T(8,128)(2,1)S(1)}, bf16[96,1536]{1,0:T(8,128)(2,1)}, u32[]{:S(2)}, u32[]{:S(2)}) collective-permute-start(bf16[96,1536]{1,0:T(8,128)(2,1)S(1)} %get-tuple-element.153), channel_id=1, source_target_pairs={{0,2},{1,3},{2,0},{3,1},{4,6},{5,7},{6,4},{7,5},{8,10},{9,11},{10,... | collective-permute-start | bytes 884744 | tf_op jit(solution)/shard_map/ppermute | solution.py:1140
  172.6 74.3 %all-to-all-start.2 = ((bf16[8,96,1536]{2,1,0:T(8,128)(2,1)}), bf16[8,96,1536]{2,1,0:T(8,128)(2,1)}, u32[]{:S(2)}, u32[]{:S(2)}) async-start(bf16[8,96,1536]{2,1,0:T(8,128)(2,1)} %bitcast.134), calls=%async_computation.2 | async-start | bytes 4718592 | tf_op jit(solution)/shard_map/all_to_all | solution.py:1163
  177.1 60.3 %all-gather.8.cloned.1.call-start = ((), (), s32[]{:S(2)}) async-start(), calls=%async_computation.9 | async-start | bytes 2211840 | tf_op jit(solution)/shard_map/all_gather | solution.py:1167
  177.9 187.1 %all-gather.10.cloned.1.call-start = ((), (), s32[]{:S(2)}) async-start(), calls=%async_computation.10 | async-start | bytes 9830400 | tf_op jit(solution)/shard_map/all_gather | solution.py:1167
  177.9 59.5 %collective-permute-start.10 = (bf16[384,2048]{1,0:T(8,128)(2,1)}, bf16[384,2048]{1,0:T(8,128)(2,1)}, u32[]{:S(2)}, u32[]{:S(2)}) collective-permute-start(bf16[384,2048]{1,0:T(8,128)(2,1)} %collective-permute-done.refs_1_.refs_5_.refs_21_.refs_25_), channel_id=1, source_target_pairs={{0,16},{8,24},{16,0},{24,8},{1,17},{9,25},{17,1},{25,9},{2,18},{10... | collective-permute-start | bytes 4718600 | tf_op jit(solution)/shard_map/ppermute | solution.py:1140
  179.0 58.4 %collective-permute-start.11 = (bf16[1024,384]{1,0:T(8,128)(2,1)}, bf16[1024,384]{1,0:T(8,128)(2,1)}, u32[]{:S(2)}, u32[]{:S(2)}) collective-permute-start(bf16[1024,384]{1,0:T(8,128)(2,1)} %collective-permute-done.3.refs_10_.refs_30_), channel_id=1, source_target_pairs={{0,8},{8,0},{16,24},{24,16},{1,9},{9,1},{17,25},{25,17},{2,10},{10... | collective-permute-start | bytes 2359304 | tf_op jit(solution)/shard_map/ppermute | solution.py:1140
  246.9 24.6 %collective-permute-start.12 = (bf16[96,1536]{1,0:T(8,128)(2,1)S(1)}, bf16[96,1536]{1,0:T(8,128)(2,1)S(1)}, u32[]{:S(2)}, u32[]{:S(2)}) collective-permute-start(bf16[96,1536]{1,0:T(8,128)(2,1)S(1)} %get-tuple-element.185), channel_id=1, source_target_pairs={{0,5},{1,4},{2,7},{3,6},{4,1},{5,0},{6,3},{7,2},{8,13},{9,12},{10,... | collective-permute-start | bytes 884744 | tf_op jit(solution)/shard_map/ppermute | solution.py:1140
  247.0 24.5 %collective-permute-start.13 = (bf16[96,1536]{1,0:T(8,128)(2,1)S(1)}, bf16[96,1536]{1,0:T(8,128)(2,1)}, u32[]{:S(2)}, u32[]{:S(2)}) collective-permute-start(bf16[96,1536]{1,0:T(8,128)(2,1)S(1)} %get-tuple-element.186), channel_id=1, source_target_pairs={{0,7},{1,6},{2,5},{3,4},{4,3},{5,2},{6,1},{7,0},{8,15},{9,14},{10,... | collective-permute-start | bytes 884744 | tf_op jit(solution)/shard_map/ppermute | solution.py:1140
  248.8 22.8 %collective-permute-start.14 = (bf16[96,1536]{1,0:T(8,128)(2,1)S(1)}, bf16[96,1536]{1,0:T(8,128)(2,1)}, u32[]{:S(2)}, u32[]{:S(2)}) collective-permute-start(bf16[96,1536]{1,0:T(8,128)(2,1)S(1)} %get-tuple-element.187), channel_id=1, source_target_pairs={{0,3},{1,2},{2,1},{3,0},{4,7},{5,6},{6,5},{7,4},{8,11},{9,10},{10,... | collective-permute-start | bytes 884744 | tf_op jit(solution)/shard_map/ppermute | solution.py:1140
  250.7 20.9 %collective-permute-start.15 = (bf16[96,1536]{1,0:T(8,128)(2,1)S(1)}, bf16[96,1536]{1,0:T(8,128)(2,1)}, u32[]{:S(2)}, u32[]{:S(2)}) collective-permute-start(bf16[96,1536]{1,0:T(8,128)(2,1)S(1)} %get-tuple-element.188), channel_id=1, source_target_pairs={{0,1},{1,0},{2,3},{3,2},{4,5},{5,4},{6,7},{7,6},{8,9},{9,8},{10,11... | collective-permute-start | bytes 884744 | tf_op jit(solution)/shard_map/ppermute | solution.py:1140
  271.5 33.5 %collective-permute-start.16 = (bf16[96,1536]{1,0:T(8,128)(2,1)}, bf16[96,1536]{1,0:T(8,128)(2,1)S(1)}, u32[]{:S(2)}, u32[]{:S(2)}) collective-permute-start(bf16[96,1536]{1,0:T(8,128)(2,1)} %get-tuple-element.200.refs_12_), channel_id=1, source_target_pairs={{0,4},{1,5},{2,6},{3,7},{4,0},{5,1},{6,2},{7,3},{8,12},{9,13},{10,... | collective-permute-start | bytes 884744 | tf_op jit(solution)/shard_map/ppermute | solution.py:1140
  276.0 29.0 %collective-permute-start.17 = (bf16[96,1536]{1,0:T(8,128)(2,1)}, bf16[96,1536]{1,0:T(8,128)(2,1)S(1)}, u32[]{:S(2)}, u32[]{:S(2)}) collective-permute-start(bf16[96,1536]{1,0:T(8,128)(2,1)} %get-tuple-element.202.refs_14_), channel_id=1, source_target_pairs={{0,6},{1,7},{2,4},{3,5},{4,2},{5,3},{6,0},{7,1},{8,14},{9,15},{10,... | collective-permute-start | bytes 884744 | tf_op jit(solution)/shard_map/ppermute | solution.py:1140
  277.4 27.6 %collective-permute-start.18 = (bf16[96,1536]{1,0:T(8,128)(2,1)}, bf16[96,1536]{1,0:T(8,128)(2,1)S(1)}, u32[]{:S(2)}, u32[]{:S(2)}) collective-permute-start(bf16[96,1536]{1,0:T(8,128)(2,1)} %get-tuple-element.198.refs_10_), channel_id=1, source_target_pairs={{0,2},{1,3},{2,0},{3,1},{4,6},{5,7},{6,4},{7,5},{8,10},{9,11},{10,... | collective-permute-start | bytes 884744 | tf_op jit(solution)/shard_map/ppermute | solution.py:1140
  277.4 27.7 %collective-permute-start.19 = (bf16[96,1536]{1,0:T(8,128)(2,1)}, bf16[96,1536]{1,0:T(8,128)(2,1)S(1)}, u32[]{:S(2)}, u32[]{:S(2)}) collective-permute-start(bf16[96,1536]{1,0:T(8,128)(2,1)} %get-tuple-element.197.refs_9_), channel_id=1, source_target_pairs={{0,1},{1,0},{2,3},{3,2},{4,5},{5,4},{6,7},{7,6},{8,9},{9,8},{10,11... | collective-permute-start | bytes 884744 | tf_op jit(solution)/shard_map/ppermute | solution.py:1140
  278.4 26.7 %collective-permute-start.20 = (bf16[96,1536]{1,0:T(8,128)(2,1)}, bf16[96,1536]{1,0:T(8,128)(2,1)S(1)}, u32[]{:S(2)}, u32[]{:S(2)}) collective-permute-start(bf16[96,1536]{1,0:T(8,128)(2,1)} %get-tuple-element.199.refs_11_), channel_id=1, source_target_pairs={{0,3},{1,2},{2,1},{3,0},{4,7},{5,6},{6,5},{7,4},{8,11},{9,10},{10,... | collective-permute-start | bytes 884744 | tf_op jit(solution)/shard_map/ppermute | solution.py:1140
  306.1 58.9 %all-to-all-start.3 = ((bf16[8,96,1536]{2,1,0:T(8,128)(2,1)}), bf16[8,96,1536]{2,1,0:T(8,128)(2,1)}, u32[]{:S(2)}, u32[]{:S(2)}) async-start(bf16[8,96,1536]{2,1,0:T(8,128)(2,1)} %bitcast.133), calls=%async_computation.3 | async-start | bytes 4718592 | tf_op jit(solution)/shard_map/all_to_all | solution.py:1163
  314.5 37.6 %collective-permute-start.21 = (bf16[384,1024]{1,0:T(8,128)(2,1)}, bf16[384,1024]{1,0:T(8,128)(2,1)S(1)}, u32[]{:S(2)}, u32[]{:S(2)}) collective-permute-start(bf16[384,1024]{1,0:T(8,128)(2,1)} %convolution_convert_fusion.8), channel_id=1, source_target_pairs={{0,8},{8,0},{16,24},{24,16},{1,9},{9,1},{17,25},{25,17},{2,10},{10... | collective-permute-start | bytes 2359304 | tf_op jit(solution)/shard_map/ppermute | solution.py:1140
  317.4 36.0 %collective-permute-start.22 = (bf16[384,1024]{1,0:T(8,128)(2,1)}, bf16[384,1024]{1,0:T(8,128)(2,1)}, u32[]{:S(2)}, u32[]{:S(2)}) collective-permute-start(bf16[384,1024]{1,0:T(8,128)(2,1)} %convolution_convert_fusion.6), channel_id=1, source_target_pairs={{0,16},{8,24},{16,0},{24,8},{1,17},{9,25},{17,1},{25,9},{2,18},{10... | collective-permute-start | bytes 2359304 | tf_op jit(solution)/shard_map/ppermute | solution.py:1140
  321.2 40.9 %collective-permute-start.23 = (bf16[384,1024]{1,0:T(8,128)(2,1)}, bf16[384,1024]{1,0:T(8,128)(2,1)}, u32[]{:S(2)}, u32[]{:S(2)}) collective-permute-start(bf16[384,1024]{1,0:T(8,128)(2,1)} %convolution_convert_fusion.4), channel_id=1, source_target_pairs={{0,8},{8,0},{16,24},{24,16},{1,9},{9,1},{17,25},{25,17},{2,10},{10... | collective-permute-start | bytes 2359304 | tf_op jit(solution)/shard_map/ppermute | solution.py:1140
  325.2 36.8 %collective-permute-start.24 = (bf16[384,1024]{1,0:T(8,128)(2,1)}, bf16[384,1024]{1,0:T(8,128)(2,1)}, u32[]{:S(2)}, u32[]{:S(2)}) collective-permute-start(bf16[384,1024]{1,0:T(8,128)(2,1)} %convolution_convert_fusion.2), channel_id=1, source_target_pairs={{0,16},{8,24},{16,0},{24,8},{1,17},{9,25},{17,1},{25,9},{2,18},{10... | collective-permute-start | bytes 2359304 | tf_op jit(solution)/shard_map/ppermute | solution.py:1140
  376.2 23.8 %all-to-all-start.4 = ((bf16[8,192,256]{2,1,0:T(8,128)(2,1)}), bf16[8,192,256]{2,1,0:T(8,128)(2,1)S(1)}, u32[]{:S(2)}, u32[]{:S(2)}) async-start(bf16[8,192,256]{2,1,0:T(8,128)(2,1)} %bitcast.123), calls=%async_computation.4 | async-start | bytes 1572864 | tf_op jit(solution)/shard_map/all_to_all | solution.py:1163
  379.7 117.7 %reduce-scatter.2.cloned.1.call-start = ((), (), s32[]{:S(2)}) async-start(), calls=%async_computation.11 | async-start | bytes 3932160 | tf_op jit(solution)/shard_map/reduce_scatter | solution.py:1350
  379.8 19.5 %collective-permute-start.26 = (bf16[384,1024]{1,0:T(8,128)(2,1)}, bf16[384,1024]{1,0:T(8,128)(2,1)}, u32[]{:S(2)}, u32[]{:S(2)}) collective-permute-start(bf16[384,1024]{1,0:T(8,128)(2,1)} %add_convert_fusion.2), channel_id=1, source_target_pairs={{0,16},{8,24},{16,0},{24,8},{1,17},{9,25},{17,1},{25,9},{2,18},{10... | collective-permute-start | bytes 2359304 | tf_op jit(solution)/shard_map/ppermute | solution.py:1140
  380.9 19.1 %collective-permute-start.27 = (bf16[384,1024]{1,0:T(8,128)(2,1)}, bf16[384,1024]{1,0:T(8,128)(2,1)}, u32[]{:S(2)}, u32[]{:S(2)}) collective-permute-start(bf16[384,1024]{1,0:T(8,128)(2,1)} %add_convert_fusion.1), channel_id=1, source_target_pairs={{0,8},{8,0},{16,24},{24,16},{1,9},{9,1},{17,25},{25,17},{2,10},{10... | collective-permute-start | bytes 2359304 | tf_op jit(solution)/shard_map/ppermute | solution.py:1140
  403.4 43.5 %collective-permute-start.28 = (bf16[2,384,768]{2,1,0:T(8,128)(2,1)}, bf16[2,384,768]{2,1,0:T(8,128)(2,1)}, u32[]{:S(2)}, u32[]{:S(2)}) collective-permute-start(bf16[2,384,768]{2,1,0:T(8,128)(2,1)} %slice.97), channel_id=1, source_target_pairs={{0,16},{8,24},{16,0},{24,8},{1,17},{9,25},{17,1},{25,9},{2,18},{10... | collective-permute-start | bytes 3538952 | tf_op jit(solution)/shard_map/ppermute | solution.py:1140
  404.3 39.5 %collective-permute-start.29 = (bf16[96,1536]{1,0:T(8,128)(2,1)}, bf16[96,1536]{1,0:T(8,128)(2,1)}, u32[]{:S(2)}, u32[]{:S(2)}) collective-permute-start(bf16[96,1536]{1,0:T(8,128)(2,1)} %get-tuple-element.234.refs_13_), channel_id=1, source_target_pairs={{0,5},{1,4},{2,7},{3,6},{4,1},{5,0},{6,3},{7,2},{8,13},{9,12},{10,... | collective-permute-start | bytes 884744 | tf_op jit(solution)/shard_map/ppermute | solution.py:1140
  407.3 36.4 %collective-permute-start.30 = (bf16[96,1536]{1,0:T(8,128)(2,1)}, bf16[96,1536]{1,0:T(8,128)(2,1)}, u32[]{:S(2)}, u32[]{:S(2)}) collective-permute-start(bf16[96,1536]{1,0:T(8,128)(2,1)} %get-tuple-element.235.refs_15_), channel_id=1, source_target_pairs={{0,7},{1,6},{2,5},{3,4},{4,3},{5,2},{6,1},{7,0},{8,15},{9,14},{10,... | collective-permute-start | bytes 884744 | tf_op jit(solution)/shard_map/ppermute | solution.py:1140
  446.8 44.6 %all-to-all-start.5 = ((bf16[8,320,256]{2,1,0:T(8,128)(2,1)}), bf16[8,320,256]{2,1,0:T(8,128)(2,1)}, u32[]{:S(2)}, u32[]{:S(2)}) async-start(bf16[8,320,256]{2,1,0:T(8,128)(2,1)} %copy-done.14), calls=%async_computation.5 | async-start | bytes 2621440 | tf_op jit(solution)/shard_map/all_to_all | solution.py:1163
  455.8 30.9 %collective-permute-start.31 = (bf16[384,768]{1,0:T(8,128)(2,1)S(1)}, bf16[384,768]{1,0:T(8,128)(2,1)S(1)}, u32[]{:S(2)}, u32[]{:S(2)}) collective-permute-start(bf16[384,768]{1,0:T(8,128)(2,1)S(1)} %fusion.12), channel_id=1, source_target_pairs={{0,8},{8,0},{16,24},{24,16},{1,9},{9,1},{17,25},{25,17},{2,10},{10... | collective-permute-start | bytes 1769480 | tf_op jit(solution)/shard_map/ppermute | solution.py:1140
  463.3 17.0 %collective-permute-start.37 = (bf16[384,384]{1,0:T(8,128)(2,1)S(1)}, bf16[384,384]{1,0:T(8,128)(2,1)S(1)}, u32[]{:S(2)}, u32[]{:S(2)}) collective-permute-start(bf16[384,384]{1,0:T(8,128)(2,1)S(1)} %get-tuple-element.325), channel_id=1, source_target_pairs={{0,24},{8,16},{16,8},{24,0},{1,25},{9,17},{17,9},{25,1},{2,26},{10... | collective-permute-start | bytes 884744 | tf_op jit(solution)/shard_map/ppermute | solution.py:1140
  465.3 15.0 %collective-permute-start.36 = (bf16[384,384]{1,0:T(8,128)(2,1)S(1)}, bf16[384,384]{1,0:T(8,128)(2,1)S(1)}, u32[]{:S(2)}, u32[]{:S(2)}) collective-permute-start(bf16[384,384]{1,0:T(8,128)(2,1)S(1)} %get-tuple-element.326), channel_id=1, source_target_pairs={{0,16},{8,24},{16,0},{24,8},{1,17},{9,25},{17,1},{25,9},{2,18},{10... | collective-permute-start | bytes 884744 | tf_op jit(solution)/shard_map/ppermute | solution.py:1140
  466.0 19.7 %collective-permute-start.35 = (bf16[384,384]{1,0:T(8,128)(2,1)S(1)}, bf16[384,384]{1,0:T(8,128)(2,1)S(1)}, u32[]{:S(2)}, u32[]{:S(2)}) collective-permute-start(bf16[384,384]{1,0:T(8,128)(2,1)S(1)} %get-tuple-element.324), channel_id=1, source_target_pairs={{0,8},{8,0},{16,24},{24,16},{1,9},{9,1},{17,25},{25,17},{2,10},{10... | collective-permute-start | bytes 884744 | tf_op jit(solution)/shard_map/ppermute | solution.py:1140
  487.8 19.1 %collective-permute-start.32 = (bf16[96,768]{1,0:T(8,128)(2,1)S(1)}, bf16[96,768]{1,0:T(8,128)(2,1)S(1)}, u32[]{:S(2)}, u32[]{:S(2)}) collective-permute-start(bf16[96,768]{1,0:T(8,128)(2,1)S(1)} %get-tuple-element.337), channel_id=1, source_target_pairs={{0,2},{1,3},{2,0},{3,1},{4,6},{5,7},{6,4},{7,5},{8,10},{9,11},{10,... | collective-permute-start | bytes 442376 | tf_op jit(solution)/shard_map/ppermute | solution.py:1140
  489.0 18.0 %collective-permute-start.33 = (bf16[96,768]{1,0:T(8,128)(2,1)S(1)}, bf16[96,768]{1,0:T(8,128)(2,1)S(1)}, u32[]{:S(2)}, u32[]{:S(2)}) collective-permute-start(bf16[96,768]{1,0:T(8,128)(2,1)S(1)} %get-tuple-element.336), channel_id=1, source_target_pairs={{0,4},{1,5},{2,6},{3,7},{4,0},{5,1},{6,2},{7,3},{8,12},{9,13},{10,... | collective-permute-start | bytes 442376 | tf_op jit(solution)/shard_map/ppermute | solution.py:1140
  491.1 15.9 %collective-permute-start.34 = (bf16[96,768]{1,0:T(8,128)(2,1)S(1)}, bf16[96,768]{1,0:T(8,128)(2,1)S(1)}, u32[]{:S(2)}, u32[]{:S(2)}) collective-permute-start(bf16[96,768]{1,0:T(8,128)(2,1)S(1)} %get-tuple-element.335), channel_id=1, source_target_pairs={{0,6},{1,7},{2,4},{3,5},{4,2},{5,3},{6,0},{7,1},{8,14},{9,15},{10,... | collective-permute-start | bytes 442376 | tf_op jit(solution)/shard_map/ppermute | solution.py:1140
  491.5 19.5 %all-to-all-start.6 = ((bf16[8,48,384]{2,1,0:T(8,128)(2,1)}), bf16[8,48,384]{2,1,0:T(8,128)(2,1)S(1)}, u32[]{:S(2)}, u32[]{:S(2)}) async-start(bf16[8,48,384]{2,1,0:T(8,128)(2,1)} %bitcast.45), calls=%async_computation.7 | async-start | bytes 589824 | tf_op jit(solution)/shard_map/all_to_all | solution.py:1163
  512.0 6.4 %collective-permute-start.38 = (f32[48,768]{1,0:T(8,128)S(1)}, f32[48,768]{1,0:T(8,128)S(1)}, u32[]{:S(2)}, u32[]{:S(2)}) collective-permute-start(f32[48,768]{1,0:T(8,128)S(1)} %get-tuple-element.339), channel_id=1, source_target_pairs={{0,1},{1,0},{2,3},{3,2},{4,5},{5,4},{6,7},{7,6},{8,9},{9,8},{10,11... | collective-permute-start | bytes 442376 | tf_op jit(solution)/shard_map/ppermute | solution.py:1140
  (69 other events, 431.3 us)
Sparse Core Ops, SparseCore 0:
  9.7 75.5 all-gather.11
  88.2 77.6 all-gather.5
  179.6 57.7 all-gather.7
  247.0 91.9 all-gather.9
  401.0 62.2 reduce-scatter.1

commit v4 on v3

--- a/solution.py
+++ b/solution.py
@@ -1016,33 +1016,79 @@
     )(middle, cot, home, weight, head_weights, slots)
 
 
-def weight_kernel(place, normed_ref, grads_ref, extra_ref, out_ref):
+def weight_kernel(place, normed_ref, grads_ref, router_ref, gain_ref, out_ref):
     total = jnp.dot(grads_ref[...], normed_ref[...], preferred_element_type=jnp.float32)
-    out_ref[0] = jnp.concatenate([total, extra_ref[...]], 0).T.astype(jnp.bfloat16)
-
-
-def weight_terms(place, normed, grads, extra, parts):
+    wide, span = total.shape
+    rest = jnp.zeros((out_ref.shape[2] - wide - router_ref.shape[0] - 8, span), jnp.float32)
+    gain = jnp.concatenate([gain_ref[...], jnp.zeros((7, span), jnp.float32)], 0)
+    out_ref[0] = jnp.concatenate([total, router_ref[...], gain, rest], 0).T.astype(jnp.bfloat16)
+
+
+def weight_terms(place, normed, grads, router, gain, router_lane, experts, lanes, parts):
     length, width = normed.shape
     wide = grads.shape[0]
     span = width // parts
-    lanes = wide + extra.shape[0]
-    near = lambda k, place: (0, jnp.bitwise_xor(place[0], k))
+    near = lambda row: lambda k, place: (row, jnp.bitwise_xor(place[0], k))
     return pl.pallas_call(
         weight_kernel,
         grid_spec=pltpu.PrefetchScalarGridSpec(
             num_scalar_prefetch=1,
             grid=(parts,),
             in_specs=[
-                pl.BlockSpec((length, span), near),
+                pl.BlockSpec((length, span), near(0)),
                 pl.BlockSpec((wide, length), lambda k, place: (0, 0)),
-                pl.BlockSpec((extra.shape[0], span), near),
+                pl.BlockSpec((experts, span), near(router_lane // experts)),
+                pl.BlockSpec((1, span), near(0)),
             ],
             out_specs=pl.BlockSpec((1, span, lanes), lambda k, place: (k, 0, 0)),
         ),
         out_shape=jax.ShapeDtypeStruct((parts, span, lanes), jnp.bfloat16),
         compiler_params=pltpu.CompilerParams(vmem_limit_bytes=40 * 2**20),
         name="weight_terms",
-    )(place, normed, grads, extra)
+    )(place, normed, grads, router, gain)
+
+
+def tokens_back_kernel(
+    lane, start_ref, middle_ref, grads_ref, weight_ref, table_ref, out_ref, total
+):
+    step = pl.program_id(0)
+
+    @pl.when(step == 0)
+    def _():
+        total[...] = jnp.zeros_like(total)
+
+    grads = jnp.concatenate([grads_ref[0], grads_ref[1]], 0).T
+    total[...] += contract(grads, weight_ref[...], 1, 1)
+
+    @pl.when(step == pl.num_programs(0) - 1)
+    def _():
+        unit, factor = unit_of(start_ref[...].astype(jnp.float32))
+        scaled = total[...] * column_as_row(table_ref[...], lane)
+        inner_part = factor * (scaled - unit * jnp.mean(scaled * unit, -1, keepdims=True))
+        out_ref[...] = middle_ref[...] + inner_part
+
+
+def tokens_back(start, grad_middle, grads, weight, head_weights, lane):
+    rows, width = start.shape
+    count, cols, _ = grads.shape
+    lanes = head_weights.shape[1]
+    whole = lambda shape: pl.BlockSpec(shape, lambda i: (0, 0))
+    return pl.pallas_call(
+        functools.partial(tokens_back_kernel, lane),
+        grid=(count // 2,),
+        in_specs=[
+            whole(start.shape),
+            whole(grad_middle.shape),
+            pl.BlockSpec((2, cols, rows), lambda i: (i, 0, 0)),
+            pl.BlockSpec((width, 2 * cols), lambda i: (0, i)),
+            pl.BlockSpec((width, 128), lambda i: (0, lanes // 128 - 1)),
+        ],
+        out_specs=whole((rows, width)),
+        out_shape=jax.ShapeDtypeStruct((rows, width), jnp.float32),
+        scratch_shapes=[pltpu.VMEM((rows, width), jnp.float32)],
+        compiler_params=pltpu.CompilerParams(vmem_limit_bytes=32 * 2**20),
+        name="tokens_back",
+    )(start, grad_middle, grads, weight, head_weights)
 
 
 def mixture_kernel(slots_ref, gates_ref, middle_ref, *refs):
@@ -1072,7 +1118,7 @@
 
 
 def weight_grads_kernel(
-    share, home_ref, query_weight_ref, keyval_weight_ref, gain_ref,
+    share, home_ref, query_weight_ref, keyval_weight_ref,
     query_ref, keyval_ref, router_ref, gains_ref,
 ):
     count = home_ref.shape[0]
@@ -1091,11 +1137,11 @@
     products = jnp.sum(
         query_ref[...] * query_weight_ref[...].astype(jnp.float32), 1, keepdims=True
     ) + jnp.sum(keyval_ref[...] * keyval_weight_ref[...].astype(jnp.float32), 1, keepdims=True)
-    gains_ref[:, 0:1] = products / gain_ref[...].astype(jnp.float32)
+    gains_ref[:, 0:1] = products
     gains_ref[:, 1:2] = small[:, experts : experts + 1]
 
 
-def weight_grads(home, query_weight, keyval_weight, gain, share, experts):
+def weight_grads(home, query_weight, keyval_weight, share, experts):
     shape = lambda width: jax.ShapeDtypeStruct((query_weight.shape[0], width), jnp.float32)
     return pl.pallas_call(
         functools.partial(weight_grads_kernel, share),
@@ -1107,7 +1153,7 @@
         ],
         compiler_params=pltpu.CompilerParams(vmem_limit_bytes=40 * 2**20),
         name="weight_grads",
-    )(home, query_weight, keyval_weight, gain)
+    )(home, query_weight, keyval_weight)
 
 
 def sum_pairs_kernel(*refs):
@@ -1257,19 +1303,23 @@
     head_weights = in_order([head_rows] + head_near, "dp").reshape(width, lanes)
     cot_sent = spread_rows(slots_near, cot_low, capacity, experts)
 
-    by_head_line = by_head.reshape(shard, count * cols)
-    tokens_all, cot_sent, head_weights, by_head_line, output_own = after(
-        (tokens_all, cot_sent, head_weights, by_head_line, output_weight.T)
-    )
-    output_all = gather(output_own, ("dp", "fsdp"))
-    normed, projected = project(tokens_all, head_weights, cols, first_lane, rows)
-    cot_first = swap_near_blocks(cot_sent, (4, 6, 2))
     firsts = segments.reshape(count, rows)
     starts = jnp.sum(segments[None, :] < firsts[:, :1], 1) // rows
     wholes = (jnp.sum(segments[None, :] < firsts[:, -1:], 1) + rows - 1) // rows
     wholes = jnp.minimum(wholes, jnp.arange(count))
     spans = jnp.stack([starts, wholes]).astype(jnp.int32)
     seg_row, seg_col = segments.reshape(1, length), segments.reshape(length, 1)
+
+    by_head_line = by_head.reshape(shard, count * cols)
+    tokens_all, cot_sent, head_weights, by_head_line, output_own, spans, seg_row, seg_col = after(
+        (
+            tokens_all, cot_sent, head_weights, by_head_line, output_weight.T, spans, seg_row,
+            seg_col,
+        )
+    )
+    output_all = gather(output_own, ("dp", "fsdp"))
+    normed, projected = project(tokens_all, head_weights, cols, first_lane, rows)
+    cot_first = swap_near_blocks(cot_sent, (4, 6, 2))
     mixed_head, mixed_exact, totals = attend(spans, projected, seg_row, seg_col)
     mixed_head, cot_first, by_head_line = after((mixed_head, cot_first, by_head_line))
     project_line = gather(by_head_line, "fsdp")
@@ -1354,35 +1404,35 @@
     grads_blocks, grads_line = attend_backward(
         spans, projected, mixed_grad, seg_row, seg_col, mixed_exact, totals
     )
-    grads_blocks, grads_line, output_part, output_near, part_last = after(
-        (grads_blocks, grads_line, output_part, output_near, part_last)
-    )
+    grads_blocks, grads_line, part_last = after((grads_blocks, grads_line, part_last))
     part_home = [parts[0], part_first[3], part_first[2], part_first[4]]
     part_home = part_home + [part_first[0], part_last[0], part_first[1], part_last[1]]
-    grad_mine = all_to_all(grads_blocks).reshape(count * cols, rows)
-    extra = jnp.concatenate(
-        [router_part[router_lane : router_lane + experts], gain_part,
-         jnp.zeros((lanes - cols - experts - 1, width), f32)]
-    )
+    grad_mine = all_to_all(grads_blocks)
+    own_group = group.reshape(1).astype(jnp.int32)
+    terms = weight_terms(
+        own_group, normed, grads_line, router_part, gain_part, router_lane, experts, lanes, 4
+    )
+    terms, output_part, output_near = after((terms, output_part, output_near))
     output_sum = output_part[:2].astype(f32) + output_near.astype(f32)
-    output_passed = output_sum[1].astype(low)
-    output_side = flip_exchange(output_passed, "dp", 1)
-    grads_line = after(grads_line, output_passed)
-    own_group = group.reshape(1).astype(jnp.int32)
-    terms = weight_terms(own_group, normed, grads_line, extra, 4)
-    weight_sum = terms[0].astype(f32)
-    for k in range(1, 4):
-        weight_sum = weight_sum + flip_exchange(terms[k], "dp", k).astype(f32)
-    block_out = mixture(slots_near, gates, middle, part_home)
     inner_grad = sum_pairs(
         [gate_terms[0], near_a, side_a], [up_terms[0], near_b, side_b], size // 4
     )
     outer_grad = outer_sum.astype(f32)
-    grad_normed = contract(
-        after(grad_mine, inner_grad, outer_grad, block_out), project_all, 0, 1
+    block_out = mixture(slots_near, gates, middle, after(part_home, outer_grad))
+    weights_near = after(
+        [flip_exchange(terms[k], "dp", k) for k in range(1, 4)], inner_grad, block_out
+    )
+    weight_sum = terms[0].astype(f32)
+    for near in weights_near:
+        weight_sum = weight_sum + near.astype(f32)
+    weight_sum, output_passed = after((weight_sum.astype(low), output_sum[1].astype(low)))
+    output_side = flip_exchange(output_passed, "dp", 1)
+    tokens_grad = tokens_back(
+        start_low, grad_middle, after(grad_mine, inner_grad, outer_grad, block_out), project_all,
+        head_weights, first_lane,
     )
     output_sum = output_sum[0] + output_side.astype(f32)
-    weight_sum = after(weight_sum.astype(low), grad_mine)
+    weight_sum = after(weight_sum, grad_mine)
     weight_home = all_to_all(weight_sum.reshape(count, shard, lanes))
     chips, pair = count // 2, 2 * shard
     output_low = output_sum.astype(low)
@@ -1394,11 +1444,11 @@
     output_line = [
         flip_exchange(line_part(output_low, k), "fsdp", 2 * k) for k in range(1, chips)
     ]
-    output_line, weight_home = after((output_line, weight_home), block_out, outer_grad)
+    output_line, weight_home = after((output_line, weight_home), tokens_grad)
     query_grad, keyval_grad, router_grad, gains = weight_grads(
-        weight_home, query_weight, key_value_weight, gain_before[:, None], share, experts
-    )
-    before_grad, middle_grad = gains[:, 0], gains[:, 1]
+        weight_home, query_weight, key_value_weight, share, experts
+    )
+    before_grad, middle_grad = gains[:, 0] / gain_before.astype(f32), gains[:, 1]
     output_grad = line_part(output_sum, 0)
     for near in output_line:
         output_grad = output_grad + near.astype(f32)
@@ -1411,10 +1461,6 @@
         jnp.concatenate([own_half, other_half], 1),
         jnp.concatenate([other_half, own_half], 1),
     ).T
-    gain_first = head_weights[:, table_lane + first_lane]
-    _, unit_first, factor_first = normalize(start_low.astype(f32), gain_first)
-    outer_back, _ = normalize_back(grad_normed, unit_first, factor_first, gain_first)
-    tokens_grad = grad_middle + outer_back
     return (
         block_out[None],
         tokens_grad[None],

time: 536 us -> 532 us (level)
  blocking collectives: 67.1 us -> 35.4 us
  waiting for transfers between devices: 141 us -> 159 us
  matrix products: 41.1 us -> 34.1 us
  Pallas kernels: 132 us -> 139 us
  starting transfers between devices: 65.9 us -> 72.9 us
  local copies, waits for them, and re-layouts: 29.5 us -> 35.5 us
    all_to_all x2 -> x1, blocking collectives: 67.1 us -> 35.4 us  [all_to_all(): lax.all_to_all(blocks, 'fsdp', split_axis=0, concat_axis=0, tiled=True)]
    all_to_all x5 -> x6, waiting for transfers between devices: 16.3 us -> 31.5 us  [all_to_all(): lax.all_to_all(blocks, 'fsdp', split_axis=0, concat_axis=0, tiled=True)]
    dot_general x15 -> x14, matrix products: 40.7 us -> 33.8 us  [contract(): lax.dot_general(left, right, (((left_axis,), (right_axis,)), ((), ())), p...]
    pallas_call x0 -> x1, Pallas kernels: none -> 6.58 us  [tokens_back(): pl.pallas_call(functools.partial(tokens_back_kernel, lane), grid=(count /...]
    all_to_all x5 -> x6, starting transfers between devices: 25.7 us -> 30.9 us  [all_to_all(): lax.all_to_all(blocks, 'fsdp', split_axis=0, concat_axis=0, tiled=True)]
    unnamed x140 -> x130, local copies, waits for them, and re-layouts: 18.9 us -> 22.6 us
  transfers between devices with their start and end apart: 49 -> 50, of which waited for: 16 -> 16; matrix products, arithmetic and copies ran while one was open for 16% -> 15% of each run, Pallas kernels for 23% -> 24%
where the time goes in v4:
time: 532 us; the launch traced here: 523 us
  waiting for transfers between devices  159 us (30%)
  Pallas kernels  139 us (26%)
  starting transfers between devices  72.9 us (14%)
  local copies, waits for them, and re-layouts  35.5 us (7%)
  blocking collectives  35.4 us (7%)
  matrix products  34.1 us (6%)
  other arithmetic  31.9 us (6%)
  between operations  15.1 us (3%)
    all_gather x4, waiting for transfers between devices, gather(): return lax.all_gather(block, axis, axis=0, tiled=True)  66.2 us
    ppermute x39, waiting for transfers between devices, flip_exchange(): return lax.ppermute(block, axis, [(i, i ^ flip) for i in range(count)])  59.4 us
    ppermute x39, starting transfers between devices, flip_exchange(): return lax.ppermute(block, axis, [(i, i ^ flip) for i in range(count)])  41.9 us
    all_to_all x1, blocking collectives, all_to_all(): lax.all_to_all(blocks, 'fsdp', split_axis=0, concat_axis=0, tiled=True)  35.4 us
    dot_general x14, matrix products, contract(): lax.dot_general(left, right, (((left_axis,), (right_axis,)), ((), ())), p...  33.8 us
    all_to_all x6, waiting for transfers between devices, all_to_all(): lax.all_to_all(blocks, 'fsdp', split_axis=0, concat_axis=0, tiled=True)  31.5 us
    all_to_all x6, starting transfers between devices, all_to_all(): lax.all_to_all(blocks, 'fsdp', split_axis=0, concat_axis=0, tiled=True)  30.9 us
    pallas_call x1, Pallas kernels, attend_backward(): pl.pallas_call(attend_back_kernel, grid_spec=pltpu.PrefetchScalarGridSpec...  25.6 us
  transfers between devices with their start and end apart: 50, of which 16 were waited for; matrix products, arithmetic and copies ran while one was open for 15% of the time, Pallas kernels for 24%

profile of v4, /device:TPU:1, one launch (start us, length us, event | category | flops | bytes accessed | tf_op | source)
XLA Modules:
  0.0 522.8 jit_solution(8800666068388070148)
XLA Ops:
  8.0 3.1 copy.74
  17.6 6.9 %all-to-all-start = ((bf16[8,64,384]{2,1,0:T(8,128)(2,1)}), bf16[8,64,384]{2,1,0:T(8,128)(2,1)}, u32[]{:S(2)}, u32[]{:S(2)}) async-start(bf16[8,64,384]{2,1,0:T(8,128)(2,1)} %copy.67), calls=%async_computation | async-start | bytes 786432 | tf_op jit(solution)/shard_map/all_to_all | solution.py:1209
  28.0 19.1 %all-to-all-done = bf16[8,64,384]{2,1,0:T(8,128)(2,1)} async-done(((bf16[8,64,384]{2,1,0:T(8,128)(2,1)}), bf16[8,64,384]{2,1,0:T(8,128)(2,1)}, u32[]{:S(2)}, u32[]{:S(2)}) %all-to-all-start) | async-done | bytes 393248 | tf_op jit(solution)/shard_map/all_to_all | solution.py:1209
  47.2 17.2 %collective-permute-done.2.refs_9_.refs_29_ = bf16[1024,384]{1,0:T(8,128)(2,1)} collective-permute-done((bf16[1024,384]{1,0:T(8,128)(2,1)S(1)}, bf16[1024,384]{1,0:T(8,128)(2,1)}, u32[]{:S(2)}, u32[]{:S(2)}) %collective-permute-start.2) | collective-permute-done | bytes 786464 | tf_op jit(solution)/shard_map/ppermute | solution.py:1186
  70.2 3.8 collective-permute-done.6
  74.0 8.5 %collective-permute-done.5 = bf16[384,384]{1,0:T(8,128)(2,1)S(1)} collective-permute-done((bf16[384,384]{1,0:T(8,128)(2,1)S(1)}, bf16[384,384]{1,0:T(8,128)(2,1)S(1)}, u32[]{:S(2)}, u32[]{:S(2)}) %collective-permute-start.5) | collective-permute-done | bytes 294944 | tf_op jit(solution)/shard_map/ppermute | solution.py:1186
  88.3 10.5 %project.1 = (bf16[2048,1536]{1,0:T(8,128)(2,1)}, bf16[8,320,256]{2,1,0:T(8,128)(2,1)}) custom-call(bf16[2048,1536]{1,0:T(8,128)(2,1)} %bitcast.121, bf16[1536,384]{1,0:T(8,128)(2,1)} %bitcast.105, bf16[1536,384]{1,0:T(8,128)(2,1)} %bitcast.106), custom_call_target="tpu_custom_call" | custom-call | tf_op jit(solution)/shard_map/project/pallas_call | solution.py:483
  100.2 21.4 %attend.1 = (bf16[8,192,256]{2,1,0:T(8,128)(2,1)S(1)}, f32[8,192,256]{2,1,0:T(8,128)S(1)}, f32[8,8,256]{2,1,0:T(8,128)S(1)}) custom-call(s32[2,8]{1,0:T(2,128)S(1)} %pad_add_fusion.spans, bf16[8,320,256]{2,1,0:T(8,128)(2,1)S(1)} %copy-done.1, bf16[8,320,256]{2,1,0:T(8,128)(2,1)S(1)} %copy-done.1, s32[1,2048]{1,0:T(1,128)S(1)} %bitcast.119, ...), custom_call_target="tpu_custom_call" | custom-call | tf_op jit(solution)/shard_map/attend/pallas_call | solution.py:567
  122.7 35.4 %all_to_all.49 = bf16[8,192,256]{2,1,0:T(8,128)(2,1)} all-to-all(bf16[8,192,256]{2,1,0:T(8,128)(2,1)S(1)} %get-tuple-element.174), channel_id=1, replica_groups=mesh['dp'=4,'fsdp'=8] {'fsdp'}, dimensions={0} | all-to-all | bytes 1572864 | tf_op jit(solution)/shard_map/all_to_all | solution.py:1209
  158.1 7.1 %all-gather.6.cloned.1.call-done.weight_ref = bf16[1536,1536]{1,0:T(8,128)(2,1)} async-done(((bf16[48,1536]{1,0:T(8,128)(2,1)}), bf16[1536,1536]{1,0:T(8,128)(2,1)}) %all-gather.6.cloned.1.call-update) | async-done | bytes 4718608 | tf_op jit(solution)/shard_map/all_gather | solution.py:1213
  165.1 6.7 %middle.1 = (f32[256,1536]{1,0:T(8,128)}, bf16[768,1536]{1,0:T(8,128)(2,1)}, f32[2,256]{1,0:T(2,128)}) custom-call(bf16[256,1536]{1,0:T(8,128)(2,1)} %bitcast.112, bf16[1536,256]{1,0:T(8,128)(2,1)} %bitcast.122, bf16[1536,1536]{1,0:T(8,128)(2,1)} %all-gather.6.cloned.1.call-done.weight_ref, bf16[1536,384]{1,0:T(8,128)(2,1)} %bitcast.107, ...), custom_call_target="tpu_custom_call" | custom-call | tf_op jit(solution)/shard_map/middle/pallas_call | solution.py:738
  171.8 4.5 all-to-all-start.2
  178.7 57.9 %all-gather.8.cloned.1.call-done = bf16[384,2560]{1,0:T(8,128)(2,1)} async-done(((bf16[48,2560]{1,0:T(8,128)(2,1)}), bf16[384,2560]{1,0:T(8,128)(2,1)}) %all-gather.8.cloned.1.call-update) | async-done | bytes 1966096 | tf_op jit(solution)/shard_map/all_gather | solution.py:1213
  236.6 9.4 %all-to-all-done.2 = bf16[8,96,1536]{2,1,0:T(8,128)(2,1)} async-done(((bf16[8,96,1536]{2,1,0:T(8,128)(2,1)}), bf16[8,96,1536]{2,1,0:T(8,128)(2,1)}, u32[]{:S(2)}, u32[]{:S(2)}) %all-to-all-start.2) | async-done | bytes 2359328 | tf_op jit(solution)/shard_map/all_to_all | solution.py:1209
  252.3 18.4 %expert.1 = (f32[768,1024]{1,0:T(8,128)}, f32[768,1024]{1,0:T(8,128)}, bf16[768,1024]{1,0:T(8,128)(2,1)}, f32[768,128]{1,0:T(8,128)}, bf16[96,1536]{1,0:T(8,128)...) custom-call(s32[2]{0:T(128)} %pad_add_fusion.1.own_ref, ...), custom_call_target="tpu_custom_call" | custom-call | tf_op jit(solution)/shard_map/expert/pallas_call | solution.py:827
  270.7 4.5 collective-permute-start.16
  279.2 24.9 %expert_backward.1 = (bf16[768,1024]{1,0:T(8,128)(2,1)}, bf16[768,1024]{1,0:T(8,128)(2,1)}, bf16[768,1536]{1,0:T(8,128)(2,1)}, bf16[768,1536]{1,0:T(8,128)(2,1)}, f32[128,1536]{1,0:T(8,128)}) custom-call(s32[2]{0:T(128)} %pad_add_fusion.1.own_ref, bf16[96,1536]{1,0:T(8,128)(2,1)} %copy-done.37, bf16[96,1536]{1,0:T(8,128)(2,1)} %collective-permute-done.15.refs_1_, ...), custom_call_target="tpu_custom_call" | custom-call | tf_op jit(solution)/shard_map/expert_backward/pallas_call | solution.py:922
  305.1 5.0 all-to-all-start.3
  310.1 3.4 convolution_convert_fusion.8
  313.5 2.9 convolution_convert_fusion.6
  317.4 2.7 convolution_convert_fusion.4
  321.2 2.8 convolution_convert_fusion.2
  324.7 3.1 convolution_convert_fusion.9
  331.9 11.0 %pad_maximum_fusion = bf16[4096,384]{1,0:T(8,128)(2,1)} fusion(bf16[1024,384]{1,0:T(8,128)(2,1)S(1)} %convolution_convert_fusion.10, bf16[1024,384]{1,0:T(8,128)(2,1)S(1)} %convolution_convert_fusion.11, bf16[1024,384]{1,0:T(8,128)(2,1)S(1)} %convolution_convert_fusion.12, bf16[1024,384]{1,0:T(8,128)(2,1)S(1)} %convolution_convert_fusion.13), kind=kLoop, calls=%fused_computation.3 | loop fusion | flops 12582912 | bytes 6291456 | tf_op jit(solution)/shard_map/concatenate | solution.py:1371
  342.9 2.5 convolution_convert_fusion.7
  345.5 2.9 convolution_convert_fusion.5.refs_0_
  348.3 2.8 convolution_convert_fusion.3.refs_3_
  354.9 6.3 %collective-permute-done.23.refs_1_ = bf16[384,1024]{1,0:T(8,128)(2,1)} collective-permute-done((bf16[384,1024]{1,0:T(8,128)(2,1)}, bf16[384,1024]{1,0:T(8,128)(2,1)}, u32[]{:S(2)}, u32[]{:S(2)}) %collective-permute-start.23) | collective-permute-done | bytes 786464 | tf_op jit(solution)/shard_map/ppermute | solution.py:1186
  361.2 2.7 all-to-all-done.3
  364.0 6.3 %back.1 = (f32[256,1536]{1,0:T(8,128)S(1)}, bf16[256,1536]{1,0:T(8,128)(2,1)S(1)}, f32[1,1536]{1,0:T(1,128)S(1)}, bf16[1536,256]{1,0:T(8,128)(2,1)S(1)}) custom-call(f32[256,1536]{1,0:T(8,128)} %get-tuple-element.177.middle_ref, bf16[256,1536]{1,0:T(8,128)(2,1)S(1)} %bitcast.115, bf16[768,1536]{1,0:T(8,128)(2,1)} %bitcast.33.home_ref, ...), custom_call_target="tpu_custom_call" | custom-call | tf_op jit(solution)/shard_map/back/pallas_call | solution.py:991
  375.2 3.5 all-to-all-start.4
  379.9 4.4 add_convert_fusion
  384.3 14.0 %collective-permute-done.26.refs_2_ = bf16[384,1024]{1,0:T(8,128)(2,1)} collective-permute-done((bf16[384,1024]{1,0:T(8,128)(2,1)}, bf16[384,1024]{1,0:T(8,128)(2,1)}, u32[]{:S(2)}, u32[]{:S(2)}) %collective-permute-start.26) | collective-permute-done | bytes 786464 | tf_op jit(solution)/shard_map/ppermute | solution.py:1186
  398.9 2.5 slice.91
  402.1 3.4 collective-permute-start.28
  407.9 25.6 %attend_backward.1 = (bf16[8,320,256]{2,1,0:T(8,128)(2,1)S(1)}, bf16[320,2048]{1,0:T(8,128)(2,1)S(1)}) custom-call(s32[2,8]{1,0:T(2,128)S(1)} %pad_add_fusion.spans, bf16[8,320,256]{2,1,0:T(8,128)(2,1)S(1)} %copy-done.2, bf16[8,192,256]{2,1,0:T(8,128)(2,1)S(1)} %all-to-all-done.4.g_ref, bf16[8,320,256]{2,1,0:T(8,128)(2,1)S(1)} %copy-done.2, ...), custom_call_target="tpu_custom_call" | custom-call | tf_op jit(solution)/shard_map/attend_backward/pallas_call | solution.py:654
  436.0 5.0 all-to-all-start.5
  441.1 4.9 sum_pairs.1
  446.0 3.0 copy-done.5
  449.0 4.6 weight_terms.1
  457.3 3.0 convert_add_fusion
  466.1 6.0 %mixture.1 = bf16[256,1536]{1,0:T(8,128)(2,1)} custom-call(s32[2,256]{1,0:T(2,128)S(1)} %get-tuple-element.375.slots_ref, f32[2,256]{1,0:T(2,128)S(1)} %copy-done.40, f32[256,1536]{1,0:T(8,128)S(1)} %copy-done.6, bf16[96,1536]{1,0:T(8,128)(2,1)S(1)} %copy-done.16, bf16[96,1536]{1,0:T(8,128)(2,1)S(1)} %copy-done.30, bf16[96,1536]{1,0:T(8,128)(2,1)S(1)} %copy-done.28, ...), custom_call_target="tpu_custom_call" | custom-call | tf_op jit(solution)/shard_map/mixture/pallas_call | solution.py:1112
  474.6 6.0 %all-to-all-start.6 = ((bf16[8,48,384]{2,1,0:T(8,128)(2,1)}), bf16[8,48,384]{2,1,0:T(8,128)(2,1)}, u32[]{:S(2)}, u32[]{:S(2)}) async-start(bf16[8,48,384]{2,1,0:T(8,128)(2,1)} %bitcast.44), calls=%async_computation.7 | async-start | bytes 589824 | tf_op jit(solution)/shard_map/all_to_all | solution.py:1209
  480.6 8.1 %collective-permute-done.34 = bf16[384,768]{1,0:T(8,128)(2,1)} collective-permute-done((bf16[384,768]{1,0:T(8,128)(2,1)}, bf16[384,768]{1,0:T(8,128)(2,1)}, u32[]{:S(2)}, u32[]{:S(2)}) %collective-permute-start.34) | collective-permute-done | bytes 589856 | tf_op jit(solution)/shard_map/ppermute | solution.py:1186
  488.8 2.6 fusion.51
  495.7 3.2 copy-done.3
  498.9 6.6 %tokens_back.1 = f32[256,1536]{1,0:T(8,128)} custom-call(bf16[256,1536]{1,0:T(8,128)(2,1)S(1)} %bitcast.113, f32[256,1536]{1,0:T(8,128)S(1)} %copy-done.10, bf16[8,320,256]{2,1,0:T(8,128)(2,1)} %all-to-all-done.5.grads_ref, bf16[1536,2560]{1,0:T(8,128)(2,1)S(1)} %copy-done.3, bf16[1536,384]{1,0:T(8,128)(2,1)S(1)} %bitcast.111), custom_call_target="tpu_custom_call" | custom-call | tf_op jit(solution)/shard_map/tokens_back/pallas_call | solution.py:1076
  510.5 2.7 collective-permute-start.38
  (273 shorter events, 84.8 us)
Async XLA Ops:
  7.2 78.1 %all-gather.12.cloned.1.call-start = ((), (), s32[]{:S(2)}) async-start(), calls=%async_computation.12 | async-start | bytes 7077888 | tf_op jit(solution)/shard_map/all_gather | solution.py:1213
  11.0 54.2 %collective-permute-start = (bf16[384,2048]{1,0:T(8,128)(2,1)}, bf16[384,2048]{1,0:T(8,128)(2,1)}, u32[]{:S(2)}, u32[]{:S(2)}) collective-permute-start(bf16[384,2048]{1,0:T(8,128)(2,1)} %bitcast.49.refs_0_.refs_4_.refs_20_.refs_24_), channel_id=1, source_target_pairs={{0,8},{8,0},{16,24},{24,16},{1,9},{9,1},{17,25},{25,17},{2,10},{10... | collective-permute-start | bytes 4718600 | tf_op jit(solution)/shard_map/ppermute | solution.py:1186
  13.1 52.1 %collective-permute-start.1 = (bf16[384,2048]{1,0:T(8,128)(2,1)}, bf16[384,2048]{1,0:T(8,128)(2,1)}, u32[]{:S(2)}, u32[]{:S(2)}) collective-permute-start(bf16[384,2048]{1,0:T(8,128)(2,1)} %bitcast.49.refs_0_.refs_4_.refs_20_.refs_24_), channel_id=1, source_target_pairs={{0,16},{8,24},{16,0},{24,8},{1,17},{9,25},{17,1},{25,9},{2,18},{10... | collective-permute-start | bytes 4718600 | tf_op jit(solution)/shard_map/ppermute | solution.py:1186
  14.3 50.0 %collective-permute-start.2 = (bf16[1024,384]{1,0:T(8,128)(2,1)S(1)}, bf16[1024,384]{1,0:T(8,128)(2,1)}, u32[]{:S(2)}, u32[]{:S(2)}) collective-permute-start(bf16[1024,384]{1,0:T(8,128)(2,1)S(1)} %copy-done.41), channel_id=1, source_target_pairs={{0,8},{8,0},{16,24},{24,16},{1,9},{9,1},{17,25},{25,17},{2,10},{10... | collective-permute-start | bytes 2359304 | tf_op jit(solution)/shard_map/ppermute | solution.py:1186
  14.6 50.6 %collective-permute-start.3 = (bf16[1024,384]{1,0:T(8,128)(2,1)S(1)}, bf16[1024,384]{1,0:T(8,128)(2,1)}, u32[]{:S(2)}, u32[]{:S(2)}) collective-permute-start(bf16[1024,384]{1,0:T(8,128)(2,1)S(1)} %copy-done.41), channel_id=1, source_target_pairs={{0,16},{8,24},{16,0},{24,8},{1,17},{9,25},{17,1},{25,9},{2,18},{10... | collective-permute-start | bytes 2359304 | tf_op jit(solution)/shard_map/ppermute | solution.py:1186
  17.6 29.5 %all-to-all-start = ((bf16[8,64,384]{2,1,0:T(8,128)(2,1)}), bf16[8,64,384]{2,1,0:T(8,128)(2,1)}, u32[]{:S(2)}, u32[]{:S(2)}) async-start(bf16[8,64,384]{2,1,0:T(8,128)(2,1)} %copy.67), calls=%async_computation | async-start | bytes 786432 | tf_op jit(solution)/shard_map/all_to_all | solution.py:1209
  24.5 140.6 %all-gather.6.cloned.1.call-start = ((), (), s32[]{:S(2)}) async-start(), calls=%async_computation.8 | async-start | bytes 4866048 | tf_op jit(solution)/shard_map/all_gather | solution.py:1213
  66.2 7.8 %collective-permute-start.6 = (bf16[384,384]{1,0:T(8,128)(2,1)S(1)}, bf16[384,384]{1,0:T(8,128)(2,1)S(1)}, u32[]{:S(2)}, u32[]{:S(2)}) collective-permute-start(bf16[384,384]{1,0:T(8,128)(2,1)S(1)} %bitcast.131), channel_id=1, source_target_pairs={{0,24},{8,16},{16,8},{24,0},{1,25},{9,17},{17,9},{25,1},{2,26},{10... | collective-permute-start | bytes 884744 | tf_op jit(solution)/shard_map/ppermute | solution.py:1186
  67.6 15.0 %collective-permute-start.5 = (bf16[384,384]{1,0:T(8,128)(2,1)S(1)}, bf16[384,384]{1,0:T(8,128)(2,1)S(1)}, u32[]{:S(2)}, u32[]{:S(2)}) collective-permute-start(bf16[384,384]{1,0:T(8,128)(2,1)S(1)} %bitcast.132), channel_id=1, source_target_pairs={{0,16},{8,24},{16,0},{24,8},{1,17},{9,25},{17,1},{25,9},{2,18},{10... | collective-permute-start | bytes 884744 | tf_op jit(solution)/shard_map/ppermute | solution.py:1186
  67.8 14.7 %collective-permute-start.4 = (bf16[384,384]{1,0:T(8,128)(2,1)S(1)}, bf16[384,384]{1,0:T(8,128)(2,1)S(1)}, u32[]{:S(2)}, u32[]{:S(2)}) collective-permute-start(bf16[384,384]{1,0:T(8,128)(2,1)S(1)} %bitcast.133), channel_id=1, source_target_pairs={{0,8},{8,0},{16,24},{24,16},{1,9},{9,1},{17,25},{25,17},{2,10},{10... | collective-permute-start | bytes 884744 | tf_op jit(solution)/shard_map/ppermute | solution.py:1186
  85.3 37.4 %collective-permute-start.7 = (bf16[96,1536]{1,0:T(8,128)(2,1)}, bf16[96,1536]{1,0:T(8,128)(2,1)}, u32[]{:S(2)}, u32[]{:S(2)}) collective-permute-start(bf16[96,1536]{1,0:T(8,128)(2,1)} %get-tuple-element.170), channel_id=1, source_target_pairs={{0,4},{1,5},{2,6},{3,7},{4,0},{5,1},{6,2},{7,3},{8,12},{9,13},{10,... | collective-permute-start | bytes 884744 | tf_op jit(solution)/shard_map/ppermute | solution.py:1186
  86.4 36.3 %collective-permute-start.8 = (bf16[96,1536]{1,0:T(8,128)(2,1)}, bf16[96,1536]{1,0:T(8,128)(2,1)}, u32[]{:S(2)}, u32[]{:S(2)}) collective-permute-start(bf16[96,1536]{1,0:T(8,128)(2,1)} %get-tuple-element.171), channel_id=1, source_target_pairs={{0,6},{1,7},{2,4},{3,5},{4,2},{5,3},{6,0},{7,1},{8,14},{9,15},{10,... | collective-permute-start | bytes 884744 | tf_op jit(solution)/shard_map/ppermute | solution.py:1186
  87.5 35.2 %collective-permute-start.9 = (bf16[96,1536]{1,0:T(8,128)(2,1)S(1)}, bf16[96,1536]{1,0:T(8,128)(2,1)}, u32[]{:S(2)}, u32[]{:S(2)}) collective-permute-start(bf16[96,1536]{1,0:T(8,128)(2,1)S(1)} %get-tuple-element.172), channel_id=1, source_target_pairs={{0,2},{1,3},{2,0},{3,1},{4,6},{5,7},{6,4},{7,5},{8,10},{9,11},{10,... | collective-permute-start | bytes 884744 | tf_op jit(solution)/shard_map/ppermute | solution.py:1186
  171.8 74.3 %all-to-all-start.2 = ((bf16[8,96,1536]{2,1,0:T(8,128)(2,1)}), bf16[8,96,1536]{2,1,0:T(8,128)(2,1)}, u32[]{:S(2)}, u32[]{:S(2)}) async-start(bf16[8,96,1536]{2,1,0:T(8,128)(2,1)} %bitcast.126), calls=%async_computation.2 | async-start | bytes 4718592 | tf_op jit(solution)/shard_map/all_to_all | solution.py:1209
  176.3 60.3 %all-gather.8.cloned.1.call-start = ((), (), s32[]{:S(2)}) async-start(), calls=%async_computation.9 | async-start | bytes 2211840 | tf_op jit(solution)/shard_map/all_gather | solution.py:1213
  177.1 186.9 %all-gather.10.cloned.1.call-start = ((), (), s32[]{:S(2)}) async-start(), calls=%async_computation.10 | async-start | bytes 9830400 | tf_op jit(solution)/shard_map/all_gather | solution.py:1213
  177.1 59.5 %collective-permute-start.10 = (bf16[384,2048]{1,0:T(8,128)(2,1)}, bf16[384,2048]{1,0:T(8,128)(2,1)}, u32[]{:S(2)}, u32[]{:S(2)}) collective-permute-start(bf16[384,2048]{1,0:T(8,128)(2,1)} %collective-permute-done.refs_1_.refs_5_.refs_21_.refs_25_), channel_id=1, source_target_pairs={{0,16},{8,24},{16,0},{24,8},{1,17},{9,25},{17,1},{25,9},{2,18},{10... | collective-permute-start | bytes 4718600 | tf_op jit(solution)/shard_map/ppermute | solution.py:1186
  177.9 58.7 %collective-permute-start.11 = (bf16[1024,384]{1,0:T(8,128)(2,1)}, bf16[1024,384]{1,0:T(8,128)(2,1)}, u32[]{:S(2)}, u32[]{:S(2)}) collective-permute-start(bf16[1024,384]{1,0:T(8,128)(2,1)} %collective-permute-done.3.refs_10_.refs_30_), channel_id=1, source_target_pairs={{0,8},{8,0},{16,24},{24,16},{1,9},{9,1},{17,25},{25,17},{2,10},{10... | collective-permute-start | bytes 2359304 | tf_op jit(solution)/shard_map/ppermute | solution.py:1186
  246.1 24.6 %collective-permute-start.12 = (bf16[96,1536]{1,0:T(8,128)(2,1)S(1)}, bf16[96,1536]{1,0:T(8,128)(2,1)S(1)}, u32[]{:S(2)}, u32[]{:S(2)}) collective-permute-start(bf16[96,1536]{1,0:T(8,128)(2,1)S(1)} %get-tuple-element.204), channel_id=1, source_target_pairs={{0,5},{1,4},{2,7},{3,6},{4,1},{5,0},{6,3},{7,2},{8,13},{9,12},{10,... | collective-permute-start | bytes 884744 | tf_op jit(solution)/shard_map/ppermute | solution.py:1186
  246.2 24.5 %collective-permute-start.13 = (bf16[96,1536]{1,0:T(8,128)(2,1)S(1)}, bf16[96,1536]{1,0:T(8,128)(2,1)}, u32[]{:S(2)}, u32[]{:S(2)}) collective-permute-start(bf16[96,1536]{1,0:T(8,128)(2,1)S(1)} %get-tuple-element.205), channel_id=1, source_target_pairs={{0,7},{1,6},{2,5},{3,4},{4,3},{5,2},{6,1},{7,0},{8,15},{9,14},{10,... | collective-permute-start | bytes 884744 | tf_op jit(solution)/shard_map/ppermute | solution.py:1186
  248.0 22.7 %collective-permute-start.14 = (bf16[96,1536]{1,0:T(8,128)(2,1)S(1)}, bf16[96,1536]{1,0:T(8,128)(2,1)}, u32[]{:S(2)}, u32[]{:S(2)}) collective-permute-start(bf16[96,1536]{1,0:T(8,128)(2,1)S(1)} %get-tuple-element.206), channel_id=1, source_target_pairs={{0,3},{1,2},{2,1},{3,0},{4,7},{5,6},{6,5},{7,4},{8,11},{9,10},{10,... | collective-permute-start | bytes 884744 | tf_op jit(solution)/shard_map/ppermute | solution.py:1186
  249.9 20.9 %collective-permute-start.15 = (bf16[96,1536]{1,0:T(8,128)(2,1)S(1)}, bf16[96,1536]{1,0:T(8,128)(2,1)}, u32[]{:S(2)}, u32[]{:S(2)}) collective-permute-start(bf16[96,1536]{1,0:T(8,128)(2,1)S(1)} %get-tuple-element.207), channel_id=1, source_target_pairs={{0,1},{1,0},{2,3},{3,2},{4,5},{5,4},{6,7},{7,6},{8,9},{9,8},{10,11... | collective-permute-start | bytes 884744 | tf_op jit(solution)/shard_map/ppermute | solution.py:1186
  270.7 33.4 %collective-permute-start.16 = (bf16[96,1536]{1,0:T(8,128)(2,1)}, bf16[96,1536]{1,0:T(8,128)(2,1)S(1)}, u32[]{:S(2)}, u32[]{:S(2)}) collective-permute-start(bf16[96,1536]{1,0:T(8,128)(2,1)} %get-tuple-element.219.refs_12_), channel_id=1, source_target_pairs={{0,4},{1,5},{2,6},{3,7},{4,0},{5,1},{6,2},{7,3},{8,12},{9,13},{10,... | collective-permute-start | bytes 884744 | tf_op jit(solution)/shard_map/ppermute | solution.py:1186
  275.2 28.9 %collective-permute-start.17 = (bf16[96,1536]{1,0:T(8,128)(2,1)}, bf16[96,1536]{1,0:T(8,128)(2,1)S(1)}, u32[]{:S(2)}, u32[]{:S(2)}) collective-permute-start(bf16[96,1536]{1,0:T(8,128)(2,1)} %get-tuple-element.221.refs_14_), channel_id=1, source_target_pairs={{0,6},{1,7},{2,4},{3,5},{4,2},{5,3},{6,0},{7,1},{8,14},{9,15},{10,... | collective-permute-start | bytes 884744 | tf_op jit(solution)/shard_map/ppermute | solution.py:1186
  276.6 27.5 %collective-permute-start.18 = (bf16[96,1536]{1,0:T(8,128)(2,1)}, bf16[96,1536]{1,0:T(8,128)(2,1)S(1)}, u32[]{:S(2)}, u32[]{:S(2)}) collective-permute-start(bf16[96,1536]{1,0:T(8,128)(2,1)} %get-tuple-element.217.refs_10_), channel_id=1, source_target_pairs={{0,2},{1,3},{2,0},{3,1},{4,6},{5,7},{6,4},{7,5},{8,10},{9,11},{10,... | collective-permute-start | bytes 884744 | tf_op jit(solution)/shard_map/ppermute | solution.py:1186
  276.6 27.6 %collective-permute-start.19 = (bf16[96,1536]{1,0:T(8,128)(2,1)}, bf16[96,1536]{1,0:T(8,128)(2,1)S(1)}, u32[]{:S(2)}, u32[]{:S(2)}) collective-permute-start(bf16[96,1536]{1,0:T(8,128)(2,1)} %get-tuple-element.216.refs_9_), channel_id=1, source_target_pairs={{0,1},{1,0},{2,3},{3,2},{4,5},{5,4},{6,7},{7,6},{8,9},{9,8},{10,11... | collective-permute-start | bytes 884744 | tf_op jit(solution)/shard_map/ppermute | solution.py:1186
  277.6 26.6 %collective-permute-start.20 = (bf16[96,1536]{1,0:T(8,128)(2,1)}, bf16[96,1536]{1,0:T(8,128)(2,1)S(1)}, u32[]{:S(2)}, u32[]{:S(2)}) collective-permute-start(bf16[96,1536]{1,0:T(8,128)(2,1)} %get-tuple-element.218.refs_11_), channel_id=1, source_target_pairs={{0,3},{1,2},{2,1},{3,0},{4,7},{5,6},{6,5},{7,4},{8,11},{9,10},{10,... | collective-permute-start | bytes 884744 | tf_op jit(solution)/shard_map/ppermute | solution.py:1186
  305.1 58.9 %all-to-all-start.3 = ((bf16[8,96,1536]{2,1,0:T(8,128)(2,1)}), bf16[8,96,1536]{2,1,0:T(8,128)(2,1)}, u32[]{:S(2)}, u32[]{:S(2)}) async-start(bf16[8,96,1536]{2,1,0:T(8,128)(2,1)} %bitcast.125), calls=%async_computation.3 | async-start | bytes 4718592 | tf_op jit(solution)/shard_map/all_to_all | solution.py:1209
  313.5 37.7 %collective-permute-start.21 = (bf16[384,1024]{1,0:T(8,128)(2,1)}, bf16[384,1024]{1,0:T(8,128)(2,1)S(1)}, u32[]{:S(2)}, u32[]{:S(2)}) collective-permute-start(bf16[384,1024]{1,0:T(8,128)(2,1)} %convolution_convert_fusion.8), channel_id=1, source_target_pairs={{0,8},{8,0},{16,24},{24,16},{1,9},{9,1},{17,25},{25,17},{2,10},{10... | collective-permute-start | bytes 2359304 | tf_op jit(solution)/shard_map/ppermute | solution.py:1186
  316.4 36.1 %collective-permute-start.22 = (bf16[384,1024]{1,0:T(8,128)(2,1)}, bf16[384,1024]{1,0:T(8,128)(2,1)}, u32[]{:S(2)}, u32[]{:S(2)}) collective-permute-start(bf16[384,1024]{1,0:T(8,128)(2,1)} %convolution_convert_fusion.6), channel_id=1, source_target_pairs={{0,16},{8,24},{16,0},{24,8},{1,17},{9,25},{17,1},{25,9},{2,18},{10... | collective-permute-start | bytes 2359304 | tf_op jit(solution)/shard_map/ppermute | solution.py:1186
  320.2 41.1 %collective-permute-start.23 = (bf16[384,1024]{1,0:T(8,128)(2,1)}, bf16[384,1024]{1,0:T(8,128)(2,1)}, u32[]{:S(2)}, u32[]{:S(2)}) collective-permute-start(bf16[384,1024]{1,0:T(8,128)(2,1)} %convolution_convert_fusion.4), channel_id=1, source_target_pairs={{0,8},{8,0},{16,24},{24,16},{1,9},{9,1},{17,25},{25,17},{2,10},{10... | collective-permute-start | bytes 2359304 | tf_op jit(solution)/shard_map/ppermute | solution.py:1186
  324.0 37.3 %collective-permute-start.24 = (bf16[384,1024]{1,0:T(8,128)(2,1)}, bf16[384,1024]{1,0:T(8,128)(2,1)}, u32[]{:S(2)}, u32[]{:S(2)}) collective-permute-start(bf16[384,1024]{1,0:T(8,128)(2,1)} %convolution_convert_fusion.2), channel_id=1, source_target_pairs={{0,16},{8,24},{16,0},{24,8},{1,17},{9,25},{17,1},{25,9},{2,18},{10... | collective-permute-start | bytes 2359304 | tf_op jit(solution)/shard_map/ppermute | solution.py:1186
  375.2 23.6 %all-to-all-start.4 = ((bf16[8,192,256]{2,1,0:T(8,128)(2,1)}), bf16[8,192,256]{2,1,0:T(8,128)(2,1)S(1)}, u32[]{:S(2)}, u32[]{:S(2)}) async-start(bf16[8,192,256]{2,1,0:T(8,128)(2,1)} %bitcast.116), calls=%async_computation.4 | async-start | bytes 1572864 | tf_op jit(solution)/shard_map/all_to_all | solution.py:1209
  378.7 83.8 %reduce-scatter.2.cloned.1.call-start = ((), (), s32[]{:S(2)}) async-start(), calls=%async_computation.11 | async-start | bytes 3932160 | tf_op jit(solution)/shard_map/reduce_scatter | solution.py:1400
  378.8 19.5 %collective-permute-start.26 = (bf16[384,1024]{1,0:T(8,128)(2,1)}, bf16[384,1024]{1,0:T(8,128)(2,1)}, u32[]{:S(2)}, u32[]{:S(2)}) collective-permute-start(bf16[384,1024]{1,0:T(8,128)(2,1)} %add_convert_fusion.2), channel_id=1, source_target_pairs={{0,16},{8,24},{16,0},{24,8},{1,17},{9,25},{17,1},{25,9},{2,18},{10... | collective-permute-start | bytes 2359304 | tf_op jit(solution)/shard_map/ppermute | solution.py:1186
  379.6 19.1 %collective-permute-start.27 = (bf16[384,1024]{1,0:T(8,128)(2,1)}, bf16[384,1024]{1,0:T(8,128)(2,1)}, u32[]{:S(2)}, u32[]{:S(2)}) collective-permute-start(bf16[384,1024]{1,0:T(8,128)(2,1)} %add_convert_fusion.1), channel_id=1, source_target_pairs={{0,8},{8,0},{16,24},{24,16},{1,9},{9,1},{17,25},{25,17},{2,10},{10... | collective-permute-start | bytes 2359304 | tf_op jit(solution)/shard_map/ppermute | solution.py:1186
  401.4 52.2 %collective-permute-start.30 = (bf16[2,384,768]{2,1,0:T(8,128)(2,1)}, bf16[2,384,768]{2,1,0:T(8,128)(2,1)}, u32[]{:S(2)}, u32[]{:S(2)}) collective-permute-start(bf16[2,384,768]{2,1,0:T(8,128)(2,1)} %slice.91), channel_id=1, source_target_pairs={{0,16},{8,24},{16,0},{24,8},{1,17},{9,25},{17,1},{25,9},{2,18},{10... | collective-permute-start | bytes 3538952 | tf_op jit(solution)/shard_map/ppermute | solution.py:1186
  402.1 32.4 %collective-permute-start.28 = (bf16[96,1536]{1,0:T(8,128)(2,1)S(1)}, bf16[96,1536]{1,0:T(8,128)(2,1)S(1)}, u32[]{:S(2)}, u32[]{:S(2)}) collective-permute-start(bf16[96,1536]{1,0:T(8,128)(2,1)S(1)} %copy-done.46), channel_id=1, source_target_pairs={{0,5},{1,4},{2,7},{3,6},{4,1},{5,0},{6,3},{7,2},{8,13},{9,12},{10,... | collective-permute-start | bytes 884744 | tf_op jit(solution)/shard_map/ppermute | solution.py:1186
  405.5 29.8 %collective-permute-start.29 = (bf16[96,1536]{1,0:T(8,128)(2,1)S(1)}, bf16[96,1536]{1,0:T(8,128)(2,1)S(1)}, u32[]{:S(2)}, u32[]{:S(2)}) collective-permute-start(bf16[96,1536]{1,0:T(8,128)(2,1)S(1)} %copy-done.45), channel_id=1, source_target_pairs={{0,7},{1,6},{2,5},{3,4},{4,3},{5,2},{6,1},{7,0},{8,15},{9,14},{10,... | collective-permute-start | bytes 884744 | tf_op jit(solution)/shard_map/ppermute | solution.py:1186
  436.0 38.6 %all-to-all-start.5 = ((bf16[8,320,256]{2,1,0:T(8,128)(2,1)}), bf16[8,320,256]{2,1,0:T(8,128)(2,1)}, u32[]{:S(2)}, u32[]{:S(2)}) async-start(bf16[8,320,256]{2,1,0:T(8,128)(2,1)} %copy-done.15), calls=%async_computation.6 | async-start | bytes 2621440 | tf_op jit(solution)/shard_map/all_to_all | solution.py:1209
  454.7 17.4 %collective-permute-start.31 = (bf16[384,384]{1,0:T(8,128)(2,1)}, bf16[384,384]{1,0:T(8,128)(2,1)}, u32[]{:S(2)}, u32[]{:S(2)}) collective-permute-start(bf16[384,384]{1,0:T(8,128)(2,1)} %get-tuple-element.358), channel_id=1, source_target_pairs={{0,8},{8,0},{16,24},{24,16},{1,9},{9,1},{17,25},{25,17},{2,10},{10... | collective-permute-start | bytes 884744 | tf_op jit(solution)/shard_map/ppermute | solution.py:1186
  454.8 17.3 %collective-permute-start.32 = (bf16[384,384]{1,0:T(8,128)(2,1)}, bf16[384,384]{1,0:T(8,128)(2,1)}, u32[]{:S(2)}, u32[]{:S(2)}) collective-permute-start(bf16[384,384]{1,0:T(8,128)(2,1)} %get-tuple-element.357), channel_id=1, source_target_pairs={{0,16},{8,24},{16,0},{24,8},{1,17},{9,25},{17,1},{25,9},{2,18},{10... | collective-permute-start | bytes 884744 | tf_op jit(solution)/shard_map/ppermute | solution.py:1186
  455.9 16.3 %collective-permute-start.33 = (bf16[384,384]{1,0:T(8,128)(2,1)}, bf16[384,384]{1,0:T(8,128)(2,1)}, u32[]{:S(2)}, u32[]{:S(2)}) collective-permute-start(bf16[384,384]{1,0:T(8,128)(2,1)} %get-tuple-element.356), channel_id=1, source_target_pairs={{0,24},{8,16},{16,8},{24,0},{1,25},{9,17},{17,9},{25,1},{2,26},{10... | collective-permute-start | bytes 884744 | tf_op jit(solution)/shard_map/ppermute | solution.py:1186
  474.3 14.5 %collective-permute-start.34 = (bf16[384,768]{1,0:T(8,128)(2,1)}, bf16[384,768]{1,0:T(8,128)(2,1)}, u32[]{:S(2)}, u32[]{:S(2)}) collective-permute-start(bf16[384,768]{1,0:T(8,128)(2,1)} %fusion.4), channel_id=1, source_target_pairs={{0,8},{8,0},{16,24},{24,16},{1,9},{9,1},{17,25},{25,17},{2,10},{10... | collective-permute-start | bytes 1769480 | tf_op jit(solution)/shard_map/ppermute | solution.py:1186
  474.6 30.9 %all-to-all-start.6 = ((bf16[8,48,384]{2,1,0:T(8,128)(2,1)}), bf16[8,48,384]{2,1,0:T(8,128)(2,1)}, u32[]{:S(2)}, u32[]{:S(2)}) async-start(bf16[8,48,384]{2,1,0:T(8,128)(2,1)} %bitcast.44), calls=%async_computation.7 | async-start | bytes 589824 | tf_op jit(solution)/shard_map/all_to_all | solution.py:1209
  492.1 13.4 %collective-permute-start.35 = (bf16[96,768]{1,0:T(8,128)(2,1)}, bf16[96,768]{1,0:T(8,128)(2,1)}, u32[]{:S(2)}, u32[]{:S(2)}) collective-permute-start(bf16[96,768]{1,0:T(8,128)(2,1)} %get-tuple-element.369), channel_id=1, source_target_pairs={{0,2},{1,3},{2,0},{3,1},{4,6},{5,7},{6,4},{7,5},{8,10},{9,11},{10,... | collective-permute-start | bytes 442376 | tf_op jit(solution)/shard_map/ppermute | solution.py:1186
  492.8 12.7 %collective-permute-start.36 = (bf16[96,768]{1,0:T(8,128)(2,1)}, bf16[96,768]{1,0:T(8,128)(2,1)}, u32[]{:S(2)}, u32[]{:S(2)}) collective-permute-start(bf16[96,768]{1,0:T(8,128)(2,1)} %get-tuple-element.368), channel_id=1, source_target_pairs={{0,4},{1,5},{2,6},{3,7},{4,0},{5,1},{6,2},{7,3},{8,12},{9,13},{10,... | collective-permute-start | bytes 442376 | tf_op jit(solution)/shard_map/ppermute | solution.py:1186
  494.9 10.6 %collective-permute-start.37 = (bf16[96,768]{1,0:T(8,128)(2,1)}, bf16[96,768]{1,0:T(8,128)(2,1)}, u32[]{:S(2)}, u32[]{:S(2)}) collective-permute-start(bf16[96,768]{1,0:T(8,128)(2,1)} %get-tuple-element.367), channel_id=1, source_target_pairs={{0,6},{1,7},{2,4},{3,5},{4,2},{5,3},{6,0},{7,1},{8,14},{9,15},{10,... | collective-permute-start | bytes 442376 | tf_op jit(solution)/shard_map/ppermute | solution.py:1186
  (65 other events, 288.6 us)
Sparse Core Ops, SparseCore 0:
  9.7 75.5 all-gather.11
  88.2 76.8 all-gather.5
  178.8 57.7 all-gather.7
  246.2 92.1 all-gather.9
  399.0 61.5 reduce-scatter.1

commit v5 on v4

--- a/solution.py
+++ b/solution.py
@@ -520,9 +520,11 @@
     def same_doc(j):
         return segc_ref[pl.ds(pl.multiple_of(j * block, block), block), :] == seg_row
 
-    def fold(j, scores, carry):
+    def fold(span, scores, carry):
         top, total, out = carry
-        values = heads_ref[j, share + HEAD_SIZE : share + 2 * HEAD_SIZE, :]
+        values = jnp.concatenate(
+            [heads_ref[j, share + HEAD_SIZE : share + 2 * HEAD_SIZE, :] for j in span], 1
+        )
         new_top = jnp.maximum(top, jnp.max(scores, 0, keepdims=True))
         probs = jnp.exp(scores - new_top)
         decay = jnp.exp(top - new_top)
@@ -534,7 +536,7 @@
 
     def masked(j, carry):
         allowed = jnp.concatenate([same_doc(j)] * heads, 1)
-        return fold(j, jnp.where(allowed, scores_of(j), NEGATIVE_LARGE), carry)
+        return fold([j], jnp.where(allowed, scores_of(j), NEGATIVE_LARGE), carry)
 
     columns = heads * block
     carry = (
@@ -544,12 +546,21 @@
     )
     first, full = spans[0, step], spans[1, step]
     carry = lax.fori_loop(first, full, masked, carry)
-    carry = lax.fori_loop(full, step, lambda j, kept: fold(j, scores_of(j), kept), carry)
+    pairs = (step - full) // 2
+
+    def whole_pair(p, kept):
+        j = full + 2 * p
+        return fold([j, j + 1], jnp.concatenate([scores_of(j), scores_of(j + 1)], 0), kept)
+
+    carry = lax.fori_loop(0, pairs, whole_pair, carry)
+    carry = lax.fori_loop(
+        full + 2 * pairs, step, lambda j, kept: fold([j], scores_of(j), kept), carry
+    )
     key_spot = lax.broadcasted_iota(jnp.int32, (block, block), 0)
     query_spot = lax.broadcasted_iota(jnp.int32, (block, block), 1)
     allowed = same_doc(step) & (key_spot <= query_spot)
     allowed = jnp.concatenate([allowed] * heads, 1)
-    top, total, out = fold(step, jnp.where(allowed, scores_of(step), NEGATIVE_LARGE), carry)
+    top, total, out = fold([step], jnp.where(allowed, scores_of(step), NEGATIVE_LARGE), carry)
     out = out / total
     totals = top + jnp.log(total)
     for h in range(heads):
@@ -625,7 +636,16 @@
     query_sum = jnp.zeros((HEAD_SIZE, heads * block), jnp.float32)
     first, full = spans[0, step], spans[1, step]
     query_sum = lax.fori_loop(first, full, lambda j, c: turn(j, c, same_doc(j)), query_sum)
-    query_sum = lax.fori_loop(full, step, lambda j, c: turn(j, c, None), query_sum)
+    pairs = (step - full) // 2
+
+    def whole_pair(p, kept):
+        j = full + 2 * p
+        return turn(j + 1, turn(j, kept, None), None)
+
+    query_sum = lax.fori_loop(0, pairs, whole_pair, query_sum)
+    query_sum = lax.fori_loop(
+        full + 2 * pairs, step, lambda j, c: turn(j, c, None), query_sum
+    )
     key_spot = lax.broadcasted_iota(jnp.int32, (block, block), 0)
     query_spot = lax.broadcasted_iota(jnp.int32, (block, block), 1)
     query_sum = turn(step, query_sum, same_doc(step) & (key_spot <= query_spot))
@@ -1086,7 +1106,7 @@
         out_specs=whole((rows, width)),
         out_shape=jax.ShapeDtypeStruct((rows, width), jnp.float32),
         scratch_shapes=[pltpu.VMEM((rows, width), jnp.float32)],
-        compiler_params=pltpu.CompilerParams(vmem_limit_bytes=32 * 2**20),
+        compiler_params=pltpu.CompilerParams(vmem_limit_bytes=56 * 2**20),
         name="tokens_back",
     )(start, grad_middle, grads, weight, head_weights)
 
@@ -1412,13 +1432,15 @@
     terms = weight_terms(
         own_group, normed, grads_line, router_part, gain_part, router_lane, experts, lanes, 4
     )
-    terms, output_part, output_near = after((terms, output_part, output_near))
+    terms, output_part, output_near, near_a, near_b, part_home = after(
+        (terms, output_part, output_near, near_a, near_b, part_home)
+    )
     output_sum = output_part[:2].astype(f32) + output_near.astype(f32)
     inner_grad = sum_pairs(
         [gate_terms[0], near_a, side_a], [up_terms[0], near_b, side_b], size // 4
     )
     outer_grad = outer_sum.astype(f32)
-    block_out = mixture(slots_near, gates, middle, after(part_home, outer_grad))
+    block_out = mixture(slots_near, gates, middle, part_home)
     weights_near = after(
         [flip_exchange(terms[k], "dp", k) for k in range(1, 4)], inner_grad, block_out
     )

time: 532 us -> 526 us (0.989)
  waiting for transfers between devices: 159 us -> 170 us
  local copies, waits for them, and re-layouts: 35.5 us -> 26.7 us
    ppermute x39, waiting for transfers between devices: 59.4 us -> 69.3 us  [flip_exchange(): return lax.ppermute(block, axis, [(i, i ^ flip) for i in range(count)])]
    unnamed x130 -> x152, local copies, waits for them, and re-layouts: 22.6 us -> 17.9 us
  transfers between devices with their start and end apart: 50 -> 50, of which waited for: 16 -> 16; matrix products, arithmetic and copies ran while one was open for 15% -> 13% of each run, Pallas kernels for 24% -> 24%
where the time goes in v5:
time: 526 us; the launch traced here: 517 us
  waiting for transfers between devices  170 us (32%)
  Pallas kernels  137 us (26%)
  starting transfers between devices  73.8 us (14%)
  blocking collectives  33.5 us (6%)
  matrix products  32.9 us (6%)
  other arithmetic  27.4 us (5%)
  local copies, waits for them, and re-layouts  26.7 us (5%)
  between operations  15.3 us (3%)
    ppermute x39, waiting for transfers between devices, flip_exchange(): return lax.ppermute(block, axis, [(i, i ^ flip) for i in range(count)])  69.3 us
    all_gather x4, waiting for transfers between devices, gather(): return lax.all_gather(block, axis, axis=0, tiled=True)  69 us
    ppermute x39, starting transfers between devices, flip_exchange(): return lax.ppermute(block, axis, [(i, i ^ flip) for i in range(count)])  43.3 us
    all_to_all x1, blocking collectives, all_to_all(): lax.all_to_all(blocks, 'fsdp', split_axis=0, concat_axis=0, tiled=True)  33.5 us
    dot_general x14, matrix products, contract(): lax.dot_general(left, right, (((left_axis,), (right_axis,)), ((), ())), p...  32.6 us
    all_to_all x6, waiting for transfers between devices, all_to_all(): lax.all_to_all(blocks, 'fsdp', split_axis=0, concat_axis=0, tiled=True)  30.6 us
    all_to_all x6, starting transfers between devices, all_to_all(): lax.all_to_all(blocks, 'fsdp', split_axis=0, concat_axis=0, tiled=True)  30.3 us
    pallas_call x1, Pallas kernels, expert_backward_pass(): pl.pallas_call(functools.partial(expert_back_kernel, router_lane, blocks)...  24.7 us
  transfers between devices with their start and end apart: 50, of which 16 were waited for; matrix products, arithmetic and copies ran while one was open for 13% of the time, Pallas kernels for 24%

profile of v5, /device:TPU:1, one launch (start us, length us, event | category | flops | bytes accessed | tf_op | source)
XLA Modules:
  0.0 516.8 jit_solution(16950337444029576459)
XLA Ops:
  8.0 3.1 copy.74
  17.7 6.9 %all-to-all-start = ((bf16[8,64,384]{2,1,0:T(8,128)(2,1)}), bf16[8,64,384]{2,1,0:T(8,128)(2,1)S(1)}, u32[]{:S(2)}, u32[]{:S(2)}) async-start(bf16[8,64,384]{2,1,0:T(8,128)(2,1)} %copy.67), calls=%async_computation | async-start | bytes 786432 | tf_op jit(solution)/shard_map/all_to_all | solution.py:1229
  28.1 19.1 %all-to-all-done = bf16[8,64,384]{2,1,0:T(8,128)(2,1)S(1)} async-done(((bf16[8,64,384]{2,1,0:T(8,128)(2,1)}), bf16[8,64,384]{2,1,0:T(8,128)(2,1)S(1)}, u32[]{:S(2)}, u32[]{:S(2)}) %all-to-all-start) | async-done | bytes 393248 | tf_op jit(solution)/shard_map/all_to_all | solution.py:1229
  47.2 17.2 %collective-permute-done.2.refs_9_.refs_29_ = bf16[1024,384]{1,0:T(8,128)(2,1)} collective-permute-done((bf16[1024,384]{1,0:T(8,128)(2,1)S(1)}, bf16[1024,384]{1,0:T(8,128)(2,1)}, u32[]{:S(2)}, u32[]{:S(2)}) %collective-permute-start.2) | collective-permute-done | bytes 786464 | tf_op jit(solution)/shard_map/ppermute | solution.py:1206
  69.2 3.8 collective-permute-done.6
  73.0 8.5 %collective-permute-done.5 = bf16[384,384]{1,0:T(8,128)(2,1)S(1)} collective-permute-done((bf16[384,384]{1,0:T(8,128)(2,1)S(1)}, bf16[384,384]{1,0:T(8,128)(2,1)S(1)}, u32[]{:S(2)}, u32[]{:S(2)}) %collective-permute-start.5) | collective-permute-done | bytes 294944 | tf_op jit(solution)/shard_map/ppermute | solution.py:1206
  88.3 10.4 %project.1 = (bf16[2048,1536]{1,0:T(8,128)(2,1)}, bf16[8,320,256]{2,1,0:T(8,128)(2,1)}) custom-call(bf16[2048,1536]{1,0:T(8,128)(2,1)} %bitcast.121, bf16[1536,384]{1,0:T(8,128)(2,1)} %bitcast.105, bf16[1536,384]{1,0:T(8,128)(2,1)} %bitcast.106), custom_call_target="tpu_custom_call" | custom-call | tf_op jit(solution)/shard_map/project/pallas_call | solution.py:483
  100.1 19.3 %attend.1 = (bf16[8,192,256]{2,1,0:T(8,128)(2,1)S(1)}, f32[8,192,256]{2,1,0:T(8,128)S(1)}, f32[8,8,256]{2,1,0:T(8,128)S(1)}) custom-call(s32[2,8]{1,0:T(2,128)S(1)} %pad_add_fusion.spans, bf16[8,320,256]{2,1,0:T(8,128)(2,1)S(1)} %copy-done.1, bf16[8,320,256]{2,1,0:T(8,128)(2,1)S(1)} %copy-done.1, s32[1,2048]{1,0:T(1,128)S(1)} %bitcast.117, ...), custom_call_target="tpu_custom_call" | custom-call | tf_op jit(solution)/shard_map/attend/pallas_call | solution.py:578
  121.2 33.5 %all_to_all.49 = bf16[8,192,256]{2,1,0:T(8,128)(2,1)} all-to-all(bf16[8,192,256]{2,1,0:T(8,128)(2,1)S(1)} %get-tuple-element.176), channel_id=1, replica_groups=mesh['dp'=4,'fsdp'=8] {'fsdp'}, dimensions={0} | all-to-all | bytes 1572864 | tf_op jit(solution)/shard_map/all_to_all | solution.py:1229
  154.8 9.3 %all-gather.6.cloned.1.call-done.weight_ref = bf16[1536,1536]{1,0:T(8,128)(2,1)} async-done(((bf16[48,1536]{1,0:T(8,128)(2,1)}), bf16[1536,1536]{1,0:T(8,128)(2,1)}) %all-gather.6.cloned.1.call-update) | async-done | bytes 4718608 | tf_op jit(solution)/shard_map/all_gather | solution.py:1233
  164.1 6.7 %middle.1 = (f32[256,1536]{1,0:T(8,128)}, bf16[768,1536]{1,0:T(8,128)(2,1)}, f32[2,256]{1,0:T(2,128)}) custom-call(bf16[256,1536]{1,0:T(8,128)(2,1)} %bitcast.119, bf16[1536,256]{1,0:T(8,128)(2,1)} %bitcast.122, bf16[1536,1536]{1,0:T(8,128)(2,1)} %all-gather.6.cloned.1.call-done.weight_ref, bf16[1536,384]{1,0:T(8,128)(2,1)} %bitcast.107, ...), custom_call_target="tpu_custom_call" | custom-call | tf_op jit(solution)/shard_map/middle/pallas_call | solution.py:758
  170.7 4.5 all-to-all-start.2
  178.2 57.6 %all-gather.8.cloned.1.call-done = bf16[384,2560]{1,0:T(8,128)(2,1)} async-done(((bf16[48,2560]{1,0:T(8,128)(2,1)}), bf16[384,2560]{1,0:T(8,128)(2,1)}) %all-gather.8.cloned.1.call-update) | async-done | bytes 1966096 | tf_op jit(solution)/shard_map/all_gather | solution.py:1233
  235.9 9.1 %all-to-all-done.2 = bf16[8,96,1536]{2,1,0:T(8,128)(2,1)} async-done(((bf16[8,96,1536]{2,1,0:T(8,128)(2,1)}), bf16[8,96,1536]{2,1,0:T(8,128)(2,1)}, u32[]{:S(2)}, u32[]{:S(2)}) %all-to-all-start.2) | async-done | bytes 2359328 | tf_op jit(solution)/shard_map/all_to_all | solution.py:1229
  251.2 18.5 %expert.1 = (f32[768,1024]{1,0:T(8,128)}, f32[768,1024]{1,0:T(8,128)}, bf16[768,1024]{1,0:T(8,128)(2,1)}, f32[768,128]{1,0:T(8,128)}, bf16[96,1536]{1,0:T(8,128)...) custom-call(s32[2]{0:T(128)} %pad_add_fusion.1.own_ref, ...), custom_call_target="tpu_custom_call" | custom-call | tf_op jit(solution)/shard_map/expert/pallas_call | solution.py:847
  269.8 4.4 collective-permute-start.16
  278.1 24.7 %expert_backward.1 = (bf16[768,1024]{1,0:T(8,128)(2,1)}, bf16[768,1024]{1,0:T(8,128)(2,1)}, bf16[768,1536]{1,0:T(8,128)(2,1)}, bf16[768,1536]{1,0:T(8,128)(2,1)}, f32[128,1536]{1,0:T(8,128)}) custom-call(s32[2]{0:T(128)} %pad_add_fusion.1.own_ref, bf16[96,1536]{1,0:T(8,128)(2,1)} %copy-done.38, bf16[96,1536]{1,0:T(8,128)(2,1)} %collective-permute-done.15.refs_1_, ...), custom_call_target="tpu_custom_call" | custom-call | tf_op jit(solution)/shard_map/expert_backward/pallas_call | solution.py:942
  303.9 5.2 %all-to-all-start.3 = ((bf16[8,96,1536]{2,1,0:T(8,128)(2,1)}), bf16[8,96,1536]{2,1,0:T(8,128)(2,1)}, u32[]{:S(2)}, u32[]{:S(2)}) async-start(bf16[8,96,1536]{2,1,0:T(8,128)(2,1)} %bitcast.125), calls=%async_computation.3 | async-start | bytes 4718592 | tf_op jit(solution)/shard_map/all_to_all | solution.py:1229
  309.1 3.4 convolution_convert_fusion.8
  313.5 2.8 convolution_convert_fusion.6
  317.0 2.7 convolution_convert_fusion.4
  320.3 2.7 convolution_convert_fusion.2
  330.0 11.0 %pad_maximum_fusion = bf16[4096,384]{1,0:T(8,128)(2,1)} fusion(bf16[1024,384]{1,0:T(8,128)(2,1)S(1)} %convolution_convert_fusion.10, bf16[1024,384]{1,0:T(8,128)(2,1)S(1)} %convolution_convert_fusion.11, bf16[1024,384]{1,0:T(8,128)(2,1)S(1)} %convolution_convert_fusion.12, bf16[1024,384]{1,0:T(8,128)(2,1)S(1)} %convolution_convert_fusion.13), kind=kLoop, calls=%fused_computation.3 | loop fusion | flops 12582912 | bytes 6291456 | tf_op jit(solution)/shard_map/concatenate | solution.py:1391
  341.0 2.5 convolution_convert_fusion.7
  343.6 2.9 convolution_convert_fusion.5.refs_0_
  346.4 2.7 convolution_convert_fusion.3.refs_3_
  350.5 2.4 add_convert_fusion.1
  352.9 7.9 %collective-permute-done.23.refs_1_ = bf16[384,1024]{1,0:T(8,128)(2,1)} collective-permute-done((bf16[384,1024]{1,0:T(8,128)(2,1)}, bf16[384,1024]{1,0:T(8,128)(2,1)}, u32[]{:S(2)}, u32[]{:S(2)}) %collective-permute-start.23) | collective-permute-done | bytes 786464 | tf_op jit(solution)/shard_map/ppermute | solution.py:1206
  360.8 2.2 all-to-all-done.3
  363.0 6.3 %back.1 = (f32[256,1536]{1,0:T(8,128)S(1)}, bf16[256,1536]{1,0:T(8,128)(2,1)S(1)}, f32[1,1536]{1,0:T(1,128)S(1)}, bf16[1536,256]{1,0:T(8,128)(2,1)S(1)}) custom-call(f32[256,1536]{1,0:T(8,128)} %get-tuple-element.179.middle_ref, bf16[256,1536]{1,0:T(8,128)(2,1)S(1)} %bitcast.113, bf16[768,1536]{1,0:T(8,128)(2,1)} %bitcast.33.home_ref, ...), custom_call_target="tpu_custom_call" | custom-call | tf_op jit(solution)/shard_map/back/pallas_call | solution.py:1011
  371.0 2.2 convolution_convert_fusion
  374.2 3.5 all-to-all-start.4
  379.6 4.4 add_convert_fusion
  384.0 13.2 %collective-permute-done.26.refs_2_ = bf16[384,1024]{1,0:T(8,128)(2,1)S(1)} collective-permute-done((bf16[384,1024]{1,0:T(8,128)(2,1)}, bf16[384,1024]{1,0:T(8,128)(2,1)S(1)}, u32[]{:S(2)}, u32[]{:S(2)}) %collective-permute-start.26) | collective-permute-done | bytes 786464 | tf_op jit(solution)/shard_map/ppermute | solution.py:1206
  398.6 2.5 slice.91
  401.8 3.5 collective-permute-start.28
  407.7 24.5 %attend_backward.1 = (bf16[8,320,256]{2,1,0:T(8,128)(2,1)S(1)}, bf16[320,2048]{1,0:T(8,128)(2,1)S(1)}) custom-call(s32[2,8]{1,0:T(2,128)S(1)} %copy-done.46, bf16[8,320,256]{2,1,0:T(8,128)(2,1)S(1)} %copy-done.2, bf16[8,192,256]{2,1,0:T(8,128)(2,1)S(1)} %all-to-all-done.4.g_ref, bf16[8,320,256]{2,1,0:T(8,128)(2,1)S(1)} %copy-done.2, ...), custom_call_target="tpu_custom_call" | custom-call | tf_op jit(solution)/shard_map/attend_backward/pallas_call | solution.py:674
  434.6 5.0 all-to-all-start.5
  439.7 2.8 copy-done.3
  442.5 4.6 weight_terms.1
  451.7 4.5 sum_pairs.1
  456.3 6.0 %mixture.1 = bf16[256,1536]{1,0:T(8,128)(2,1)} custom-call(s32[2,256]{1,0:T(2,128)S(1)} %copy-done.44, f32[2,256]{1,0:T(2,128)S(1)} %copy-done.49, f32[256,1536]{1,0:T(8,128)S(1)} %copy-done.4, bf16[96,1536]{1,0:T(8,128)(2,1)S(1)} %copy-done.10, bf16[96,1536]{1,0:T(8,128)(2,1)S(1)} %copy-done.31, bf16[96,1536]{1,0:T(8,128)(2,1)S(1)} %copy-done.29, ...), custom_call_target="tpu_custom_call" | custom-call | tf_op jit(solution)/shard_map/mixture/pallas_call | solution.py:1132
  463.2 8.4 %collective-permute-done.33 = bf16[384,384]{1,0:T(8,128)(2,1)S(1)} collective-permute-done((bf16[384,384]{1,0:T(8,128)(2,1)S(1)}, bf16[384,384]{1,0:T(8,128)(2,1)S(1)}, u32[]{:S(2)}, u32[]{:S(2)}) %collective-permute-start.33) | collective-permute-done | bytes 294944 | tf_op jit(solution)/shard_map/ppermute | solution.py:1206
  473.0 5.2 %all-to-all-start.6 = ((bf16[8,48,384]{2,1,0:T(8,128)(2,1)}), bf16[8,48,384]{2,1,0:T(8,128)(2,1)S(1)}, u32[]{:S(2)}, u32[]{:S(2)}) async-start(bf16[8,48,384]{2,1,0:T(8,128)(2,1)} %bitcast.44), calls=%async_computation.7 | async-start | bytes 589824 | tf_op jit(solution)/shard_map/all_to_all | solution.py:1229
  478.3 8.8 %collective-permute-done.34 = bf16[384,768]{1,0:T(8,128)(2,1)S(1)} collective-permute-done((bf16[384,768]{1,0:T(8,128)(2,1)}, bf16[384,768]{1,0:T(8,128)(2,1)S(1)}, u32[]{:S(2)}, u32[]{:S(2)}) %collective-permute-start.34) | collective-permute-done | bytes 589856 | tf_op jit(solution)/shard_map/ppermute | solution.py:1206
  491.8 2.4 convert_element_type.228
  494.2 8.7 %tokens_back.1 = f32[256,1536]{1,0:T(8,128)} custom-call(bf16[256,1536]{1,0:T(8,128)(2,1)} %bitcast.120, f32[256,1536]{1,0:T(8,128)} %copy-done.6, bf16[8,320,256]{2,1,0:T(8,128)(2,1)} %all-to-all-done.5.grads_ref, bf16[1536,2560]{1,0:T(8,128)(2,1)} %all-gather.10.cloned.1.call-done.weight_ref, bf16[1536,384]{1,0:T(8,128)(2,1)} %bitcast.110), custom_call_target="tpu_custom_call" | custom-call | tf_op jit(solution)/shard_map/tokens_back/pallas_call | solution.py:1096
  504.9 2.2 collective-permute-start.38
  (295 shorter events, 77.6 us)
Async XLA Ops:
  7.2 78.1 %all-gather.12.cloned.1.call-start = ((), (), s32[]{:S(2)}) async-start(), calls=%async_computation.12 | async-start | bytes 7077888 | tf_op jit(solution)/shard_map/all_gather | solution.py:1233
  11.0 54.2 %collective-permute-start = (bf16[384,2048]{1,0:T(8,128)(2,1)}, bf16[384,2048]{1,0:T(8,128)(2,1)}, u32[]{:S(2)}, u32[]{:S(2)}) collective-permute-start(bf16[384,2048]{1,0:T(8,128)(2,1)} %bitcast.49.refs_0_.refs_4_.refs_20_.refs_24_), channel_id=1, source_target_pairs={{0,8},{8,0},{16,24},{24,16},{1,9},{9,1},{17,25},{25,17},{2,10},{10... | collective-permute-start | bytes 4718600 | tf_op jit(solution)/shard_map/ppermute | solution.py:1206
  13.1 52.1 %collective-permute-start.1 = (bf16[384,2048]{1,0:T(8,128)(2,1)}, bf16[384,2048]{1,0:T(8,128)(2,1)}, u32[]{:S(2)}, u32[]{:S(2)}) collective-permute-start(bf16[384,2048]{1,0:T(8,128)(2,1)} %bitcast.49.refs_0_.refs_4_.refs_20_.refs_24_), channel_id=1, source_target_pairs={{0,16},{8,24},{16,0},{24,8},{1,17},{9,25},{17,1},{25,9},{2,18},{10... | collective-permute-start | bytes 4718600 | tf_op jit(solution)/shard_map/ppermute | solution.py:1206
  14.3 50.0 %collective-permute-start.2 = (bf16[1024,384]{1,0:T(8,128)(2,1)S(1)}, bf16[1024,384]{1,0:T(8,128)(2,1)}, u32[]{:S(2)}, u32[]{:S(2)}) collective-permute-start(bf16[1024,384]{1,0:T(8,128)(2,1)S(1)} %copy-done.50), channel_id=1, source_target_pairs={{0,8},{8,0},{16,24},{24,16},{1,9},{9,1},{17,25},{25,17},{2,10},{10... | collective-permute-start | bytes 2359304 | tf_op jit(solution)/shard_map/ppermute | solution.py:1206
  14.6 50.6 %collective-permute-start.3 = (bf16[1024,384]{1,0:T(8,128)(2,1)S(1)}, bf16[1024,384]{1,0:T(8,128)(2,1)}, u32[]{:S(2)}, u32[]{:S(2)}) collective-permute-start(bf16[1024,384]{1,0:T(8,128)(2,1)S(1)} %copy-done.50), channel_id=1, source_target_pairs={{0,16},{8,24},{16,0},{24,8},{1,17},{9,25},{17,1},{25,9},{2,18},{10... | collective-permute-start | bytes 2359304 | tf_op jit(solution)/shard_map/ppermute | solution.py:1206
  17.7 29.5 %all-to-all-start = ((bf16[8,64,384]{2,1,0:T(8,128)(2,1)}), bf16[8,64,384]{2,1,0:T(8,128)(2,1)S(1)}, u32[]{:S(2)}, u32[]{:S(2)}) async-start(bf16[8,64,384]{2,1,0:T(8,128)(2,1)} %copy.67), calls=%async_computation | async-start | bytes 786432 | tf_op jit(solution)/shard_map/all_to_all | solution.py:1229
  24.5 139.5 %all-gather.6.cloned.1.call-start = ((), (), s32[]{:S(2)}) async-start(), calls=%async_computation.8 | async-start | bytes 4866048 | tf_op jit(solution)/shard_map/all_gather | solution.py:1233
  65.2 7.8 %collective-permute-start.6 = (bf16[384,384]{1,0:T(8,128)(2,1)S(1)}, bf16[384,384]{1,0:T(8,128)(2,1)S(1)}, u32[]{:S(2)}, u32[]{:S(2)}) collective-permute-start(bf16[384,384]{1,0:T(8,128)(2,1)S(1)} %bitcast.131), channel_id=1, source_target_pairs={{0,24},{8,16},{16,8},{24,0},{1,25},{9,17},{17,9},{25,1},{2,26},{10... | collective-permute-start | bytes 884744 | tf_op jit(solution)/shard_map/ppermute | solution.py:1206
  66.6 15.0 %collective-permute-start.5 = (bf16[384,384]{1,0:T(8,128)(2,1)S(1)}, bf16[384,384]{1,0:T(8,128)(2,1)S(1)}, u32[]{:S(2)}, u32[]{:S(2)}) collective-permute-start(bf16[384,384]{1,0:T(8,128)(2,1)S(1)} %bitcast.132), channel_id=1, source_target_pairs={{0,16},{8,24},{16,0},{24,8},{1,17},{9,25},{17,1},{25,9},{2,18},{10... | collective-permute-start | bytes 884744 | tf_op jit(solution)/shard_map/ppermute | solution.py:1206
  66.9 14.7 %collective-permute-start.4 = (bf16[384,384]{1,0:T(8,128)(2,1)S(1)}, bf16[384,384]{1,0:T(8,128)(2,1)S(1)}, u32[]{:S(2)}, u32[]{:S(2)}) collective-permute-start(bf16[384,384]{1,0:T(8,128)(2,1)S(1)} %bitcast.133), channel_id=1, source_target_pairs={{0,8},{8,0},{16,24},{24,16},{1,9},{9,1},{17,25},{25,17},{2,10},{10... | collective-permute-start | bytes 884744 | tf_op jit(solution)/shard_map/ppermute | solution.py:1206
  85.3 36.0 %collective-permute-start.7 = (bf16[96,1536]{1,0:T(8,128)(2,1)}, bf16[96,1536]{1,0:T(8,128)(2,1)S(1)}, u32[]{:S(2)}, u32[]{:S(2)}) collective-permute-start(bf16[96,1536]{1,0:T(8,128)(2,1)} %get-tuple-element.172), channel_id=1, source_target_pairs={{0,4},{1,5},{2,6},{3,7},{4,0},{5,1},{6,2},{7,3},{8,12},{9,13},{10,... | collective-permute-start | bytes 884744 | tf_op jit(solution)/shard_map/ppermute | solution.py:1206
  85.4 35.8 %collective-permute-start.8 = (bf16[96,1536]{1,0:T(8,128)(2,1)}, bf16[96,1536]{1,0:T(8,128)(2,1)}, u32[]{:S(2)}, u32[]{:S(2)}) collective-permute-start(bf16[96,1536]{1,0:T(8,128)(2,1)} %get-tuple-element.173), channel_id=1, source_target_pairs={{0,6},{1,7},{2,4},{3,5},{4,2},{5,3},{6,0},{7,1},{8,14},{9,15},{10,... | collective-permute-start | bytes 884744 | tf_op jit(solution)/shard_map/ppermute | solution.py:1206
  86.5 34.7 %collective-permute-start.9 = (bf16[96,1536]{1,0:T(8,128)(2,1)}, bf16[96,1536]{1,0:T(8,128)(2,1)}, u32[]{:S(2)}, u32[]{:S(2)}) collective-permute-start(bf16[96,1536]{1,0:T(8,128)(2,1)} %get-tuple-element.174), channel_id=1, source_target_pairs={{0,2},{1,3},{2,0},{3,1},{4,6},{5,7},{6,4},{7,5},{8,10},{9,11},{10,... | collective-permute-start | bytes 884744 | tf_op jit(solution)/shard_map/ppermute | solution.py:1206
  170.7 74.3 %all-to-all-start.2 = ((bf16[8,96,1536]{2,1,0:T(8,128)(2,1)}), bf16[8,96,1536]{2,1,0:T(8,128)(2,1)}, u32[]{:S(2)}, u32[]{:S(2)}) async-start(bf16[8,96,1536]{2,1,0:T(8,128)(2,1)} %bitcast.126), calls=%async_computation.2 | async-start | bytes 4718592 | tf_op jit(solution)/shard_map/all_to_all | solution.py:1229
  175.3 60.6 %all-gather.8.cloned.1.call-start = ((), (), s32[]{:S(2)}) async-start(), calls=%async_computation.9 | async-start | bytes 2211840 | tf_op jit(solution)/shard_map/all_gather | solution.py:1233
  176.0 187.0 %all-gather.10.cloned.1.call-start = ((), (), s32[]{:S(2)}) async-start(), calls=%async_computation.10 | async-start | bytes 9830400 | tf_op jit(solution)/shard_map/all_gather | solution.py:1233
  176.0 59.9 %collective-permute-start.10 = (bf16[384,2048]{1,0:T(8,128)(2,1)}, bf16[384,2048]{1,0:T(8,128)(2,1)}, u32[]{:S(2)}, u32[]{:S(2)}) collective-permute-start(bf16[384,2048]{1,0:T(8,128)(2,1)} %collective-permute-done.refs_1_.refs_5_.refs_21_.refs_25_), channel_id=1, source_target_pairs={{0,16},{8,24},{16,0},{24,8},{1,17},{9,25},{17,1},{25,9},{2,18},{10... | collective-permute-start | bytes 4718600 | tf_op jit(solution)/shard_map/ppermute | solution.py:1206
  177.2 58.7 %collective-permute-start.11 = (bf16[1024,384]{1,0:T(8,128)(2,1)}, bf16[1024,384]{1,0:T(8,128)(2,1)}, u32[]{:S(2)}, u32[]{:S(2)}) collective-permute-start(bf16[1024,384]{1,0:T(8,128)(2,1)} %collective-permute-done.3.refs_10_.refs_30_), channel_id=1, source_target_pairs={{0,8},{8,0},{16,24},{24,16},{1,9},{9,1},{17,25},{25,17},{2,10},{10... | collective-permute-start | bytes 2359304 | tf_op jit(solution)/shard_map/ppermute | solution.py:1206
  245.0 24.7 %collective-permute-start.12 = (bf16[96,1536]{1,0:T(8,128)(2,1)S(1)}, bf16[96,1536]{1,0:T(8,128)(2,1)S(1)}, u32[]{:S(2)}, u32[]{:S(2)}) collective-permute-start(bf16[96,1536]{1,0:T(8,128)(2,1)S(1)} %get-tuple-element.207), channel_id=1, source_target_pairs={{0,5},{1,4},{2,7},{3,6},{4,1},{5,0},{6,3},{7,2},{8,13},{9,12},{10,... | collective-permute-start | bytes 884744 | tf_op jit(solution)/shard_map/ppermute | solution.py:1206
  245.1 24.6 %collective-permute-start.13 = (bf16[96,1536]{1,0:T(8,128)(2,1)S(1)}, bf16[96,1536]{1,0:T(8,128)(2,1)}, u32[]{:S(2)}, u32[]{:S(2)}) collective-permute-start(bf16[96,1536]{1,0:T(8,128)(2,1)S(1)} %get-tuple-element.208), channel_id=1, source_target_pairs={{0,7},{1,6},{2,5},{3,4},{4,3},{5,2},{6,1},{7,0},{8,15},{9,14},{10,... | collective-permute-start | bytes 884744 | tf_op jit(solution)/shard_map/ppermute | solution.py:1206
  246.9 22.9 %collective-permute-start.14 = (bf16[96,1536]{1,0:T(8,128)(2,1)S(1)}, bf16[96,1536]{1,0:T(8,128)(2,1)}, u32[]{:S(2)}, u32[]{:S(2)}) collective-permute-start(bf16[96,1536]{1,0:T(8,128)(2,1)S(1)} %get-tuple-element.209), channel_id=1, source_target_pairs={{0,3},{1,2},{2,1},{3,0},{4,7},{5,6},{6,5},{7,4},{8,11},{9,10},{10,... | collective-permute-start | bytes 884744 | tf_op jit(solution)/shard_map/ppermute | solution.py:1206
  248.8 21.0 %collective-permute-start.15 = (bf16[96,1536]{1,0:T(8,128)(2,1)S(1)}, bf16[96,1536]{1,0:T(8,128)(2,1)}, u32[]{:S(2)}, u32[]{:S(2)}) collective-permute-start(bf16[96,1536]{1,0:T(8,128)(2,1)S(1)} %get-tuple-element.210), channel_id=1, source_target_pairs={{0,1},{1,0},{2,3},{3,2},{4,5},{5,4},{6,7},{7,6},{8,9},{9,8},{10,11... | collective-permute-start | bytes 884744 | tf_op jit(solution)/shard_map/ppermute | solution.py:1206
  269.8 33.0 %collective-permute-start.16 = (bf16[96,1536]{1,0:T(8,128)(2,1)}, bf16[96,1536]{1,0:T(8,128)(2,1)S(1)}, u32[]{:S(2)}, u32[]{:S(2)}) collective-permute-start(bf16[96,1536]{1,0:T(8,128)(2,1)} %get-tuple-element.222.refs_12_), channel_id=1, source_target_pairs={{0,4},{1,5},{2,6},{3,7},{4,0},{5,1},{6,2},{7,3},{8,12},{9,13},{10,... | collective-permute-start | bytes 884744 | tf_op jit(solution)/shard_map/ppermute | solution.py:1206
  274.2 28.7 %collective-permute-start.17 = (bf16[96,1536]{1,0:T(8,128)(2,1)}, bf16[96,1536]{1,0:T(8,128)(2,1)S(1)}, u32[]{:S(2)}, u32[]{:S(2)}) collective-permute-start(bf16[96,1536]{1,0:T(8,128)(2,1)} %get-tuple-element.224.refs_14_), channel_id=1, source_target_pairs={{0,6},{1,7},{2,4},{3,5},{4,2},{5,3},{6,0},{7,1},{8,14},{9,15},{10,... | collective-permute-start | bytes 884744 | tf_op jit(solution)/shard_map/ppermute | solution.py:1206
  275.5 27.3 %collective-permute-start.18 = (bf16[96,1536]{1,0:T(8,128)(2,1)}, bf16[96,1536]{1,0:T(8,128)(2,1)S(1)}, u32[]{:S(2)}, u32[]{:S(2)}) collective-permute-start(bf16[96,1536]{1,0:T(8,128)(2,1)} %get-tuple-element.220.refs_10_), channel_id=1, source_target_pairs={{0,2},{1,3},{2,0},{3,1},{4,6},{5,7},{6,4},{7,5},{8,10},{9,11},{10,... | collective-permute-start | bytes 884744 | tf_op jit(solution)/shard_map/ppermute | solution.py:1206
  275.5 27.4 %collective-permute-start.19 = (bf16[96,1536]{1,0:T(8,128)(2,1)}, bf16[96,1536]{1,0:T(8,128)(2,1)S(1)}, u32[]{:S(2)}, u32[]{:S(2)}) collective-permute-start(bf16[96,1536]{1,0:T(8,128)(2,1)} %get-tuple-element.219.refs_9_), channel_id=1, source_target_pairs={{0,1},{1,0},{2,3},{3,2},{4,5},{5,4},{6,7},{7,6},{8,9},{9,8},{10,11... | collective-permute-start | bytes 884744 | tf_op jit(solution)/shard_map/ppermute | solution.py:1206
  276.5 26.4 %collective-permute-start.20 = (bf16[96,1536]{1,0:T(8,128)(2,1)}, bf16[96,1536]{1,0:T(8,128)(2,1)S(1)}, u32[]{:S(2)}, u32[]{:S(2)}) collective-permute-start(bf16[96,1536]{1,0:T(8,128)(2,1)} %get-tuple-element.221.refs_11_), channel_id=1, source_target_pairs={{0,3},{1,2},{2,1},{3,0},{4,7},{5,6},{6,5},{7,4},{8,11},{9,10},{10,... | collective-permute-start | bytes 884744 | tf_op jit(solution)/shard_map/ppermute | solution.py:1206
  303.9 59.1 %all-to-all-start.3 = ((bf16[8,96,1536]{2,1,0:T(8,128)(2,1)}), bf16[8,96,1536]{2,1,0:T(8,128)(2,1)}, u32[]{:S(2)}, u32[]{:S(2)}) async-start(bf16[8,96,1536]{2,1,0:T(8,128)(2,1)} %bitcast.125), calls=%async_computation.3 | async-start | bytes 4718592 | tf_op jit(solution)/shard_map/all_to_all | solution.py:1229
  312.5 36.7 %collective-permute-start.21 = (bf16[384,1024]{1,0:T(8,128)(2,1)}, bf16[384,1024]{1,0:T(8,128)(2,1)S(1)}, u32[]{:S(2)}, u32[]{:S(2)}) collective-permute-start(bf16[384,1024]{1,0:T(8,128)(2,1)} %convolution_convert_fusion.8), channel_id=1, source_target_pairs={{0,8},{8,0},{16,24},{24,16},{1,9},{9,1},{17,25},{25,17},{2,10},{10... | collective-permute-start | bytes 2359304 | tf_op jit(solution)/shard_map/ppermute | solution.py:1206
  316.2 34.2 %collective-permute-start.22 = (bf16[384,1024]{1,0:T(8,128)(2,1)}, bf16[384,1024]{1,0:T(8,128)(2,1)}, u32[]{:S(2)}, u32[]{:S(2)}) collective-permute-start(bf16[384,1024]{1,0:T(8,128)(2,1)} %convolution_convert_fusion.6), channel_id=1, source_target_pairs={{0,16},{8,24},{16,0},{24,8},{1,17},{9,25},{17,1},{25,9},{2,18},{10... | collective-permute-start | bytes 2359304 | tf_op jit(solution)/shard_map/ppermute | solution.py:1206
  319.7 41.1 %collective-permute-start.23 = (bf16[384,1024]{1,0:T(8,128)(2,1)}, bf16[384,1024]{1,0:T(8,128)(2,1)}, u32[]{:S(2)}, u32[]{:S(2)}) collective-permute-start(bf16[384,1024]{1,0:T(8,128)(2,1)} %convolution_convert_fusion.4), channel_id=1, source_target_pairs={{0,8},{8,0},{16,24},{24,16},{1,9},{9,1},{17,25},{25,17},{2,10},{10... | collective-permute-start | bytes 2359304 | tf_op jit(solution)/shard_map/ppermute | solution.py:1206
  323.0 37.8 %collective-permute-start.24 = (bf16[384,1024]{1,0:T(8,128)(2,1)}, bf16[384,1024]{1,0:T(8,128)(2,1)}, u32[]{:S(2)}, u32[]{:S(2)}) collective-permute-start(bf16[384,1024]{1,0:T(8,128)(2,1)} %convolution_convert_fusion.2), channel_id=1, source_target_pairs={{0,16},{8,24},{16,0},{24,8},{1,17},{9,25},{17,1},{25,9},{2,18},{10... | collective-permute-start | bytes 2359304 | tf_op jit(solution)/shard_map/ppermute | solution.py:1206
  374.2 23.6 %all-to-all-start.4 = ((bf16[8,192,256]{2,1,0:T(8,128)(2,1)}), bf16[8,192,256]{2,1,0:T(8,128)(2,1)S(1)}, u32[]{:S(2)}, u32[]{:S(2)}) async-start(bf16[8,192,256]{2,1,0:T(8,128)(2,1)} %bitcast.114), calls=%async_computation.4 | async-start | bytes 1572864 | tf_op jit(solution)/shard_map/all_to_all | solution.py:1229
  377.7 114.1 %reduce-scatter.2.cloned.1.call-start = ((), (), s32[]{:S(2)}) async-start(), calls=%async_computation.11 | async-start | bytes 3932160 | tf_op jit(solution)/shard_map/reduce_scatter | solution.py:1420
  377.8 19.4 %collective-permute-start.26 = (bf16[384,1024]{1,0:T(8,128)(2,1)}, bf16[384,1024]{1,0:T(8,128)(2,1)S(1)}, u32[]{:S(2)}, u32[]{:S(2)}) collective-permute-start(bf16[384,1024]{1,0:T(8,128)(2,1)} %add_convert_fusion.2), channel_id=1, source_target_pairs={{0,16},{8,24},{16,0},{24,8},{1,17},{9,25},{17,1},{25,9},{2,18},{10... | collective-permute-start | bytes 2359304 | tf_op jit(solution)/shard_map/ppermute | solution.py:1206
  378.7 19.0 %collective-permute-start.27 = (bf16[384,1024]{1,0:T(8,128)(2,1)}, bf16[384,1024]{1,0:T(8,128)(2,1)S(1)}, u32[]{:S(2)}, u32[]{:S(2)}) collective-permute-start(bf16[384,1024]{1,0:T(8,128)(2,1)} %add_convert_fusion.1), channel_id=1, source_target_pairs={{0,8},{8,0},{16,24},{24,16},{1,9},{9,1},{17,25},{25,17},{2,10},{10... | collective-permute-start | bytes 2359304 | tf_op jit(solution)/shard_map/ppermute | solution.py:1206
  401.1 46.0 %collective-permute-start.30 = (bf16[2,384,768]{2,1,0:T(8,128)(2,1)}, bf16[2,384,768]{2,1,0:T(8,128)(2,1)}, u32[]{:S(2)}, u32[]{:S(2)}) collective-permute-start(bf16[2,384,768]{2,1,0:T(8,128)(2,1)} %slice.91), channel_id=1, source_target_pairs={{0,16},{8,24},{16,0},{24,8},{1,17},{9,25},{17,1},{25,9},{2,18},{10... | collective-permute-start | bytes 3538952 | tf_op jit(solution)/shard_map/ppermute | solution.py:1206
  401.8 31.4 %collective-permute-start.28 = (bf16[96,1536]{1,0:T(8,128)(2,1)S(1)}, bf16[96,1536]{1,0:T(8,128)(2,1)S(1)}, u32[]{:S(2)}, u32[]{:S(2)}) collective-permute-start(bf16[96,1536]{1,0:T(8,128)(2,1)S(1)} %copy-done.55), channel_id=1, source_target_pairs={{0,5},{1,4},{2,7},{3,6},{4,1},{5,0},{6,3},{7,2},{8,13},{9,12},{10,... | collective-permute-start | bytes 884744 | tf_op jit(solution)/shard_map/ppermute | solution.py:1206
  405.3 28.7 %collective-permute-start.29 = (bf16[96,1536]{1,0:T(8,128)(2,1)S(1)}, bf16[96,1536]{1,0:T(8,128)(2,1)S(1)}, u32[]{:S(2)}, u32[]{:S(2)}) collective-permute-start(bf16[96,1536]{1,0:T(8,128)(2,1)S(1)} %copy-done.54), channel_id=1, source_target_pairs={{0,7},{1,6},{2,5},{3,4},{4,3},{5,2},{6,1},{7,0},{8,15},{9,14},{10,... | collective-permute-start | bytes 884744 | tf_op jit(solution)/shard_map/ppermute | solution.py:1206
  434.6 38.4 %all-to-all-start.5 = ((bf16[8,320,256]{2,1,0:T(8,128)(2,1)}), bf16[8,320,256]{2,1,0:T(8,128)(2,1)}, u32[]{:S(2)}, u32[]{:S(2)}) async-start(bf16[8,320,256]{2,1,0:T(8,128)(2,1)} %copy-done.9), calls=%async_computation.5 | async-start | bytes 2621440 | tf_op jit(solution)/shard_map/all_to_all | solution.py:1229
  447.2 15.9 %collective-permute-start.31 = (bf16[384,384]{1,0:T(8,128)(2,1)S(1)}, bf16[384,384]{1,0:T(8,128)(2,1)S(1)}, u32[]{:S(2)}, u32[]{:S(2)}) collective-permute-start(bf16[384,384]{1,0:T(8,128)(2,1)S(1)} %get-tuple-element.362), channel_id=1, source_target_pairs={{0,8},{8,0},{16,24},{24,16},{1,9},{9,1},{17,25},{25,17},{2,10},{10... | collective-permute-start | bytes 884744 | tf_op jit(solution)/shard_map/ppermute | solution.py:1206
  448.2 14.9 %collective-permute-start.32 = (bf16[384,384]{1,0:T(8,128)(2,1)S(1)}, bf16[384,384]{1,0:T(8,128)(2,1)S(1)}, u32[]{:S(2)}, u32[]{:S(2)}) collective-permute-start(bf16[384,384]{1,0:T(8,128)(2,1)S(1)} %get-tuple-element.361), channel_id=1, source_target_pairs={{0,16},{8,24},{16,0},{24,8},{1,17},{9,25},{17,1},{25,9},{2,18},{10... | collective-permute-start | bytes 884744 | tf_op jit(solution)/shard_map/ppermute | solution.py:1206
  449.0 22.5 %collective-permute-start.33 = (bf16[384,384]{1,0:T(8,128)(2,1)S(1)}, bf16[384,384]{1,0:T(8,128)(2,1)S(1)}, u32[]{:S(2)}, u32[]{:S(2)}) collective-permute-start(bf16[384,384]{1,0:T(8,128)(2,1)S(1)} %get-tuple-element.360), channel_id=1, source_target_pairs={{0,24},{8,16},{16,8},{24,0},{1,25},{9,17},{17,9},{25,1},{2,26},{10... | collective-permute-start | bytes 884744 | tf_op jit(solution)/shard_map/ppermute | solution.py:1206
  472.4 14.6 %collective-permute-start.34 = (bf16[384,768]{1,0:T(8,128)(2,1)}, bf16[384,768]{1,0:T(8,128)(2,1)S(1)}, u32[]{:S(2)}, u32[]{:S(2)}) collective-permute-start(bf16[384,768]{1,0:T(8,128)(2,1)} %fusion.4), channel_id=1, source_target_pairs={{0,8},{8,0},{16,24},{24,16},{1,9},{9,1},{17,25},{25,17},{2,10},{10... | collective-permute-start | bytes 1769480 | tf_op jit(solution)/shard_map/ppermute | solution.py:1206
  473.0 29.9 %all-to-all-start.6 = ((bf16[8,48,384]{2,1,0:T(8,128)(2,1)}), bf16[8,48,384]{2,1,0:T(8,128)(2,1)S(1)}, u32[]{:S(2)}, u32[]{:S(2)}) async-start(bf16[8,48,384]{2,1,0:T(8,128)(2,1)} %bitcast.44), calls=%async_computation.7 | async-start | bytes 589824 | tf_op jit(solution)/shard_map/all_to_all | solution.py:1229
  488.2 14.7 %collective-permute-start.35 = (bf16[96,768]{1,0:T(8,128)(2,1)S(1)}, bf16[96,768]{1,0:T(8,128)(2,1)S(1)}, u32[]{:S(2)}, u32[]{:S(2)}) collective-permute-start(bf16[96,768]{1,0:T(8,128)(2,1)S(1)} %get-tuple-element.373), channel_id=1, source_target_pairs={{0,2},{1,3},{2,0},{3,1},{4,6},{5,7},{6,4},{7,5},{8,10},{9,11},{10,... | collective-permute-start | bytes 442376 | tf_op jit(solution)/shard_map/ppermute | solution.py:1206
  489.7 13.2 %collective-permute-start.36 = (bf16[96,768]{1,0:T(8,128)(2,1)S(1)}, bf16[96,768]{1,0:T(8,128)(2,1)S(1)}, u32[]{:S(2)}, u32[]{:S(2)}) collective-permute-start(bf16[96,768]{1,0:T(8,128)(2,1)S(1)} %get-tuple-element.372), channel_id=1, source_target_pairs={{0,4},{1,5},{2,6},{3,7},{4,0},{5,1},{6,2},{7,3},{8,12},{9,13},{10,... | collective-permute-start | bytes 442376 | tf_op jit(solution)/shard_map/ppermute | solution.py:1206
  491.8 11.2 %collective-permute-start.37 = (bf16[96,768]{1,0:T(8,128)(2,1)S(1)}, bf16[96,768]{1,0:T(8,128)(2,1)S(1)}, u32[]{:S(2)}, u32[]{:S(2)}) collective-permute-start(bf16[96,768]{1,0:T(8,128)(2,1)S(1)} %get-tuple-element.371), channel_id=1, source_target_pairs={{0,6},{1,7},{2,4},{3,5},{4,2},{5,3},{6,0},{7,1},{8,14},{9,15},{10,... | collective-permute-start | bytes 442376 | tf_op jit(solution)/shard_map/ppermute | solution.py:1206
  (76 other events, 448.8 us)
Sparse Core Ops, SparseCore 0:
  9.7 75.5 all-gather.11
  88.2 75.7 all-gather.5
  177.7 58.1 all-gather.7
  245.1 93.3 all-gather.9
  398.0 69.9 reduce-scatter.1
